TPU v7x, 32 devices: a whole 2x2x4 slice. The times are simulated.
32 devices in a mesh: wide: 32 (over z, y, x, core), narrow: 1.
Axes of the slice: x: 2, y: 2, z: 4, core: 2. Of those that a mesh axis runs over, the one named last changes fastest.
Arguments:
- tokens: bfloat16 [768, 4096], P('wide', 'narrow'), may hold values from -6 to 6
- grad_out: bfloat16 [768, 4096], P('wide', 'narrow'), may hold values from -1.1953125 to 1.1953125
- expert_ids: int32 [768, 8], P('wide'), may hold values from 0 to 31, all different within a row; in each aligned block of 24 rows (0 to 23, 24 to 47, ...) at most 12 rows name the same one
- route_weights: bfloat16 [768, 8], P('wide'), may hold values from 0.049804688 to 1
- w_gate: bfloat16 [32, 4096, 1536], P('wide', None, 'narrow'), may hold values from -0.09375 to 0.09375
- w_up: bfloat16 [32, 4096, 1536], P('wide', None, 'narrow'), may hold values from -0.09375 to 0.09375
- w_down: bfloat16 [32, 1536, 4096], P('wide', 'narrow'), may hold values from -0.15625 to 0.15625
Outputs:
- grad_tokens: bfloat16 [768, 4096], P('wide', 'narrow')
- grad_route: bfloat16 [768, 8], P('wide')
- grad_down: bfloat16 [32, 1536, 4096], P('wide', 'narrow')
Inputs may be any that keep to these rules, and one draw needn't show every extreme that they name: `expert_ids`: each row names 8 different experts. In each aligned block of 24 rows (the tokens of one index of wide) no expert is named by more than 12 rows, a bound that some block reaches.
All inputs are finite; a program needn't handle non-finite values.
Results may differ from a plain program's by a relative error of at most 0.019.
Values may be sent and summed in bfloat16 or wider, within the bound.
No kernel may reach another device: no remote copies, remote signals or barrier semaphores. Data moves between devices by JAX's collectives and lax.ppermute only.
A program may use at most 128 MiB of HBM per device.

v0:
```python
import functools

import jax
import jax.numpy as jnp
from jax import lax
from jax.experimental import pallas as pl
from jax.experimental.pallas import tpu as pltpu
from jax.sharding import PartitionSpec as P

LANES = 128
CHUNKS = 2
bf16, f32 = jnp.bfloat16, jnp.float32


def dot(a, b, dims):
    return lax.dot_general(a, b, ((dims[0], dims[1]), ((), ())), preferred_element_type=f32)


def add(*terms):
    total = terms[0].astype(f32)
    for term in terms[1:]:
        total = total + term.astype(f32)
    return total.astype(terms[0].dtype)


def tile(size, most):
    fits = [t for t in range(LANES, min(size, most) + 1, LANES) if size % t == 0]
    return fits[-1] if fits else size


def call(kernel, flops, moved, **kwargs):
    return pl.pallas_call(
        kernel,
        compiler_params=pltpu.CompilerParams(vmem_limit_bytes=52 * 1024 * 1024),
        cost_estimate=pl.CostEstimate(flops=flops, bytes_accessed=moved, transcendentals=0),
        **kwargs,
    )


def whole(*shape):
    return pl.BlockSpec(shape, lambda i: (0,) * len(shape))


CORE, X, Y, Z = 1, 2, 4, 8


def flip(value, mask):
    count = lax.axis_size("wide")
    return lax.ppermute(value, "wide", [(i, i ^ mask) for i in range(count)])


def depth():
    return lax.axis_size("wide") // Z


def gather_z(shard):
    return jnp.concatenate([shard] + [flip(shard, Z * k) for k in range(1, depth())], axis=0)


def gather_square(first):
    by_x, by_y = flip(first, X), flip(first, Y)
    half = first.shape[0] // 2
    return [first, by_x, by_y, flip(by_y[:half], X), flip(by_x[half:], Y)]


def gather_core(pieces):
    return pieces + [flip(piece, CORE) for piece in pieces]


def offsets():
    return [Z * k + m + c for c in (0, CORE) for m in (0, X, Y, X | Y) for k in range(depth())]


def scatter_rows(own, other):
    mine = add(own, flip(other, CORE))
    size = mine.shape[0] // 4
    parts = [mine[k * size : (k + 1) * size] for k in range(4)]
    first = add(parts[0], flip(parts[1], X), flip(parts[2], Y), flip(parts[3], X | Y))
    step = size // depth()
    blocks = [first[k * step : (k + 1) * step] for k in range(depth())]
    return add(blocks[0], *[flip(blocks[k], Z * k) for k in range(1, depth())])


def pick_kernel(sizes, block, slot_ref, *refs):
    pieces, (out_ref, held, place, sems) = refs[: len(sizes)], refs[len(sizes) :]
    step = pl.program_id(0)
    starts = [sum(sizes[:k]) for k in range(len(sizes))]

    def copy(at, k):
        return pltpu.make_async_copy(
            pieces[k].at[:, pl.ds(pl.multiple_of(at * block, LANES), block)],
            held.at[at, pl.ds(starts[k], sizes[k]), :],
            sems.at[at, k],
        )

    @pl.when(step == 0)
    def _():
        @pl.loop(0, pl.num_programs(0))
        def _(at):
            for k in range(len(sizes)):
                copy(at, k).start()

        rows = lax.broadcasted_iota(jnp.int32, place.shape, 0)
        place[...] = jnp.where(rows == slot_ref[...], 1.0, 0.0).astype(bf16)

    for k in range(len(sizes)):
        copy(step, k).wait()
    out_ref[...] = dot(place[...], held[step], ((1,), (0,))).astype(bf16)


def pick_rows(slot, pieces, rows, cols):
    sizes = [piece.shape[0] for piece in pieces]
    total = sum(sizes)
    block = tile(cols, 512)
    steps = cols // block
    return call(
        functools.partial(pick_kernel, sizes, block),
        2 * rows * total * cols,
        2 * (rows + total) * cols,
        grid=(steps,),
        in_specs=[whole(1, total)] + [pl.BlockSpec(memory_space=pl.ANY)] * len(pieces),
        out_specs=pl.BlockSpec((rows, block), lambda i: (0, i)),
        out_shape=jax.ShapeDtypeStruct((rows, cols), bf16),
        scratch_shapes=[
            pltpu.VMEM((steps, total, block), bf16),
            pltpu.VMEM((rows, total), bf16),
            pltpu.SemaphoreType.DMA((steps, len(sizes))),
        ],
    )(slot.reshape(1, total), *pieces)


def forward_kernel(x_ref, gate_ref, up_ref, hidden_ref, active_ref, pull_ref):
    gate_pre = dot(x_ref[...], gate_ref[...], ((1,), (0,)))
    up_pre = dot(x_ref[...], up_ref[...], ((1,), (0,)))
    sig = jax.nn.sigmoid(gate_pre)
    active = gate_pre * sig
    hidden_ref[...] = (active * up_pre).astype(bf16)
    active_ref[...] = active.astype(bf16)
    pull_ref[...] = (up_pre * (sig * (1.0 + gate_pre * (1.0 - sig)))).astype(bf16)


def forward(x, w_gate, w_up):
    rows, width = x.shape
    units = w_gate.shape[1]
    block = tile(units, 256)
    weight = pl.BlockSpec((width, block), lambda i: (0, i))
    unit = pl.BlockSpec((rows, block), lambda i: (0, i))
    shape = jax.ShapeDtypeStruct((rows, units), bf16)
    return call(
        forward_kernel,
        4 * rows * width * units,
        4 * width * units,
        grid=(units // block,),
        in_specs=[whole(rows, width), weight, weight],
        out_specs=[unit] * 3,
        out_shape=[shape] * 3,
    )(x, w_gate, w_up)


def back_kernel(g_ref, gain_ref, down_ref, hidden_ref, active_ref, pull_ref, d_gate_ref, d_up_ref, route_ref):
    back = dot(g_ref[...], down_ref[...], ((1,), (1,)))
    d_hidden = gain_ref[...] * back
    d_gate_ref[...] = (d_hidden * pull_ref[...].astype(f32)).astype(bf16)
    d_up_ref[...] = (d_hidden * active_ref[...].astype(f32)).astype(bf16)

    @pl.when(pl.program_id(0) == 0)
    def _():
        route_ref[...] = jnp.zeros_like(route_ref)

    route_ref[...] += jnp.sum(hidden_ref[...].astype(f32) * back, axis=1, keepdims=True)


def back_project(g, gain, w_down, hidden, active, pull):
    rows, width = g.shape
    units = w_down.shape[0]
    block = tile(units, 256)
    unit = pl.BlockSpec((rows, block), lambda i: (0, i))
    shape = jax.ShapeDtypeStruct((rows, units), bf16)
    return call(
        back_kernel,
        2 * rows * width * units,
        2 * width * units,
        grid=(units // block,),
        in_specs=[
            whole(rows, width),
            whole(rows, 1),
            pl.BlockSpec((block, width), lambda i: (i, 0)),
            unit,
            unit,
            unit,
        ],
        out_specs=[unit, unit, whole(rows, 1)],
        out_shape=[shape, shape, jax.ShapeDtypeStruct((rows, 1), f32)],
    )(g, gain, w_down, hidden, active, pull)


def token_kernel(spread, d_gate_ref, d_up_ref, slot_ref, gate_ref, up_ref, *outs):
    part = dot(d_gate_ref[...], gate_ref[...], ((1,), (1,)))
    part = (part + dot(d_up_ref[...], up_ref[...], ((1,), (1,)))).astype(bf16)
    if not spread:
        outs[0][...] = part
        return
    half = slot_ref.shape[0] // 2
    rows = part.shape[0]
    for k in range(2):
        slot = slot_ref[k * half : (k + 1) * half, :]
        lanes = lax.broadcasted_iota(jnp.int32, (half, rows), 1)
        place = jnp.where(lanes == slot, 1.0, 0.0).astype(bf16)
        outs[k][...] = dot(place, part, ((1,), (0,))).astype(bf16)


def token_grad(d_gate, d_up, slot, w_gate, w_up, chunk, chunks, spread):
    rows, units = d_gate.shape
    width = w_gate.shape[0] // chunks
    total = slot.shape[0]
    block = tile(width, 512)
    first = chunk * (width // block)
    weight = pl.BlockSpec((block, units), lambda i: (first + i, 0))
    out_rows = [total // 2] * 2 if spread else [rows]
    return call(
        functools.partial(token_kernel, spread),
        4 * rows * width * units + 2 * rows * width * total * spread,
        4 * width * units + 2 * total * width,
        grid=(width // block,),
        in_specs=[whole(rows, units), whole(rows, units), whole(total, 1), weight, weight],
        out_specs=[pl.BlockSpec((n, block), lambda i: (0, i)) for n in out_rows],
        out_shape=[jax.ShapeDtypeStruct((n, width), bf16) for n in out_rows],
    )(d_gate, d_up, slot.reshape(total, 1), w_gate, w_up)


def down_kernel(g_ref, gain_ref, hidden_ref, out_ref, scaled):
    @pl.when(pl.program_id(0) == 0)
    def _():
        scaled[...] = (gain_ref[...] * g_ref[...].astype(f32)).astype(bf16)

    out_ref[...] = dot(hidden_ref[...], scaled[...], ((0,), (0,))).astype(bf16)


def down_grad(g, gain, hidden):
    rows, width = g.shape
    units = hidden.shape[1]
    block = tile(units, 256)
    return call(
        down_kernel,
        2 * rows * width * units,
        2 * width * units,
        grid=(units // block,),
        in_specs=[whole(rows, width), whole(rows, 1), pl.BlockSpec((rows, block), lambda i: (0, i))],
        out_specs=pl.BlockSpec((block, width), lambda i: (i, 0)),
        out_shape=jax.ShapeDtypeStruct((units, width), bf16),
        scratch_shapes=[pltpu.VMEM((rows, width), bf16)],
    )(g, gain, hidden)


def body(tokens, grad_out, expert_ids, route_weights, w_gate, w_up, w_down):
    wide_count = lax.axis_size("wide")
    narrow_count = lax.axis_size("narrow")
    local_experts = w_gate.shape[0]
    experts_all = local_experts * wide_count
    tok_count, top_count = expert_ids.shape
    capacity = min(tok_count, 2 * tok_count * top_count // experts_all)
    rows = wide_count * capacity
    total = wide_count * tok_count
    cols = tokens.shape[1]
    me = lax.axis_index("wide")
    pad = -2 * top_count % LANES
    meta = jnp.concatenate(
        [expert_ids.astype(bf16), route_weights, jnp.zeros((tok_count, pad), bf16)], axis=1
    )
    first_t = gather_z(jnp.concatenate([tokens, meta], axis=1))
    first_t, grad_out = lax.optimization_barrier((first_t, grad_out))
    square_t = gather_square(first_t)
    first_g = gather_z(grad_out)
    pieces_t = gather_core(square_t)
    pieces_g = gather_core(gather_square(first_g))
    all_meta = jnp.concatenate([piece[:, cols : cols + 2 * top_count] for piece in pieces_t], axis=0)
    all_ids = all_meta[:, :top_count].astype(jnp.int32)
    all_weights = all_meta[:, top_count:].astype(f32)
    first = me * local_experts
    fused = narrow_count == 1 and local_experts == 1
    chunks = CHUNKS if fused else 1
    dense = [[0, 0] for _ in range(chunks)]
    route_cols = []
    grad_downs = []
    for j in range(local_experts):
        match = all_ids == first + j
        chosen = jnp.any(match, axis=1)
        gain = jnp.sum(jnp.where(match, all_weights, 0.0), axis=1)
        rank = jnp.cumsum(chosen.astype(jnp.int32)) - 1
        slot = jnp.where(chosen, rank, -1)
        place = slot[None, :] == jnp.arange(rows, dtype=jnp.int32)[:, None]
        row_gain = jnp.sum(jnp.where(place, gain[None, :], 0.0), axis=1, keepdims=True)
        x = pick_rows(slot, pieces_t, rows, cols)
        x = lax.all_gather(x, "narrow", axis=1, tiled=True)
        hidden, active, pull = forward(x, w_gate[j], w_up[j])
        g = pick_rows(slot, pieces_g, rows, cols)
        g = lax.all_gather(g, "narrow", axis=1, tiled=True)
        d_gate, d_up, route = back_project(g, row_gain, w_down[j], hidden, active, pull)
        for c in range(chunks):
            part = token_grad(d_gate, d_up, slot, w_gate[j], w_up[j], c, chunks, fused)
            if fused:
                dense[c] = part
            else:
                part = lax.psum_scatter(part[0], "narrow", scatter_dimension=1, tiled=True)
                part = dot(place.astype(bf16), part, ((0,), (0,)))
                dense[c] = [dense[c][0] + part[: total // 2], dense[c][1] + part[total // 2 :]]
        route = lax.psum(route.astype(bf16).astype(f32), "narrow")
        route_cols.append(jnp.sum(jnp.where(place, route, 0.0), axis=0))
        grad_downs.append(down_grad(g, row_gain, hidden))
    shares = [scatter_rows(own.astype(bf16), other.astype(bf16)) for own, other in dense]
    grad_tokens = jnp.concatenate(shares, axis=1)
    came_from = me ^ jnp.array(offsets(), jnp.int32)
    order = (jnp.arange(wide_count, dtype=jnp.int32)[:, None] == came_from[None, :]).astype(bf16)
    route = jnp.stack(route_cols, axis=1).astype(bf16).reshape(wide_count, tok_count * local_experts)
    route = dot(order, route, ((1,), (0,))).astype(bf16)
    route = lax.all_to_all(
        route.reshape(wide_count, tok_count, local_experts), "wide", split_axis=0, concat_axis=0, tiled=True
    )
    by_expert = jnp.swapaxes(route, 0, 1).reshape(tok_count, experts_all)
    pick = expert_ids[:, :, None] == jnp.arange(experts_all, dtype=jnp.int32)[None, None, :]
    grad_route = jnp.sum(jnp.where(pick, by_expert.astype(f32)[:, None, :], 0.0), axis=2)
    return (grad_tokens, grad_route.astype(bf16), jnp.stack(grad_downs))


def solution(mesh):
    in_specs = (
        P("wide", "narrow"),
        P("wide", "narrow"),
        P("wide", None),
        P("wide", None),
        P("wide", None, "narrow"),
        P("wide", None, "narrow"),
        P("wide", "narrow", None),
    )
    out_specs = (P("wide", "narrow"), P("wide", None), P("wide", "narrow", None))
    return jax.shard_map(body, mesh=mesh, in_specs=in_specs, out_specs=out_specs, check_vma=False)
```

profile of v0, /device:TPU:0, one launch (start us, length us, event | category | flops | bytes accessed | tf_op | source)
XLA Modules:
  0.0 232.4 jit_solution(7759518079092443406)
XLA Ops:
  3.2 5.1 %collective-permute-start.2 = (bf16[24,4224]{1,0:T(8,128)(2,1)S(1)}, bf16[24,4224]{1,0:T(8,128)(2,1)S(1)}, u32[]{:S(2)}, u32[]{:S(2)}) collective-permute-start(bf16[24,4224]{1,0:T(8,128)(2,1)S(1)} %concatenate.15), channel_id=1, source_target_pairs={{0,24},{1,25},{2,26},{3,27},{4,28},{5,29},{6,30},{7,31},{8,16},{9,... | collective-permute-start | bytes 608264 | tf_op jit(solution)/shard_map/ppermute | solution.py:49
  9.0 5.4 %collective-permute-done.2 = bf16[24,4224]{1,0:T(8,128)(2,1)S(1)} collective-permute-done((bf16[24,4224]{1,0:T(8,128)(2,1)S(1)}, bf16[24,4224]{1,0:T(8,128)(2,1)S(1)}, u32[]{:S(2)}, u32[]{:S(2)}) %collective-permute-start.2) | collective-permute-done | bytes 202784 | tf_op jit(solution)/shard_map/ppermute | solution.py:49
  14.3 11.2 %collective-permute-done.1 = bf16[24,4224]{1,0:T(8,128)(2,1)S(1)} collective-permute-done((bf16[24,4224]{1,0:T(8,128)(2,1)S(1)}, bf16[24,4224]{1,0:T(8,128)(2,1)S(1)}, u32[]{:S(2)}, u32[]{:S(2)}) %collective-permute-start.1) | collective-permute-done | bytes 202784 | tf_op jit(solution)/shard_map/ppermute | solution.py:49
  25.6 2.6 %collective-permute-start.14 = (bf16[24,4096]{1,0:T(8,128)(2,1)S(1)}, bf16[24,4096]{1,0:T(8,128)(2,1)S(1)}, u32[]{:S(2)}, u32[]{:S(2)}) collective-permute-start(bf16[24,4096]{1,0:T(8,128)(2,1)S(1)} %copy-done.11), channel_id=1, source_target_pairs={{0,24},{1,25},{2,26},{3,27},{4,28},{5,29},{6,30},{7,31},{8,16},{9,... | collective-permute-start | bytes 589832 | tf_op jit(solution)/shard_map/ppermute | solution.py:49
  28.3 1.8 collective-permute-start.12
  33.2 6.8 %collective-permute-done.12 = bf16[24,4096]{1,0:T(8,128)(2,1)S(1)} collective-permute-done((bf16[24,4096]{1,0:T(8,128)(2,1)S(1)}, bf16[24,4096]{1,0:T(8,128)(2,1)S(1)}, u32[]{:S(2)}, u32[]{:S(2)}) %collective-permute-start.12) | collective-permute-done | bytes 196640 | tf_op jit(solution)/shard_map/ppermute | solution.py:49
  40.0 3.2 %collective-permute-done.13 = bf16[24,4096]{1,0:T(8,128)(2,1)S(1)} collective-permute-done((bf16[24,4096]{1,0:T(8,128)(2,1)S(1)}, bf16[24,4096]{1,0:T(8,128)(2,1)S(1)}, u32[]{:S(2)}, u32[]{:S(2)}) %collective-permute-start.13) | collective-permute-done | bytes 196640 | tf_op jit(solution)/shard_map/ppermute | solution.py:49
  46.4 4.8 %collective-permute-done.4.refs_2_ = bf16[96,4224]{1,0:T(8,128)(2,1)S(1)} collective-permute-done((bf16[96,4224]{1,0:T(8,128)(2,1)S(1)}, bf16[96,4224]{1,0:T(8,128)(2,1)S(1)}, u32[]{:S(2)}, u32[]{:S(2)}) %collective-permute-start.4) | collective-permute-done | bytes 811040 | tf_op jit(solution)/shard_map/ppermute | solution.py:49
  52.9 12.5 %collective-permute-done.16.refs_2_ = bf16[96,4096]{1,0:T(8,128)(2,1)S(1)} collective-permute-done((bf16[96,4096]{1,0:T(8,128)(2,1)S(1)}, bf16[96,4096]{1,0:T(8,128)(2,1)S(1)}, u32[]{:S(2)}, u32[]{:S(2)}) %collective-permute-start.16) | collective-permute-done | bytes 786464 | tf_op jit(solution)/shard_map/ppermute | solution.py:49
  69.5 5.8 %collective-permute-done.5.refs_3_ = bf16[48,4224]{1,0:T(8,128)(2,1)S(1)} collective-permute-done((bf16[48,4224]{1,0:T(8,128)(2,1)S(1)}, bf16[48,4224]{1,0:T(8,128)(2,1)S(1)}, u32[]{:S(2)}, u32[]{:S(2)}) %collective-permute-start.5) | collective-permute-done | bytes 405536 | tf_op jit(solution)/shard_map/ppermute | solution.py:49
  85.2 4.5 %collective-permute-done.17.refs_3_ = bf16[48,4096]{1,0:T(8,128)(2,1)S(1)} collective-permute-done((bf16[48,4096]{1,0:T(8,128)(2,1)}, bf16[48,4096]{1,0:T(8,128)(2,1)S(1)}, u32[]{:S(2)}, u32[]{:S(2)}) %collective-permute-start.17) | collective-permute-done | bytes 393248 | tf_op jit(solution)/shard_map/ppermute | solution.py:49
  91.7 7.3 %shard_map.104.x_ref = bf16[384,4096]{1,0:T(8,128)(2,1)} custom-call(s32[1,768]{1,0:T(1,128)S(1)} %get-tuple-element.33.slot_ref, bf16[96,4224]{1,0:T(8,128)(2,1)} %copy-done.2, bf16[96,4224]{1,0:T(8,128)(2,1)} %collective-permute-done.3.refs_1_, bf16[96,4224]{1,0:T(8,128)(2,1)} %copy-done.3, bf16[48,4224]{1,0:T(8,128)(2,1)S(1)} %collective-permute-done.5.refs_3_, ...), custom_call_target="tpu_custom_call" | custom-call | flops 2415919104 | bytes 9437184 | tf_op jit(solution)/shard_map/pallas_call | solution.py:116
  99.0 16.5 %shard_map.105 = (bf16[384,1536]{1,0:T(8,128)(2,1)S(1)}, bf16[384,1536]{1,0:T(8,128)(2,1)}, bf16[384,1536]{1,0:T(8,128)(2,1)}) custom-call(bf16[384,4096]{1,0:T(8,128)(2,1)} %shard_map.104.x_ref, bf16[4096,1536]{1,0:T(8,128)(2,1)} %bitcast.25, bf16[4096,1536]{1,0:T(8,128)(2,1)} %bitcast.28), custom_call_target="tpu_custom_call" | custom-call | flops 9663676416 | bytes 25165824 | tf_op jit(solution)/shard_map/pallas_call | solution.py:149
  117.4 7.5 %shard_map.103.g_ref = bf16[384,4096]{1,0:T(8,128)(2,1)} custom-call(s32[1,768]{1,0:T(1,128)S(1)} %get-tuple-element.33.slot_ref, bf16[96,4096]{1,0:T(8,128)(2,1)} %copy-done.8, bf16[96,4096]{1,0:T(8,128)(2,1)} %copy-done.5, bf16[96,4096]{1,0:T(8,128)(2,1)} %copy-done.4, bf16[48,4096]{1,0:T(8,128)(2,1)S(1)} %collective-permute-done.17.refs_3_, ...), custom_call_target="tpu_custom_call" | custom-call | flops 2415919104 | bytes 9437184 | tf_op jit(solution)/shard_map/pallas_call | solution.py:116
  125.0 12.7 %shard_map.106 = (bf16[384,1536]{1,0:T(8,128)(2,1)S(1)}, bf16[384,1536]{1,0:T(8,128)(2,1)}, f32[384,1]{1,0:T(8,128)S(1)}) custom-call(bf16[384,4096]{1,0:T(8,128)(2,1)} %shard_map.103.g_ref, f32[384,1]{1,0:T(8,128)S(1)} %broadcast_in_dim.70.gain_ref, bf16[1536,4096]{1,0:T(8,128)(2,1)} %bitcast.31, bf16[384,1536]{1,0:T(8,128)(2,1)} %copy-done, ...), custom_call_target="tpu_custom_call" | custom-call | flops 4831838208 | bytes 12582912 | tf_op jit(solution)/shard_map/pallas_call | solution.py:179
  137.7 10.9 %shard_map.107 = (bf16[384,2048]{1,0:T(8,128)(2,1)}, bf16[384,2048]{1,0:T(8,128)(2,1)}) custom-call(bf16[384,1536]{1,0:T(8,128)(2,1)S(1)} %get-tuple-element.20.d_gate_ref, bf16[384,1536]{1,0:T(8,128)(2,1)} %get-tuple-element.21.d_up_ref, s32[768,1]{1,0:T(8,128)S(1)} %bitcast_select_fusion.slot_ref, bf16[4096,1536]{1,0:T(8,128)(2,1)} %bitcast.26, ...), custom_call_target="tpu_custom_call" | custom-call | flops 6039797760 | bytes 15728640 | tf_op jit(solution)/shard_map/pallas_call | solution.py:220
  150.1 4.3 %all-to-all-start = ((bf16[32,24,1]{1,2,0:T(2,128)(2,1)}), bf16[32,24,1]{1,2,0:T(2,128)(2,1)S(1)}, u32[]{:S(2)}, u32[]{:S(2)}) async-start(bf16[32,24,1]{1,2,0:T(2,128)(2,1)} %copy.76), calls=%async_computation | async-start | bytes 32768 | tf_op jit(solution)/shard_map/all_to_all | solution.py:316
  154.3 11.0 %shard_map.108 = (bf16[384,2048]{1,0:T(8,128)(2,1)}, bf16[384,2048]{1,0:T(8,128)(2,1)}) custom-call(bf16[384,1536]{1,0:T(8,128)(2,1)S(1)} %get-tuple-element.20.d_gate_ref, bf16[384,1536]{1,0:T(8,128)(2,1)} %get-tuple-element.21.d_up_ref, s32[768,1]{1,0:T(8,128)S(1)} %bitcast_select_fusion.slot_ref, bf16[4096,1536]{1,0:T(8,128)(2,1)} %bitcast.27, ...), custom_call_target="tpu_custom_call" | custom-call | flops 6039797760 | bytes 15728640 | tf_op jit(solution)/shard_map/pallas_call | solution.py:220
  165.4 11.7 %shard_map.109 = bf16[1536,4096]{1,0:T(8,128)(2,1)} custom-call(bf16[384,4096]{1,0:T(8,128)(2,1)} %shard_map.103.g_ref, f32[384,1]{1,0:T(8,128)S(1)} %broadcast_in_dim.70.gain_ref, bf16[384,1536]{1,0:T(8,128)(2,1)S(1)} %copy-done.1), custom_call_target="tpu_custom_call" | custom-call | flops 4831838208 | bytes 12582912 | tf_op jit(solution)/shard_map/pallas_call | solution.py:243
  178.0 2.0 add_convert_fusion.1
  180.2 1.7 collective-permute-start.25
  183.7 2.0 add_convert_fusion
  185.8 1.7 collective-permute-start.32
  189.0 3.2 %collective-permute-done.25 = bf16[96,2048]{1,0:T(8,128)(2,1)S(1)} collective-permute-done((bf16[96,2048]{1,0:T(8,128)(2,1)S(1)}, bf16[96,2048]{1,0:T(8,128)(2,1)S(1)}, u32[]{:S(2)}, u32[]{:S(2)}) %collective-permute-start.25) | collective-permute-done | bytes 393248 | tf_op jit(solution)/shard_map/ppermute | solution.py:49
  193.8 7.9 %collective-permute-done.27 = bf16[96,2048]{1,0:T(8,128)(2,1)S(1)} collective-permute-done((bf16[96,2048]{1,0:T(8,128)(2,1)S(1)}, bf16[96,2048]{1,0:T(8,128)(2,1)S(1)}, u32[]{:S(2)}, u32[]{:S(2)}) %collective-permute-start.27) | collective-permute-done | bytes 393248 | tf_op jit(solution)/shard_map/ppermute | solution.py:49
  201.7 2.1 collective-permute-done.26
  205.6 2.4 %collective-permute-start.30 = (bf16[24,2048]{1,0:T(8,128)(2,1)S(1)}, bf16[24,2048]{1,0:T(8,128)(2,1)S(1)}, u32[]{:S(2)}, u32[]{:S(2)}) collective-permute-start(bf16[24,2048]{1,0:T(8,128)(2,1)S(1)} %get-tuple-element.42), channel_id=1, source_target_pairs={{0,24},{1,25},{2,26},{3,27},{4,28},{5,29},{6,30},{7,31},{8,16},{9,... | collective-permute-start | bytes 294920 | tf_op jit(solution)/shard_map/ppermute | solution.py:49
  209.1 2.6 %collective-permute-start.29 = (bf16[24,2048]{1,0:T(8,128)(2,1)S(1)}, bf16[24,2048]{1,0:T(8,128)(2,1)S(1)}, u32[]{:S(2)}, u32[]{:S(2)}) collective-permute-start(bf16[24,2048]{1,0:T(8,128)(2,1)S(1)} %get-tuple-element.43), channel_id=1, source_target_pairs={{0,16},{1,17},{2,18},{3,19},{4,20},{5,21},{6,22},{7,23},{8,24},{9,... | collective-permute-start | bytes 294920 | tf_op jit(solution)/shard_map/ppermute | solution.py:49
  211.6 6.5 %collective-permute-done.34 = bf16[96,2048]{1,0:T(8,128)(2,1)S(1)} collective-permute-done((bf16[96,2048]{1,0:T(8,128)(2,1)S(1)}, bf16[96,2048]{1,0:T(8,128)(2,1)S(1)}, u32[]{:S(2)}, u32[]{:S(2)}) %collective-permute-start.34) | collective-permute-done | bytes 393248 | tf_op jit(solution)/shard_map/ppermute | solution.py:49
  221.2 2.4 %collective-permute-start.37 = (bf16[24,2048]{1,0:T(8,128)(2,1)S(1)}, bf16[24,2048]{1,0:T(8,128)(2,1)S(1)}, u32[]{:S(2)}, u32[]{:S(2)}) collective-permute-start(bf16[24,2048]{1,0:T(8,128)(2,1)S(1)} %get-tuple-element.45), channel_id=1, source_target_pairs={{0,24},{1,25},{2,26},{3,27},{4,28},{5,29},{6,30},{7,31},{8,16},{9,... | collective-permute-start | bytes 294920 | tf_op jit(solution)/shard_map/ppermute | solution.py:49
  225.4 3.2 %collective-permute-done.37 = bf16[24,2048]{1,0:T(8,128)(2,1)S(1)} collective-permute-done((bf16[24,2048]{1,0:T(8,128)(2,1)S(1)}, bf16[24,2048]{1,0:T(8,128)(2,1)S(1)}, u32[]{:S(2)}, u32[]{:S(2)}) %collective-permute-start.37) | collective-permute-done | bytes 98336 | tf_op jit(solution)/shard_map/ppermute | solution.py:49
  228.6 3.1 %collective-permute-done.36 = bf16[24,2048]{1,0:T(8,128)(2,1)S(1)} collective-permute-done((bf16[24,2048]{1,0:T(8,128)(2,1)S(1)}, bf16[24,2048]{1,0:T(8,128)(2,1)S(1)}, u32[]{:S(2)}, u32[]{:S(2)}) %collective-permute-start.36) | collective-permute-done | bytes 98336 | tf_op jit(solution)/shard_map/ppermute | solution.py:49
  (152 shorter events, 45.1 us)
Async XLA Ops:
  8.3 17.2 %collective-permute-start.1 = (bf16[24,4224]{1,0:T(8,128)(2,1)S(1)}, bf16[24,4224]{1,0:T(8,128)(2,1)S(1)}, u32[]{:S(2)}, u32[]{:S(2)}) collective-permute-start(bf16[24,4224]{1,0:T(8,128)(2,1)S(1)} %concatenate.15), channel_id=1, source_target_pairs={{0,16},{1,17},{2,18},{3,19},{4,20},{5,21},{6,22},{7,23},{8,24},{9,... | collective-permute-start | bytes 608264 | tf_op jit(solution)/shard_map/ppermute | solution.py:49
  8.3 17.2 %collective-permute-start = (bf16[24,4224]{1,0:T(8,128)(2,1)S(1)}, bf16[24,4224]{1,0:T(8,128)(2,1)S(1)}, u32[]{:S(2)}, u32[]{:S(2)}) collective-permute-start(bf16[24,4224]{1,0:T(8,128)(2,1)S(1)} %concatenate.15), channel_id=1, source_target_pairs={{0,8},{1,9},{2,10},{3,11},{4,12},{5,13},{6,14},{7,15},{8,0},{9,1},... | collective-permute-start | bytes 608264 | tf_op jit(solution)/shard_map/ppermute | solution.py:49
  25.6 17.6 %collective-permute-start.14 = (bf16[24,4096]{1,0:T(8,128)(2,1)S(1)}, bf16[24,4096]{1,0:T(8,128)(2,1)S(1)}, u32[]{:S(2)}, u32[]{:S(2)}) collective-permute-start(bf16[24,4096]{1,0:T(8,128)(2,1)S(1)} %copy-done.11), channel_id=1, source_target_pairs={{0,24},{1,25},{2,26},{3,27},{4,28},{5,29},{6,30},{7,31},{8,16},{9,... | collective-permute-start | bytes 589832 | tf_op jit(solution)/shard_map/ppermute | solution.py:49
  28.3 15.0 %collective-permute-start.13 = (bf16[24,4096]{1,0:T(8,128)(2,1)S(1)}, bf16[24,4096]{1,0:T(8,128)(2,1)S(1)}, u32[]{:S(2)}, u32[]{:S(2)}) collective-permute-start(bf16[24,4096]{1,0:T(8,128)(2,1)S(1)} %copy-done.11), channel_id=1, source_target_pairs={{0,16},{1,17},{2,18},{3,19},{4,20},{5,21},{6,22},{7,23},{8,24},{9,... | collective-permute-start | bytes 589832 | tf_op jit(solution)/shard_map/ppermute | solution.py:49
  28.3 11.7 %collective-permute-start.12 = (bf16[24,4096]{1,0:T(8,128)(2,1)S(1)}, bf16[24,4096]{1,0:T(8,128)(2,1)S(1)}, u32[]{:S(2)}, u32[]{:S(2)}) collective-permute-start(bf16[24,4096]{1,0:T(8,128)(2,1)S(1)} %copy-done.11), channel_id=1, source_target_pairs={{0,8},{1,9},{2,10},{3,11},{4,12},{5,13},{6,14},{7,15},{8,0},{9,1},... | collective-permute-start | bytes 589832 | tf_op jit(solution)/shard_map/ppermute | solution.py:49
  30.1 21.1 %collective-permute-start.4 = (bf16[96,4224]{1,0:T(8,128)(2,1)S(1)}, bf16[96,4224]{1,0:T(8,128)(2,1)S(1)}, u32[]{:S(2)}, u32[]{:S(2)}) collective-permute-start(bf16[96,4224]{1,0:T(8,128)(2,1)S(1)} %pad_maximum_fusion.refs_0_), channel_id=1, source_target_pairs={{0,4},{1,5},{2,6},{3,7},{4,0},{5,1},{6,2},{7,3},{8,12},{9,13},{10,... | collective-permute-start | bytes 2433032 | tf_op jit(solution)/shard_map/ppermute | solution.py:49
  31.7 21.1 %collective-permute-start.3 = (bf16[96,4224]{1,0:T(8,128)(2,1)S(1)}, bf16[96,4224]{1,0:T(8,128)(2,1)}, u32[]{:S(2)}, u32[]{:S(2)}) collective-permute-start(bf16[96,4224]{1,0:T(8,128)(2,1)S(1)} %pad_maximum_fusion.refs_0_), channel_id=1, source_target_pairs={{0,2},{1,3},{2,0},{3,1},{4,6},{5,7},{6,4},{7,5},{8,10},{9,11},{10,... | collective-permute-start | bytes 2433032 | tf_op jit(solution)/shard_map/ppermute | solution.py:49
  43.3 22.0 %collective-permute-start.16 = (bf16[96,4096]{1,0:T(8,128)(2,1)S(1)}, bf16[96,4096]{1,0:T(8,128)(2,1)S(1)}, u32[]{:S(2)}, u32[]{:S(2)}) collective-permute-start(bf16[96,4096]{1,0:T(8,128)(2,1)S(1)} %constant_dynamic-update-slice_fusion.refs_0_), channel_id=1, source_target_pairs={{0,4},{1,5},{2,6},{3,7},{4,0},{5,1},{6,2},{7,3},{8,12},{9,13},{10,... | collective-permute-start | bytes 2359304 | tf_op jit(solution)/shard_map/ppermute | solution.py:49
  44.9 23.0 %collective-permute-start.15 = (bf16[96,4096]{1,0:T(8,128)(2,1)S(1)}, bf16[96,4096]{1,0:T(8,128)(2,1)S(1)}, u32[]{:S(2)}, u32[]{:S(2)}) collective-permute-start(bf16[96,4096]{1,0:T(8,128)(2,1)S(1)} %constant_dynamic-update-slice_fusion.refs_0_), channel_id=1, source_target_pairs={{0,2},{1,3},{2,0},{3,1},{4,6},{5,7},{6,4},{7,5},{8,10},{9,11},{10,... | collective-permute-start | bytes 2359304 | tf_op jit(solution)/shard_map/ppermute | solution.py:49
  46.4 31.6 %collective-permute-start.7 = (bf16[96,4224]{1,0:T(8,128)(2,1)S(1)}, bf16[96,4224]{1,0:T(8,128)(2,1)S(1)}, u32[]{:S(2)}, u32[]{:S(2)}) collective-permute-start(bf16[96,4224]{1,0:T(8,128)(2,1)S(1)} %pad_maximum_fusion.refs_0_), channel_id=1, source_target_pairs={{0,1},{1,0},{2,3},{3,2},{4,5},{5,4},{6,7},{7,6},{8,9},{9,8},{10,11... | collective-permute-start | bytes 2433032 | tf_op jit(solution)/shard_map/ppermute | solution.py:49
  51.2 27.7 %collective-permute-start.9 = (bf16[96,4224]{1,0:T(8,128)(2,1)S(1)}, bf16[96,4224]{1,0:T(8,128)(2,1)S(1)}, u32[]{:S(2)}, u32[]{:S(2)}) collective-permute-start(bf16[96,4224]{1,0:T(8,128)(2,1)S(1)} %collective-permute-done.4.refs_2_), channel_id=1, source_target_pairs={{0,1},{1,0},{2,3},{3,2},{4,5},{5,4},{6,7},{7,6},{8,9},{9,8},{10,11... | collective-permute-start | bytes 2433032 | tf_op jit(solution)/shard_map/ppermute | solution.py:49
  52.8 30.9 %collective-permute-start.8 = (bf16[96,4224]{1,0:T(8,128)(2,1)}, bf16[96,4224]{1,0:T(8,128)(2,1)}, u32[]{:S(2)}, u32[]{:S(2)}) collective-permute-start(bf16[96,4224]{1,0:T(8,128)(2,1)} %collective-permute-done.3.refs_1_), channel_id=1, source_target_pairs={{0,1},{1,0},{2,3},{3,2},{4,5},{5,4},{6,7},{7,6},{8,9},{9,8},{10,11... | collective-permute-start | bytes 2433032 | tf_op jit(solution)/shard_map/ppermute | solution.py:49
  76.3 14.0 %collective-permute-start.11 = (bf16[48,4224]{1,0:T(8,128)(2,1)S(1)}, bf16[48,4224]{1,0:T(8,128)(2,1)S(1)}, u32[]{:S(2)}, u32[]{:S(2)}) collective-permute-start(bf16[48,4224]{1,0:T(8,128)(2,1)S(1)} %collective-permute-done.6.refs_4_), channel_id=1, source_target_pairs={{0,1},{1,0},{2,3},{3,2},{4,5},{5,4},{6,7},{7,6},{8,9},{9,8},{10,11... | collective-permute-start | bytes 1216520 | tf_op jit(solution)/shard_map/ppermute | solution.py:49
  77.9 11.8 %collective-permute-start.17 = (bf16[48,4096]{1,0:T(8,128)(2,1)}, bf16[48,4096]{1,0:T(8,128)(2,1)S(1)}, u32[]{:S(2)}, u32[]{:S(2)}) collective-permute-start(bf16[48,4096]{1,0:T(8,128)(2,1)} %slice.149), channel_id=1, source_target_pairs={{0,2},{1,3},{2,0},{3,1},{4,6},{5,7},{6,4},{7,5},{8,10},{9,11},{10,... | collective-permute-start | bytes 1179656 | tf_op jit(solution)/shard_map/ppermute | solution.py:49
  78.9 11.4 %collective-permute-start.18 = (bf16[48,4096]{1,0:T(8,128)(2,1)}, bf16[48,4096]{1,0:T(8,128)(2,1)S(1)}, u32[]{:S(2)}, u32[]{:S(2)}) collective-permute-start(bf16[48,4096]{1,0:T(8,128)(2,1)} %slice.150), channel_id=1, source_target_pairs={{0,4},{1,5},{2,6},{3,7},{4,0},{5,1},{6,2},{7,3},{8,12},{9,13},{10,... | collective-permute-start | bytes 1179656 | tf_op jit(solution)/shard_map/ppermute | solution.py:49
  83.7 33.6 %collective-permute-start.19 = (bf16[96,4096]{1,0:T(8,128)(2,1)}, bf16[96,4096]{1,0:T(8,128)(2,1)}, u32[]{:S(2)}, u32[]{:S(2)}) collective-permute-start(bf16[96,4096]{1,0:T(8,128)(2,1)} %copy-done.8), channel_id=1, source_target_pairs={{0,1},{1,0},{2,3},{3,2},{4,5},{5,4},{6,7},{7,6},{8,9},{9,8},{10,11... | collective-permute-start | bytes 2359304 | tf_op jit(solution)/shard_map/ppermute | solution.py:49
  84.6 32.8 %collective-permute-start.21 = (bf16[96,4096]{1,0:T(8,128)(2,1)}, bf16[96,4096]{1,0:T(8,128)(2,1)}, u32[]{:S(2)}, u32[]{:S(2)}) collective-permute-start(bf16[96,4096]{1,0:T(8,128)(2,1)} %copy-done.4), channel_id=1, source_target_pairs={{0,1},{1,0},{2,3},{3,2},{4,5},{5,4},{6,7},{7,6},{8,9},{9,8},{10,11... | collective-permute-start | bytes 2359304 | tf_op jit(solution)/shard_map/ppermute | solution.py:49
  89.7 27.7 %collective-permute-start.20 = (bf16[96,4096]{1,0:T(8,128)(2,1)}, bf16[96,4096]{1,0:T(8,128)(2,1)}, u32[]{:S(2)}, u32[]{:S(2)}) collective-permute-start(bf16[96,4096]{1,0:T(8,128)(2,1)} %copy-done.5), channel_id=1, source_target_pairs={{0,1},{1,0},{2,3},{3,2},{4,5},{5,4},{6,7},{7,6},{8,9},{9,8},{10,11... | collective-permute-start | bytes 2359304 | tf_op jit(solution)/shard_map/ppermute | solution.py:49
  90.4 27.0 %collective-permute-start.22 = (bf16[48,4096]{1,0:T(8,128)(2,1)S(1)}, bf16[48,4096]{1,0:T(8,128)(2,1)S(1)}, u32[]{:S(2)}, u32[]{:S(2)}) collective-permute-start(bf16[48,4096]{1,0:T(8,128)(2,1)S(1)} %collective-permute-done.17.refs_3_), channel_id=1, source_target_pairs={{0,1},{1,0},{2,3},{3,2},{4,5},{5,4},{6,7},{7,6},{8,9},{9,8},{10,11... | collective-permute-start | bytes 1179656 | tf_op jit(solution)/shard_map/ppermute | solution.py:49
  90.4 27.0 %collective-permute-start.23 = (bf16[48,4096]{1,0:T(8,128)(2,1)S(1)}, bf16[48,4096]{1,0:T(8,128)(2,1)S(1)}, u32[]{:S(2)}, u32[]{:S(2)}) collective-permute-start(bf16[48,4096]{1,0:T(8,128)(2,1)S(1)} %collective-permute-done.18.refs_4_), channel_id=1, source_target_pairs={{0,1},{1,0},{2,3},{3,2},{4,5},{5,4},{6,7},{7,6},{8,9},{9,8},{10,11... | collective-permute-start | bytes 1179656 | tf_op jit(solution)/shard_map/ppermute | solution.py:49
  148.6 29.5 %collective-permute-start.24 = (bf16[384,2048]{1,0:T(8,128)(2,1)}, bf16[384,2048]{1,0:T(8,128)(2,1)}, u32[]{:S(2)}, u32[]{:S(2)}) collective-permute-start(bf16[384,2048]{1,0:T(8,128)(2,1)} %get-tuple-element.23), channel_id=1, source_target_pairs={{0,1},{1,0},{2,3},{3,2},{4,5},{5,4},{6,7},{7,6},{8,9},{9,8},{10,11... | collective-permute-start | bytes 4718600 | tf_op jit(solution)/shard_map/ppermute | solution.py:49
  150.1 27.0 %all-to-all-start = ((bf16[32,24,1]{1,2,0:T(2,128)(2,1)}), bf16[32,24,1]{1,2,0:T(2,128)(2,1)S(1)}, u32[]{:S(2)}, u32[]{:S(2)}) async-start(bf16[32,24,1]{1,2,0:T(2,128)(2,1)} %copy.76), calls=%async_computation | async-start | bytes 32768 | tf_op jit(solution)/shard_map/all_to_all | solution.py:316
  165.3 18.4 %collective-permute-start.31 = (bf16[384,2048]{1,0:T(8,128)(2,1)}, bf16[384,2048]{1,0:T(8,128)(2,1)}, u32[]{:S(2)}, u32[]{:S(2)}) collective-permute-start(bf16[384,2048]{1,0:T(8,128)(2,1)} %get-tuple-element.25), channel_id=1, source_target_pairs={{0,1},{1,0},{2,3},{3,2},{4,5},{5,4},{6,7},{7,6},{8,9},{9,8},{10,11... | collective-permute-start | bytes 4718600 | tf_op jit(solution)/shard_map/ppermute | solution.py:49
  180.2 12.0 %collective-permute-start.25 = (bf16[96,2048]{1,0:T(8,128)(2,1)S(1)}, bf16[96,2048]{1,0:T(8,128)(2,1)S(1)}, u32[]{:S(2)}, u32[]{:S(2)}) collective-permute-start(bf16[96,2048]{1,0:T(8,128)(2,1)S(1)} %get-tuple-element.35), channel_id=1, source_target_pairs={{0,2},{1,3},{2,0},{3,1},{4,6},{5,7},{6,4},{7,5},{8,10},{9,11},{10,... | collective-permute-start | bytes 1179656 | tf_op jit(solution)/shard_map/ppermute | solution.py:49
  181.9 19.8 %collective-permute-start.27 = (bf16[96,2048]{1,0:T(8,128)(2,1)S(1)}, bf16[96,2048]{1,0:T(8,128)(2,1)S(1)}, u32[]{:S(2)}, u32[]{:S(2)}) collective-permute-start(bf16[96,2048]{1,0:T(8,128)(2,1)S(1)} %get-tuple-element.36), channel_id=1, source_target_pairs={{0,6},{1,7},{2,4},{3,5},{4,2},{5,3},{6,0},{7,1},{8,14},{9,15},{10,... | collective-permute-start | bytes 1179656 | tf_op jit(solution)/shard_map/ppermute | solution.py:49
  183.3 20.4 %collective-permute-start.26 = (bf16[96,2048]{1,0:T(8,128)(2,1)S(1)}, bf16[96,2048]{1,0:T(8,128)(2,1)S(1)}, u32[]{:S(2)}, u32[]{:S(2)}) collective-permute-start(bf16[96,2048]{1,0:T(8,128)(2,1)S(1)} %get-tuple-element.37), channel_id=1, source_target_pairs={{0,4},{1,5},{2,6},{3,7},{4,0},{5,1},{6,2},{7,3},{8,12},{9,13},{10,... | collective-permute-start | bytes 1179656 | tf_op jit(solution)/shard_map/ppermute | solution.py:49
  185.8 23.2 %collective-permute-start.32 = (bf16[96,2048]{1,0:T(8,128)(2,1)S(1)}, bf16[96,2048]{1,0:T(8,128)(2,1)S(1)}, u32[]{:S(2)}, u32[]{:S(2)}) collective-permute-start(bf16[96,2048]{1,0:T(8,128)(2,1)S(1)} %get-tuple-element.38), channel_id=1, source_target_pairs={{0,2},{1,3},{2,0},{3,1},{4,6},{5,7},{6,4},{7,5},{8,10},{9,11},{10,... | collective-permute-start | bytes 1179656 | tf_op jit(solution)/shard_map/ppermute | solution.py:49
  187.6 30.6 %collective-permute-start.34 = (bf16[96,2048]{1,0:T(8,128)(2,1)S(1)}, bf16[96,2048]{1,0:T(8,128)(2,1)S(1)}, u32[]{:S(2)}, u32[]{:S(2)}) collective-permute-start(bf16[96,2048]{1,0:T(8,128)(2,1)S(1)} %get-tuple-element.39), channel_id=1, source_target_pairs={{0,6},{1,7},{2,4},{3,5},{4,2},{5,3},{6,0},{7,1},{8,14},{9,15},{10,... | collective-permute-start | bytes 1179656 | tf_op jit(solution)/shard_map/ppermute | solution.py:49
  192.2 27.3 %collective-permute-start.33 = (bf16[96,2048]{1,0:T(8,128)(2,1)S(1)}, bf16[96,2048]{1,0:T(8,128)(2,1)S(1)}, u32[]{:S(2)}, u32[]{:S(2)}) collective-permute-start(bf16[96,2048]{1,0:T(8,128)(2,1)S(1)} %get-tuple-element.40), channel_id=1, source_target_pairs={{0,4},{1,5},{2,6},{3,7},{4,0},{5,1},{6,2},{7,3},{8,12},{9,13},{10,... | collective-permute-start | bytes 1179656 | tf_op jit(solution)/shard_map/ppermute | solution.py:49
  204.1 19.6 %collective-permute-start.28 = (bf16[24,2048]{1,0:T(8,128)(2,1)S(1)}, bf16[24,2048]{1,0:T(8,128)(2,1)S(1)}, u32[]{:S(2)}, u32[]{:S(2)}) collective-permute-start(bf16[24,2048]{1,0:T(8,128)(2,1)S(1)} %get-tuple-element.41), channel_id=1, source_target_pairs={{0,8},{1,9},{2,10},{3,11},{4,12},{5,13},{6,14},{7,15},{8,0},{9,1},... | collective-permute-start | bytes 294920 | tf_op jit(solution)/shard_map/ppermute | solution.py:49
  205.6 18.1 %collective-permute-start.30 = (bf16[24,2048]{1,0:T(8,128)(2,1)S(1)}, bf16[24,2048]{1,0:T(8,128)(2,1)S(1)}, u32[]{:S(2)}, u32[]{:S(2)}) collective-permute-start(bf16[24,2048]{1,0:T(8,128)(2,1)S(1)} %get-tuple-element.42), channel_id=1, source_target_pairs={{0,24},{1,25},{2,26},{3,27},{4,28},{5,29},{6,30},{7,31},{8,16},{9,... | collective-permute-start | bytes 294920 | tf_op jit(solution)/shard_map/ppermute | solution.py:49
  209.1 14.6 %collective-permute-start.29 = (bf16[24,2048]{1,0:T(8,128)(2,1)S(1)}, bf16[24,2048]{1,0:T(8,128)(2,1)S(1)}, u32[]{:S(2)}, u32[]{:S(2)}) collective-permute-start(bf16[24,2048]{1,0:T(8,128)(2,1)S(1)} %get-tuple-element.43), channel_id=1, source_target_pairs={{0,16},{1,17},{2,18},{3,19},{4,20},{5,21},{6,22},{7,23},{8,24},{9,... | collective-permute-start | bytes 294920 | tf_op jit(solution)/shard_map/ppermute | solution.py:49
  (21 other events, 270.4 us)
where the time goes:
time: 233 us; the launch traced here: 232 us
  waiting for transfers between devices  87.5 us (38%)
  Pallas kernels  77.7 us (33%)
  starting transfers between devices  45.9 us (20%)
  local copies, waits for them, and re-layouts  12.6 us (5%)
  other arithmetic  7.56 us (3%)
    ppermute x38, waiting for transfers between devices, flip(): return lax.ppermute(value, 'wide', [(i, i ^ mask) for i in range(count)])  87.5 us
    ppermute x38, starting transfers between devices, flip(): return lax.ppermute(value, 'wide', [(i, i ^ mask) for i in range(count)])  41.6 us
    pallas_call x2, Pallas kernels, token_grad(): call(functools.partial(token_kernel, spread), 4 * rows * width * units +...  21.8 us
    pallas_call x1, Pallas kernels, forward(): call(forward_kernel, 4 * rows * width * units, 4 * width * units, grid=(u...  16.5 us
    pallas_call x2, Pallas kernels, pick_rows(): call(functools.partial(pick_kernel, sizes, block), 2 * rows * total * col...  14.9 us
    pallas_call x1, Pallas kernels, back_project(): call(back_kernel, 2 * rows * width * units, 2 * width * units, grid=(unit...  12.7 us
    pallas_call x1, Pallas kernels, down_grad(): call(down_kernel, 2 * rows * width * units, 2 * width * units, grid=(unit...  11.7 us
  transfers between devices with their start and end apart: 39, of which 20 were waited for; matrix products, arithmetic and copies ran while one was open for 7% of the time, Pallas kernels for 20%

commit v1 on v0

v1 whole, which is shorter than its diff:
```python
import functools

import jax
import jax.numpy as jnp
from jax import lax
from jax.experimental import pallas as pl
from jax.experimental.pallas import tpu as pltpu
from jax.sharding import PartitionSpec as P

LANES = 128
CHUNKS = 2
bf16, f32 = jnp.bfloat16, jnp.float32


def dot(a, b, dims):
    return lax.dot_general(a, b, ((dims[0], dims[1]), ((), ())), preferred_element_type=f32)


def add(*terms):
    total = terms[0].astype(f32)
    for term in terms[1:]:
        total = total + term.astype(f32)
    return total.astype(terms[0].dtype)


def tile(size, most):
    fits = [t for t in range(LANES, min(size, most) + 1, LANES) if size % t == 0]
    return fits[-1] if fits else size


def call(kernel, flops, moved, **kwargs):
    return pl.pallas_call(
        kernel,
        compiler_params=pltpu.CompilerParams(vmem_limit_bytes=52 * 1024 * 1024),
        cost_estimate=pl.CostEstimate(flops=flops, bytes_accessed=moved, transcendentals=0),
        **kwargs,
    )


def whole(*shape):
    return pl.BlockSpec(shape, lambda i: (0,) * len(shape))


CORE, X, Y, Z = 1, 2, 4, 8


def flip(value, mask):
    count = lax.axis_size("wide")
    return lax.ppermute(value, "wide", [(i, i ^ mask) for i in range(count)])


def after(value, *deps):
    return lax.optimization_barrier((value, *deps))[0]


def depth():
    return lax.axis_size("wide") // Z


def gather_z(shard):
    return jnp.concatenate([shard] + [flip(shard, Z * k) for k in range(1, depth())], axis=0)


def gather_sides(first):
    return flip(first, X), flip(first, Y)


def gather_far(by_x, by_y):
    half = by_x.shape[0] // 2
    return [flip(by_y[:half], X), flip(by_x[half:], Y)]


def gather_core(pieces):
    return pieces + [flip(piece, CORE) for piece in pieces]


def offsets():
    return [Z * k + m + c for c in (0, CORE) for m in (0, X, Y, X | Y) for k in range(depth())]


def quarters(mine):
    size = mine.shape[0] // 4
    return [mine[k * size : (k + 1) * size] for k in range(4)]


def scatter_far(mine):
    first, by_x, by_y, far = quarters(mine)
    half = far.shape[0] // 2
    to_y, to_x = flip(far[:half], X), flip(far[half:], Y)
    by_y = jnp.concatenate([add(by_y[:half], to_y), by_y[half:]], axis=0)
    by_x = jnp.concatenate([by_x[:half], add(by_x[half:], to_x)], axis=0)
    return first, by_x, by_y


def scatter_sides(first, by_x, by_y):
    return add(first, flip(by_x, X), flip(by_y, Y))


def scatter_z(first):
    step = first.shape[0] // depth()
    blocks = [first[k * step : (k + 1) * step] for k in range(depth())]
    return add(blocks[0], *[flip(blocks[k], Z * k) for k in range(1, depth())])


def meta_kernel(sizes, cols, *refs):
    pieces, (out_ref, sems) = refs[: len(sizes)], refs[len(sizes) :]
    starts = [sum(sizes[:k]) for k in range(len(sizes))]
    copies = [
        pltpu.make_async_copy(
            pieces[k].at[:, pl.ds(cols, LANES)], out_ref.at[pl.ds(starts[k], sizes[k]), :], sems.at[k]
        )
        for k in range(len(sizes))
    ]
    for copy in copies:
        copy.start()
    for copy in copies:
        copy.wait()


def gather_meta(pieces, cols):
    sizes = [piece.shape[0] for piece in pieces]
    return call(
        functools.partial(meta_kernel, sizes, cols),
        0,
        4 * sum(sizes) * LANES,
        grid=(1,),
        in_specs=[pl.BlockSpec(memory_space=pl.ANY)] * len(pieces),
        out_specs=whole(sum(sizes), LANES),
        out_shape=jax.ShapeDtypeStruct((sum(sizes), LANES), bf16),
        scratch_shapes=[pltpu.SemaphoreType.DMA((len(sizes),))],
    )(*pieces)


def pick_kernel(sizes, block, slot_ref, *refs):
    pieces, (out_ref, held, place, sems) = refs[: len(sizes)], refs[len(sizes) :]
    step = pl.program_id(0)
    starts = [sum(sizes[:k]) for k in range(len(sizes))]

    def copy(at, k):
        return pltpu.make_async_copy(
            pieces[k].at[:, pl.ds(pl.multiple_of(at * block, LANES), block)],
            held.at[at, pl.ds(starts[k], sizes[k]), :],
            sems.at[at, k],
        )

    @pl.when(step == 0)
    def _():
        @pl.loop(0, pl.num_programs(0))
        def _(at):
            for k in range(len(sizes)):
                copy(at, k).start()

        rows = lax.broadcasted_iota(jnp.int32, place.shape, 0)
        place[...] = jnp.where(rows == slot_ref[...], 1.0, 0.0).astype(bf16)

    for k in range(len(sizes)):
        copy(step, k).wait()
    out_ref[...] = dot(place[...], held[step], ((1,), (0,))).astype(bf16)


def pick_rows(slot, pieces, rows, cols):
    sizes = [piece.shape[0] for piece in pieces]
    total = sum(sizes)
    block = tile(cols, 512)
    steps = cols // block
    return call(
        functools.partial(pick_kernel, sizes, block),
        2 * rows * total * cols,
        2 * (rows + total) * cols,
        grid=(steps,),
        in_specs=[whole(1, total)] + [pl.BlockSpec(memory_space=pl.ANY)] * len(pieces),
        out_specs=pl.BlockSpec((rows, block), lambda i: (0, i)),
        out_shape=jax.ShapeDtypeStruct((rows, cols), bf16),
        scratch_shapes=[
            pltpu.VMEM((steps, total, block), bf16),
            pltpu.VMEM((rows, total), bf16),
            pltpu.SemaphoreType.DMA((steps, len(sizes))),
        ],
    )(slot.reshape(1, total), *pieces)


def forward_kernel(x_ref, gate_ref, up_ref, hidden_ref, active_ref, pull_ref):
    gate_pre = dot(x_ref[...], gate_ref[...], ((1,), (0,)))
    up_pre = dot(x_ref[...], up_ref[...], ((1,), (0,)))
    sig = jax.nn.sigmoid(gate_pre)
    active = gate_pre * sig
    hidden_ref[...] = (active * up_pre).astype(bf16)
    active_ref[...] = active.astype(bf16)
    pull_ref[...] = (up_pre * (sig * (1.0 + gate_pre * (1.0 - sig)))).astype(bf16)


def forward(x, w_gate, w_up, part, parts):
    rows, width = x.shape
    units = w_gate.shape[1] // parts
    block = tile(units, 256)
    first = part * (units // block)
    weight = pl.BlockSpec((width, block), lambda i: (0, first + i))
    unit = pl.BlockSpec((rows, block), lambda i: (0, i))
    shape = jax.ShapeDtypeStruct((rows, units), bf16)
    return call(
        forward_kernel,
        4 * rows * width * units,
        4 * width * units,
        grid=(units // block,),
        in_specs=[whole(rows, width), weight, weight],
        out_specs=[unit] * 3,
        out_shape=[shape] * 3,
    )(x, w_gate, w_up)


def back_kernel(steps, g_ref, gain_ref, down_ref, *refs):
    parts, (d_gate_ref, d_up_ref, route_ref) = refs[:-3], refs[-3:]
    step = pl.program_id(0)
    back = dot(g_ref[...], down_ref[...], ((1,), (1,)))
    d_hidden = gain_ref[...] * back

    @pl.when(step == 0)
    def _():
        route_ref[...] = jnp.zeros_like(route_ref)

    for k in range(len(parts) // 3):
        hidden_ref, active_ref, pull_ref = parts[3 * k : 3 * k + 3]

        @pl.when((step >= k * steps) & (step < (k + 1) * steps))
        def _(hidden_ref=hidden_ref, active_ref=active_ref, pull_ref=pull_ref):
            d_gate_ref[...] = (d_hidden * pull_ref[...].astype(f32)).astype(bf16)
            d_up_ref[...] = (d_hidden * active_ref[...].astype(f32)).astype(bf16)
            route_ref[...] += jnp.sum(hidden_ref[...].astype(f32) * back, axis=1, keepdims=True)


def back_project(g, gain, w_down, parts):
    rows, width = g.shape
    units = w_down.shape[0]
    block = tile(parts[0][0].shape[1], 256)
    steps = units // block // len(parts)
    unit = pl.BlockSpec((rows, block), lambda i: (0, i))

    def unit_of(part):
        return pl.BlockSpec((rows, block), lambda i: (0, jnp.clip(i - part * steps, 0, steps - 1)))

    shape = jax.ShapeDtypeStruct((rows, units), bf16)
    return call(
        functools.partial(back_kernel, steps),
        2 * rows * width * units,
        2 * width * units,
        grid=(units // block,),
        in_specs=[
            whole(rows, width),
            whole(rows, 1),
            pl.BlockSpec((block, width), lambda i: (i, 0)),
        ]
        + [unit_of(k) for k in range(len(parts)) for _ in range(3)],
        out_specs=[unit, unit, whole(rows, 1)],
        out_shape=[shape, shape, jax.ShapeDtypeStruct((rows, 1), f32)],
    )(g, gain, w_down, *[array for part in parts for array in part])


def token_kernel(steps, spread, d_gate_ref, d_up_ref, slot_ref, route_ref, gate_ref, up_ref, *outs):
    step = pl.program_id(0)

    def store(part):
        if not spread:
            outs[0][...] = part
            return
        half = slot_ref.shape[0] // 2
        width = part.shape[1]
        for k in range(2):
            slot = slot_ref[k * half : (k + 1) * half, :]
            lanes = lax.broadcasted_iota(jnp.int32, (half, part.shape[0]), 1)
            place = jnp.where(lanes == slot, 1.0, 0.0).astype(bf16)
            outs[k][:, :width] = dot(place, part, ((1,), (0,))).astype(bf16)

    @pl.when(step < steps)
    def _():
        part = dot(d_gate_ref[...], gate_ref[...], ((1,), (1,)))
        store((part + dot(d_up_ref[...], up_ref[...], ((1,), (1,)))).astype(bf16))

    if spread:

        @pl.when(step >= steps)
        def _():
            store(route_ref[...])


def token_grad(d_gate, d_up, slot, route, w_gate, w_up, chunk, chunks, spread):
    rows, units = d_gate.shape
    width = w_gate.shape[0] // chunks
    total = slot.shape[0]
    block = tile(width, 512)
    steps = width // block
    first = chunk * steps
    extra = route.shape[1] if spread and chunk == chunks - 1 else 0
    weight = pl.BlockSpec((block, units), lambda i: (first + jnp.minimum(i, steps - 1), 0))
    out_rows = [total // 2] * 2 if spread else [rows]
    return call(
        functools.partial(token_kernel, steps, spread),
        4 * rows * width * units + 2 * rows * width * total * spread,
        4 * width * units + 2 * total * width,
        grid=(steps + (extra > 0),),
        in_specs=[whole(rows, units), whole(rows, units), whole(total, 1), whole(*route.shape), weight, weight],
        out_specs=[pl.BlockSpec((n, block), lambda i: (0, i)) for n in out_rows],
        out_shape=[jax.ShapeDtypeStruct((n, width + extra), bf16) for n in out_rows],
    )(d_gate, d_up, slot.reshape(total, 1), route, w_gate, w_up)


def down_kernel(g_ref, gain_ref, hidden_ref, *refs):
    out_ref, scaled = refs[-2:]

    @pl.when(pl.program_id(0) == 0)
    def _():
        scaled[...] = (gain_ref[...] * g_ref[...].astype(f32)).astype(bf16)

    out_ref[...] = dot(hidden_ref[...], scaled[...], ((0,), (0,))).astype(bf16)


def down_grad(g, gain, hidden, low, mine, first, units, into):
    rows, width = g.shape
    block = tile(mine, 256)
    start, source = first // block, low // block
    kept = [] if into is None else [into]
    return call(
        down_kernel,
        2 * rows * width * mine,
        2 * width * mine,
        grid=(mine // block,),
        in_specs=[whole(rows, width), whole(rows, 1), pl.BlockSpec((rows, block), lambda i: (0, source + i))]
        + [pl.BlockSpec(memory_space=pl.ANY)] * len(kept),
        out_specs=pl.BlockSpec((block, width), lambda i: (start + i, 0)),
        out_shape=jax.ShapeDtypeStruct((units, width), bf16),
        scratch_shapes=[pltpu.VMEM((rows, width), bf16)],
        input_output_aliases={3: 0} if kept else {},
    )(g, gain, hidden, *kept)


def body(tokens, grad_out, expert_ids, route_weights, w_gate, w_up, w_down):
    wide_count = lax.axis_size("wide")
    narrow_count = lax.axis_size("narrow")
    local_experts = w_gate.shape[0]
    experts_all = local_experts * wide_count
    tok_count, top_count = expert_ids.shape
    capacity = min(tok_count, 2 * tok_count * top_count // experts_all)
    rows = wide_count * capacity
    total = wide_count * tok_count
    cols = tokens.shape[1]
    me = lax.axis_index("wide")
    pad = -2 * top_count % LANES
    meta = jnp.concatenate(
        [expert_ids.astype(bf16), route_weights, jnp.zeros((tok_count, pad), bf16)], axis=1
    )
    first_t = gather_z(jnp.concatenate([tokens, meta], axis=1))
    x_t, y_t = gather_sides(first_t)
    first_g = gather_z(after(grad_out, first_t))
    far_t = gather_far(x_t, y_t)
    x_g, y_g = gather_sides(after(first_g, *far_t))
    pieces_t = gather_core([first_t, x_t, y_t] + far_t)
    all_meta = gather_meta(pieces_t, cols)
    all_ids = all_meta[:, :top_count].astype(jnp.int32)
    all_weights = all_meta[:, top_count : 2 * top_count].astype(f32)
    first = me * local_experts
    fused = narrow_count == 1 and local_experts == 1
    chunks = CHUNKS if fused else 1
    units = w_gate.shape[2]
    parts = 2 if units % (2 * LANES) == 0 else 1
    picked = []
    for j in range(local_experts):
        match = all_ids == first + j
        chosen = jnp.any(match, axis=1)
        gain = jnp.sum(jnp.where(match, all_weights, 0.0), axis=1)
        rank = jnp.cumsum(chosen.astype(jnp.int32)) - 1
        slot = jnp.where(chosen, rank, -1)
        place = slot[None, :] == jnp.arange(rows, dtype=jnp.int32)[:, None]
        row_gain = jnp.sum(jnp.where(place, gain[None, :], 0.0), axis=1, keepdims=True)
        x = pick_rows(slot, pieces_t, rows, cols)
        x = lax.all_gather(x, "narrow", axis=1, tiled=True)
        ahead = [forward(x, w_gate[j], w_up[j], 0, parts)]
        picked.append((slot, place, row_gain, x, ahead))
    x_g, y_g, *_ = lax.optimization_barrier((x_g, y_g, *[ahead[0][0] for *_, ahead in picked]))
    far_g = gather_far(x_g, y_g)
    for j in range(local_experts):
        slot, place, row_gain, x, ahead = picked[j]
        if parts == 2:
            ahead.append(forward(after(x, x_g, y_g), w_gate[j], w_up[j], 1, parts))
    far_g = lax.optimization_barrier((*far_g, *[ahead[-1][0] for *_, ahead in picked]))[: len(far_g)]
    pieces_g = gather_core([first_g, x_g, y_g, *far_g])
    expert_cols = experts_all + -experts_all % LANES
    dense = [0, 0]
    route_all = 0
    ends = []
    for j in range(local_experts):
        slot, place, row_gain, x, ahead = picked[j]
        g = pick_rows(slot, pieces_g, rows, cols)
        g = lax.all_gather(g, "narrow", axis=1, tiled=True)
        d_gate, d_up, route = back_project(g, row_gain, w_down[j], ahead)
        route = lax.psum(route.astype(bf16).astype(f32), "narrow")
        at = jnp.arange(expert_cols, dtype=jnp.int32) == first + j
        route = jnp.where(at[None, :], route, 0.0).astype(bf16)
        ends.append((g, row_gain, [part[0] for part in ahead]))
        if fused:
            own, other = token_grad(d_gate, d_up, slot, route, w_gate[j], w_up[j], 0, chunks, True)
            dense = [own, other]
            continue
        (part,) = token_grad(d_gate, d_up, slot, route, w_gate[j], w_up[j], 0, 1, False)
        part = lax.psum_scatter(part, "narrow", scatter_dimension=1, tiled=True)
        part = jnp.concatenate([part, route], axis=1)
        part = dot(place.astype(bf16), part, ((0,), (0,)))
        dense = [dense[0] + part[: total // 2], dense[1] + part[total // 2 :]]
    mine = [add(dense[0].astype(bf16), flip(dense[1].astype(bf16), CORE))]
    if fused and chunks == 2:
        own, other = token_grad(after(d_gate, dense[0]), d_up, slot, route, w_gate[0], w_up[0], 1, chunks, True)
        mine[0] = add(after(dense[0], own), flip(dense[1], CORE))
        mine.append(add(own, flip(other, CORE)))
    sides = [scatter_far(rows_) for rows_ in mine]
    firsts = [scatter_sides(*side) for side in sides]
    shares = [scatter_z(first_) for first_ in firsts]
    gates = iter([mine[0], sides[0][1], firsts[0], firsts[-1]])
    grad_downs = []
    for g, row_gain, hidden in ends:
        out, first_unit = None, 0
        for piece in hidden:
            count = piece.shape[1]
            cut = 2 * LANES * (count // (4 * LANES)) if len(hidden) > 1 and count % (2 * LANES) == 0 else 0
            for low, high in ((0, cut), (cut, count)):
                if high > low:
                    ready = after(piece, next(gates)) if local_experts == 1 else piece
                    out = down_grad(g, row_gain, ready, low, high - low, first_unit + low, units, out)
            first_unit += count
        grad_downs.append(out)
    joined = jnp.concatenate(shares, axis=1)
    width = tokens.shape[1]
    by_expert = joined[:, width : width + experts_all].astype(f32)
    pick = expert_ids[:, :, None] == jnp.arange(experts_all, dtype=jnp.int32)[None, None, :]
    grad_route = jnp.sum(jnp.where(pick, by_expert[:, None, :], 0.0), axis=2)
    return (joined[:, :width], grad_route.astype(bf16), jnp.stack(grad_downs))


def solution(mesh):
    in_specs = (
        P("wide", "narrow"),
        P("wide", "narrow"),
        P("wide", None),
        P("wide", None),
        P("wide", None, "narrow"),
        P("wide", None, "narrow"),
        P("wide", "narrow", None),
    )
    out_specs = (P("wide", "narrow"), P("wide", None), P("wide", "narrow", None))
    return jax.shard_map(body, mesh=mesh, in_specs=in_specs, out_specs=out_specs, check_vma=False)
```

time: 233 us -> 196 us (0.84)
  waiting for transfers between devices: 87.5 us -> 46.2 us
  Pallas kernels: 77.7 us -> 91 us
  starting transfers between devices: 45.9 us -> 37.9 us
    ppermute x38 -> x40, waiting for transfers between devices: 87.5 us -> 46.2 us  [flip(): return lax.ppermute(value, 'wide', [(i, i ^ mask) for i in range(count)])]
    pallas_call x4 -> x8, Pallas kernels: 46.3 us -> 57.7 us  [the longest x2 22.6 us: token_grad(): call(functools.partial(token_kernel, steps, spread), 4 * rows * width * u...]
    slice x29 -> x9, local copies, waits for them, and re-layouts: 7.49 us -> 2.35 us  [the longest x4 2.1 us: gather_far(): return [flip(by_y[:half], X), flip(by_x[half:], Y)]]
    unnamed x35 -> x37, local copies, waits for them, and re-layouts: 2.79 us -> 7.85 us
    all_to_all x1 -> x0, starting transfers between devices: 4.25 us -> none  [body(): lax.all_to_all(route.reshape(wide_count, tok_count, local_experts), 'wide...]
    ppermute x38 -> x40, starting transfers between devices: 41.6 us -> 37.9 us  [flip(): return lax.ppermute(value, 'wide', [(i, i ^ mask) for i in range(count)])]
    pallas_call x1 -> x2, Pallas kernels: 16.5 us -> 18.5 us  [forward(): call(forward_kernel, 4 * rows * width * units, 4 * width * units, grid=(u...]
  transfers between devices with their start and end apart: 39 -> 40, of which waited for: 20 -> 14; matrix products, arithmetic and copies ran while one was open for 7% -> 5% of each run, Pallas kernels for 20% -> 31%
where the time goes in v1:
time: 196 us; the launch traced here: 195 us
  Pallas kernels  91 us (46%)
  waiting for transfers between devices  46.2 us (24%)
  starting transfers between devices  37.9 us (19%)
  local copies, waits for them, and re-layouts  12.2 us (6%)
  other arithmetic  6.87 us (4%)
    ppermute x40, waiting for transfers between devices, flip(): return lax.ppermute(value, 'wide', [(i, i ^ mask) for i in range(count)])  46.2 us
    ppermute x40, starting transfers between devices, flip(): return lax.ppermute(value, 'wide', [(i, i ^ mask) for i in range(count)])  37.9 us
    pallas_call x2, Pallas kernels, token_grad(): call(functools.partial(token_kernel, steps, spread), 4 * rows * width * u...  22.6 us
    pallas_call x4, Pallas kernels, down_grad(): call(down_kernel, 2 * rows * width * mine, 2 * width * mine, grid=(mine /...  21.9 us
    pallas_call x2, Pallas kernels, forward(): call(forward_kernel, 4 * rows * width * units, 4 * width * units, grid=(u...  18.5 us
    pallas_call x2, Pallas kernels, pick_rows(): call(functools.partial(pick_kernel, sizes, block), 2 * rows * total * col...  14.8 us
    pallas_call x1, Pallas kernels, back_project(): call(functools.partial(back_kernel, steps), 2 * rows * width * units, 2 *...  12.3 us
    unnamed x37, local copies, waits for them, and re-layouts  7.85 us
  transfers between devices with their start and end apart: 40, of which 14 were waited for; matrix products, arithmetic and copies ran while one was open for 5% of the time, Pallas kernels for 31%

profile of v1, /device:TPU:0, one launch (start us, length us, event | category | flops | bytes accessed | tf_op | source)
XLA Modules:
  0.0 195.2 jit_solution(1627263528829276196)
XLA Ops:
  3.2 5.1 %collective-permute-start.2 = (bf16[24,4224]{1,0:T(8,128)(2,1)S(1)}, bf16[24,4224]{1,0:T(8,128)(2,1)S(1)}, u32[]{:S(2)}, u32[]{:S(2)}) collective-permute-start(bf16[24,4224]{1,0:T(8,128)(2,1)S(1)} %concatenate.24), channel_id=1, source_target_pairs={{0,24},{1,25},{2,26},{3,27},{4,28},{5,29},{6,30},{7,31},{8,16},{9,... | collective-permute-start | bytes 608264 | tf_op jit(solution)/shard_map/ppermute | solution.py:49
  9.0 5.4 %collective-permute-done.2 = bf16[24,4224]{1,0:T(8,128)(2,1)S(1)} collective-permute-done((bf16[24,4224]{1,0:T(8,128)(2,1)S(1)}, bf16[24,4224]{1,0:T(8,128)(2,1)S(1)}, u32[]{:S(2)}, u32[]{:S(2)}) %collective-permute-start.2) | collective-permute-done | bytes 202784 | tf_op jit(solution)/shard_map/ppermute | solution.py:49
  14.3 11.2 %collective-permute-done.1 = bf16[24,4224]{1,0:T(8,128)(2,1)S(1)} collective-permute-done((bf16[24,4224]{1,0:T(8,128)(2,1)S(1)}, bf16[24,4224]{1,0:T(8,128)(2,1)S(1)}, u32[]{:S(2)}, u32[]{:S(2)}) %collective-permute-start.1) | collective-permute-done | bytes 202784 | tf_op jit(solution)/shard_map/ppermute | solution.py:49
  25.6 2.6 %collective-permute-start.14 = (bf16[24,4096]{1,0:T(8,128)(2,1)S(1)}, bf16[24,4096]{1,0:T(8,128)(2,1)S(1)}, u32[]{:S(2)}, u32[]{:S(2)}) collective-permute-start(bf16[24,4096]{1,0:T(8,128)(2,1)S(1)} %copy-done.13), channel_id=1, source_target_pairs={{0,24},{1,25},{2,26},{3,27},{4,28},{5,29},{6,30},{7,31},{8,16},{9,... | collective-permute-start | bytes 589832 | tf_op jit(solution)/shard_map/ppermute | solution.py:49
  28.3 1.8 collective-permute-start.12
  30.1 1.5 collective-permute-start.4
  31.6 1.5 collective-permute-start.3
  33.8 6.2 %collective-permute-done.12 = bf16[24,4096]{1,0:T(8,128)(2,1)S(1)} collective-permute-done((bf16[24,4096]{1,0:T(8,128)(2,1)S(1)}, bf16[24,4096]{1,0:T(8,128)(2,1)S(1)}, u32[]{:S(2)}, u32[]{:S(2)}) %collective-permute-start.12) | collective-permute-done | bytes 196640 | tf_op jit(solution)/shard_map/ppermute | solution.py:49
  40.7 7.7 %collective-permute-done.4.refs_2_ = bf16[96,4224]{1,0:T(8,128)(2,1)S(1)} collective-permute-done((bf16[96,4224]{1,0:T(8,128)(2,1)S(1)}, bf16[96,4224]{1,0:T(8,128)(2,1)S(1)}, u32[]{:S(2)}, u32[]{:S(2)}) %collective-permute-start.4) | collective-permute-done | bytes 811040 | tf_op jit(solution)/shard_map/ppermute | solution.py:49
  48.4 1.6 collective-permute-start.5
  52.8 5.5 %collective-permute-done.5.refs_3_ = bf16[48,4224]{1,0:T(8,128)(2,1)S(1)} collective-permute-done((bf16[48,4224]{1,0:T(8,128)(2,1)S(1)}, bf16[48,4224]{1,0:T(8,128)(2,1)S(1)}, u32[]{:S(2)}, u32[]{:S(2)}) %collective-permute-start.5) | collective-permute-done | bytes 405536 | tf_op jit(solution)/shard_map/ppermute | solution.py:49
  59.9 1.3 collective-permute-start.16
  63.9 7.3 %shard_map.95.x_ref = bf16[384,4096]{1,0:T(8,128)(2,1)} custom-call(s32[1,768]{1,0:T(1,128)S(1)} %get-tuple-element.61.slot_ref, bf16[96,4224]{1,0:T(8,128)(2,1)} %copy-done.6, bf16[96,4224]{1,0:T(8,128)(2,1)} %copy-done.8, bf16[96,4224]{1,0:T(8,128)(2,1)} %copy-done.7, bf16[48,4224]{1,0:T(8,128)(2,1)S(1)} %collective-permute-done.5.refs_3_, ...), custom_call_target="tpu_custom_call" | custom-call | flops 2415919104 | bytes 9437184 | tf_op jit(solution)/shard_map/pallas_call | solution.py:166
  71.2 9.3 %shard_map.96 = (bf16[384,768]{1,0:T(8,128)(2,1)S(1)}, bf16[384,768]{1,0:T(8,128)(2,1)S(1)}, bf16[384,768]{1,0:T(8,128)(2,1)S(1)}) custom-call(bf16[384,4096]{1,0:T(8,128)(2,1)} %shard_map.95.x_ref, bf16[4096,1536]{1,0:T(8,128)(2,1)} %bitcast.19, bf16[4096,1536]{1,0:T(8,128)(2,1)} %bitcast.23), custom_call_target="tpu_custom_call" | custom-call | flops 4831838208 | bytes 12582912 | tf_op jit(solution)/shard_map/pallas_call | solution.py:200
  85.7 9.3 %shard_map.97 = (bf16[384,768]{1,0:T(8,128)(2,1)S(1)}, bf16[384,768]{1,0:T(8,128)(2,1)S(1)}, bf16[384,768]{1,0:T(8,128)(2,1)S(1)}) custom-call(bf16[384,4096]{1,0:T(8,128)(2,1)} %shard_map.95.x_ref, bf16[4096,1536]{1,0:T(8,128)(2,1)} %bitcast.20, bf16[4096,1536]{1,0:T(8,128)(2,1)} %bitcast.24), custom_call_target="tpu_custom_call" | custom-call | flops 4831838208 | bytes 12582912 | tf_op jit(solution)/shard_map/pallas_call | solution.py:200
  99.7 7.5 %shard_map.98.g_ref = bf16[384,4096]{1,0:T(8,128)(2,1)} custom-call(s32[1,768]{1,0:T(1,128)S(1)} %get-tuple-element.61.slot_ref, bf16[96,4096]{1,0:T(8,128)(2,1)} %constant_dynamic-update-slice_fusion.refs_0_, bf16[96,4096]{1,0:T(8,128)(2,1)} %collective-permute-done.15.refs_1_, bf16[96,4096]{1,0:T(8,128)(2,1)} %collective-permute-done.16.refs_2_, ...), custom_call_target="tpu_custom_call" | custom-call | flops 2415919104 | bytes 9437184 | tf_op jit(solution)/shard_map/pallas_call | solution.py:166
  107.2 12.3 %shard_map.99 = (bf16[384,1536]{1,0:T(8,128)(2,1)}, bf16[384,1536]{1,0:T(8,128)(2,1)}, f32[384,1]{1,0:T(8,128)S(1)}) custom-call(bf16[384,4096]{1,0:T(8,128)(2,1)} %shard_map.98.g_ref, f32[384,1]{1,0:T(8,128)S(1)} %broadcast_in_dim.81.gain_ref, bf16[1536,4096]{1,0:T(8,128)(2,1)} %bitcast.28, bf16[384,768]{1,0:T(8,128)(2,1)S(1)} %get-tuple-element.54.refs_0_.hidden_ref, ...), custom_call_target="tpu_custom_call" | custom-call | flops 4831838208 | bytes 12582912 | tf_op jit(solution)/shard_map/pallas_call | solution.py:242
  119.8 1.3 copy-done.2
  121.1 11.2 %shard_map.100 = (bf16[384,2048]{1,0:T(8,128)(2,1)}, bf16[384,2048]{1,0:T(8,128)(2,1)}) custom-call(bf16[384,1536]{1,0:T(8,128)(2,1)S(1)} %copy-done.2, bf16[384,1536]{1,0:T(8,128)(2,1)} %get-tuple-element.43.d_up_ref, s32[768,1]{1,0:T(8,128)S(1)} %bitcast_select_fusion.slot_ref, bf16[384,128]{1,0:T(8,128)(2,1)S(1)} %select_convert_fusion.route_ref, ...), custom_call_target="tpu_custom_call" | custom-call | flops 6039797760 | bytes 15728640 | tf_op jit(solution)/shard_map/pallas_call | solution.py:295
  132.3 11.4 %shard_map.101 = (bf16[384,2176]{1,0:T(8,128)(2,1)}, bf16[384,2176]{1,0:T(8,128)(2,1)}) custom-call(bf16[384,1536]{1,0:T(8,128)(2,1)S(1)} %copy-done.2, bf16[384,1536]{1,0:T(8,128)(2,1)} %get-tuple-element.43.d_up_ref, s32[768,1]{1,0:T(8,128)S(1)} %bitcast_select_fusion.slot_ref, bf16[384,128]{1,0:T(8,128)(2,1)S(1)} %select_convert_fusion.route_ref, ...), custom_call_target="tpu_custom_call" | custom-call | flops 6039797760 | bytes 15728640 | tf_op jit(solution)/shard_map/pallas_call | solution.py:295
  144.2 2.5 %add_convert_fusion.1 = bf16[384,2048]{1,0:T(8,128)(2,1)S(1)} fusion(bf16[384,2048]{1,0:T(8,128)(2,1)} %collective-permute-done.24, bf16[384,2048]{1,0:T(8,128)(2,1)} %get-tuple-element.48), kind=kLoop, calls=%fused_computation.1 | loop fusion | flops 3145728 | bytes 4718592 | tf_op jit(solution)/shard_map/convert_element_type | solution.py:23
  148.7 4.6 %shard_map.102.refs_0_ = bf16[1536,4096]{1,0:T(8,128)(2,1)} custom-call(bf16[384,4096]{1,0:T(8,128)(2,1)} %shard_map.98.g_ref, f32[384,1]{1,0:T(8,128)S(1)} %broadcast_in_dim.81.gain_ref, bf16[384,768]{1,0:T(8,128)(2,1)S(1)} %get-tuple-element.54.refs_0_.hidden_ref), custom_call_target="tpu_custom_call" | custom-call | flops 805306368 | bytes 2097152 | tf_op jit(solution)/shard_map/pallas_call | solution.py:321
  153.7 1.2 collective-permute-start.35
  158.2 6.4 %shard_map.103.refs_0_ = bf16[1536,4096]{1,0:T(8,128)(2,1)} custom-call(bf16[384,4096]{1,0:T(8,128)(2,1)} %shard_map.98.g_ref, f32[384,1]{1,0:T(8,128)S(1)} %broadcast_in_dim.81.gain_ref, bf16[384,768]{1,0:T(8,128)(2,1)S(1)} %get-tuple-element.54.refs_0_.hidden_ref, bf16[1536,4096]{1,0:T(8,128)(2,1)} %shard_map.102.refs_0_), custom_call_target="tpu_custom_call", output_to_operand_aliasing={{}: (3, {})} | custom-call | flops 1610612736 | bytes 4194304 | tf_op jit(solution)/shard_map/pallas_call | solution.py:321
  164.7 1.4 collective-permute-start.36
  166.1 5.3 %collective-permute-done.28 = bf16[96,2048]{1,0:T(8,128)(2,1)S(1)} collective-permute-done((bf16[96,2048]{1,0:T(8,128)(2,1)S(1)}, bf16[96,2048]{1,0:T(8,128)(2,1)S(1)}, u32[]{:S(2)}, u32[]{:S(2)}) %collective-permute-start.28) | collective-permute-done | bytes 393248 | tf_op jit(solution)/shard_map/ppermute | solution.py:49
  172.1 2.2 %collective-permute-start.31 = (bf16[24,2048]{1,0:T(8,128)(2,1)S(1)}, bf16[24,2048]{1,0:T(8,128)(2,1)S(1)}, u32[]{:S(2)}, u32[]{:S(2)}) collective-permute-start(bf16[24,2048]{1,0:T(8,128)(2,1)S(1)} %get-tuple-element.79), channel_id=1, source_target_pairs={{0,24},{1,25},{2,26},{3,27},{4,28},{5,29},{6,30},{7,31},{8,16},{9,... | collective-permute-start | bytes 294920 | tf_op jit(solution)/shard_map/ppermute | solution.py:49
  176.2 4.6 %shard_map.104.refs_0_ = bf16[1536,4096]{1,0:T(8,128)(2,1)} custom-call(bf16[384,4096]{1,0:T(8,128)(2,1)} %shard_map.98.g_ref, f32[384,1]{1,0:T(8,128)S(1)} %broadcast_in_dim.81.gain_ref, bf16[384,768]{1,0:T(8,128)(2,1)S(1)} %copy-done.1, bf16[1536,4096]{1,0:T(8,128)(2,1)} %shard_map.103.refs_0_), custom_call_target="tpu_custom_call", output_to_operand_aliasing={{}: (3, {})} | custom-call | flops 805306368 | bytes 2097152 | tf_op jit(solution)/shard_map/pallas_call | solution.py:321
  181.0 2.3 %collective-permute-done.34 = bf16[96,2176]{1,0:T(8,128)(2,1)S(1)} collective-permute-done((bf16[96,2176]{1,0:T(8,128)(2,1)S(1)}, bf16[96,2176]{1,0:T(8,128)(2,1)S(1)}, u32[]{:S(2)}, u32[]{:S(2)}) %collective-permute-start.34) | collective-permute-done | bytes 417824 | tf_op jit(solution)/shard_map/ppermute | solution.py:49
  183.5 1.3 collective-permute-start.37
  184.9 2.2 %collective-permute-start.39 = (bf16[24,2176]{1,0:T(8,128)(2,1)S(1)}, bf16[24,2176]{1,0:T(8,128)(2,1)S(1)}, u32[]{:S(2)}, u32[]{:S(2)}) collective-permute-start(bf16[24,2176]{1,0:T(8,128)(2,1)S(1)} %get-tuple-element.76), channel_id=1, source_target_pairs={{0,24},{1,25},{2,26},{3,27},{4,28},{5,29},{6,30},{7,31},{8,16},{9,... | collective-permute-start | bytes 313352 | tf_op jit(solution)/shard_map/ppermute | solution.py:49
  187.1 6.4 %shard_map.105 = bf16[1536,4096]{1,0:T(8,128)(2,1)} custom-call(bf16[384,4096]{1,0:T(8,128)(2,1)} %shard_map.98.g_ref, f32[384,1]{1,0:T(8,128)S(1)} %broadcast_in_dim.81.gain_ref, bf16[384,768]{1,0:T(8,128)(2,1)S(1)} %copy-done.1, bf16[1536,4096]{1,0:T(8,128)(2,1)} %shard_map.104.refs_0_), custom_call_target="tpu_custom_call", output_to_operand_aliasing={{}: (3, {})} | custom-call | flops 1610612736 | bytes 4194304 | tf_op jit(solution)/shard_map/pallas_call | solution.py:321
  (142 shorter events, 32.9 us)
Async XLA Ops:
  3.2 11.1 %collective-permute-start.2 = (bf16[24,4224]{1,0:T(8,128)(2,1)S(1)}, bf16[24,4224]{1,0:T(8,128)(2,1)S(1)}, u32[]{:S(2)}, u32[]{:S(2)}) collective-permute-start(bf16[24,4224]{1,0:T(8,128)(2,1)S(1)} %concatenate.24), channel_id=1, source_target_pairs={{0,24},{1,25},{2,26},{3,27},{4,28},{5,29},{6,30},{7,31},{8,16},{9,... | collective-permute-start | bytes 608264 | tf_op jit(solution)/shard_map/ppermute | solution.py:49
  8.3 17.2 %collective-permute-start.1 = (bf16[24,4224]{1,0:T(8,128)(2,1)S(1)}, bf16[24,4224]{1,0:T(8,128)(2,1)S(1)}, u32[]{:S(2)}, u32[]{:S(2)}) collective-permute-start(bf16[24,4224]{1,0:T(8,128)(2,1)S(1)} %concatenate.24), channel_id=1, source_target_pairs={{0,16},{1,17},{2,18},{3,19},{4,20},{5,21},{6,22},{7,23},{8,24},{9,... | collective-permute-start | bytes 608264 | tf_op jit(solution)/shard_map/ppermute | solution.py:49
  8.3 17.2 %collective-permute-start = (bf16[24,4224]{1,0:T(8,128)(2,1)S(1)}, bf16[24,4224]{1,0:T(8,128)(2,1)S(1)}, u32[]{:S(2)}, u32[]{:S(2)}) collective-permute-start(bf16[24,4224]{1,0:T(8,128)(2,1)S(1)} %concatenate.24), channel_id=1, source_target_pairs={{0,8},{1,9},{2,10},{3,11},{4,12},{5,13},{6,14},{7,15},{8,0},{9,1},... | collective-permute-start | bytes 608264 | tf_op jit(solution)/shard_map/ppermute | solution.py:49
  25.6 26.0 %collective-permute-start.14 = (bf16[24,4096]{1,0:T(8,128)(2,1)S(1)}, bf16[24,4096]{1,0:T(8,128)(2,1)S(1)}, u32[]{:S(2)}, u32[]{:S(2)}) collective-permute-start(bf16[24,4096]{1,0:T(8,128)(2,1)S(1)} %copy-done.13), channel_id=1, source_target_pairs={{0,24},{1,25},{2,26},{3,27},{4,28},{5,29},{6,30},{7,31},{8,16},{9,... | collective-permute-start | bytes 589832 | tf_op jit(solution)/shard_map/ppermute | solution.py:49
  28.3 23.4 %collective-permute-start.13 = (bf16[24,4096]{1,0:T(8,128)(2,1)S(1)}, bf16[24,4096]{1,0:T(8,128)(2,1)S(1)}, u32[]{:S(2)}, u32[]{:S(2)}) collective-permute-start(bf16[24,4096]{1,0:T(8,128)(2,1)S(1)} %copy-done.13), channel_id=1, source_target_pairs={{0,16},{1,17},{2,18},{3,19},{4,20},{5,21},{6,22},{7,23},{8,24},{9,... | collective-permute-start | bytes 589832 | tf_op jit(solution)/shard_map/ppermute | solution.py:49
  28.3 11.7 %collective-permute-start.12 = (bf16[24,4096]{1,0:T(8,128)(2,1)S(1)}, bf16[24,4096]{1,0:T(8,128)(2,1)S(1)}, u32[]{:S(2)}, u32[]{:S(2)}) collective-permute-start(bf16[24,4096]{1,0:T(8,128)(2,1)S(1)} %copy-done.13), channel_id=1, source_target_pairs={{0,8},{1,9},{2,10},{3,11},{4,12},{5,13},{6,14},{7,15},{8,0},{9,1},... | collective-permute-start | bytes 589832 | tf_op jit(solution)/shard_map/ppermute | solution.py:49
  30.1 18.3 %collective-permute-start.4 = (bf16[96,4224]{1,0:T(8,128)(2,1)S(1)}, bf16[96,4224]{1,0:T(8,128)(2,1)S(1)}, u32[]{:S(2)}, u32[]{:S(2)}) collective-permute-start(bf16[96,4224]{1,0:T(8,128)(2,1)S(1)} %pad_maximum_fusion.refs_0_), channel_id=1, source_target_pairs={{0,4},{1,5},{2,6},{3,7},{4,0},{5,1},{6,2},{7,3},{8,12},{9,13},{10,... | collective-permute-start | bytes 2433032 | tf_op jit(solution)/shard_map/ppermute | solution.py:49
  31.6 19.1 %collective-permute-start.3 = (bf16[96,4224]{1,0:T(8,128)(2,1)S(1)}, bf16[96,4224]{1,0:T(8,128)(2,1)S(1)}, u32[]{:S(2)}, u32[]{:S(2)}) collective-permute-start(bf16[96,4224]{1,0:T(8,128)(2,1)S(1)} %pad_maximum_fusion.refs_0_), channel_id=1, source_target_pairs={{0,2},{1,3},{2,0},{3,1},{4,6},{5,7},{6,4},{7,5},{8,10},{9,11},{10,... | collective-permute-start | bytes 2433032 | tf_op jit(solution)/shard_map/ppermute | solution.py:49
  40.0 19.5 %collective-permute-start.7 = (bf16[96,4224]{1,0:T(8,128)(2,1)S(1)}, bf16[96,4224]{1,0:T(8,128)(2,1)S(1)}, u32[]{:S(2)}, u32[]{:S(2)}) collective-permute-start(bf16[96,4224]{1,0:T(8,128)(2,1)S(1)} %pad_maximum_fusion.refs_0_), channel_id=1, source_target_pairs={{0,1},{1,0},{2,3},{3,2},{4,5},{5,4},{6,7},{7,6},{8,9},{9,8},{10,11... | collective-permute-start | bytes 2433032 | tf_op jit(solution)/shard_map/ppermute | solution.py:49
  48.4 9.9 %collective-permute-start.5 = (bf16[48,4224]{1,0:T(8,128)(2,1)S(1)}, bf16[48,4224]{1,0:T(8,128)(2,1)S(1)}, u32[]{:S(2)}, u32[]{:S(2)}) collective-permute-start(bf16[48,4224]{1,0:T(8,128)(2,1)S(1)} %slice.147), channel_id=1, source_target_pairs={{0,2},{1,3},{2,0},{3,1},{4,6},{5,7},{6,4},{7,5},{8,10},{9,11},{10,... | collective-permute-start | bytes 1216520 | tf_op jit(solution)/shard_map/ppermute | solution.py:49
  51.6 8.3 %collective-permute-start.9 = (bf16[96,4224]{1,0:T(8,128)(2,1)S(1)}, bf16[96,4224]{1,0:T(8,128)(2,1)S(1)}, u32[]{:S(2)}, u32[]{:S(2)}) collective-permute-start(bf16[96,4224]{1,0:T(8,128)(2,1)S(1)} %collective-permute-done.4.refs_2_), channel_id=1, source_target_pairs={{0,1},{1,0},{2,3},{3,2},{4,5},{5,4},{6,7},{7,6},{8,9},{9,8},{10,11... | collective-permute-start | bytes 2433032 | tf_op jit(solution)/shard_map/ppermute | solution.py:49
  51.6 9.6 %collective-permute-start.8 = (bf16[96,4224]{1,0:T(8,128)(2,1)S(1)}, bf16[96,4224]{1,0:T(8,128)(2,1)S(1)}, u32[]{:S(2)}, u32[]{:S(2)}) collective-permute-start(bf16[96,4224]{1,0:T(8,128)(2,1)S(1)} %collective-permute-done.3.refs_1_), channel_id=1, source_target_pairs={{0,1},{1,0},{2,3},{3,2},{4,5},{5,4},{6,7},{7,6},{8,9},{9,8},{10,11... | collective-permute-start | bytes 2433032 | tf_op jit(solution)/shard_map/ppermute | solution.py:49
  59.5 39.3 %collective-permute-start.19 = (bf16[96,4096]{1,0:T(8,128)(2,1)}, bf16[96,4096]{1,0:T(8,128)(2,1)}, u32[]{:S(2)}, u32[]{:S(2)}) collective-permute-start(bf16[96,4096]{1,0:T(8,128)(2,1)} %constant_dynamic-update-slice_fusion.refs_0_), channel_id=1, source_target_pairs={{0,1},{1,0},{2,3},{3,2},{4,5},{5,4},{6,7},{7,6},{8,9},{9,8},{10,11... | collective-permute-start | bytes 2359304 | tf_op jit(solution)/shard_map/ppermute | solution.py:49
  59.9 20.6 %collective-permute-start.16 = (bf16[96,4096]{1,0:T(8,128)(2,1)}, bf16[96,4096]{1,0:T(8,128)(2,1)}, u32[]{:S(2)}, u32[]{:S(2)}) collective-permute-start(bf16[96,4096]{1,0:T(8,128)(2,1)} %constant_dynamic-update-slice_fusion.refs_0_), channel_id=1, source_target_pairs={{0,4},{1,5},{2,6},{3,7},{4,0},{5,1},{6,2},{7,3},{8,12},{9,13},{10,... | collective-permute-start | bytes 2359304 | tf_op jit(solution)/shard_map/ppermute | solution.py:49
  61.2 19.6 %collective-permute-start.15 = (bf16[96,4096]{1,0:T(8,128)(2,1)}, bf16[96,4096]{1,0:T(8,128)(2,1)}, u32[]{:S(2)}, u32[]{:S(2)}) collective-permute-start(bf16[96,4096]{1,0:T(8,128)(2,1)} %constant_dynamic-update-slice_fusion.refs_0_), channel_id=1, source_target_pairs={{0,2},{1,3},{2,0},{3,1},{4,6},{5,7},{6,4},{7,5},{8,10},{9,11},{10,... | collective-permute-start | bytes 2359304 | tf_op jit(solution)/shard_map/ppermute | solution.py:49
  82.8 16.9 %collective-permute-start.20 = (bf16[96,4096]{1,0:T(8,128)(2,1)}, bf16[96,4096]{1,0:T(8,128)(2,1)}, u32[]{:S(2)}, u32[]{:S(2)}) collective-permute-start(bf16[96,4096]{1,0:T(8,128)(2,1)} %collective-permute-done.15.refs_1_), channel_id=1, source_target_pairs={{0,1},{1,0},{2,3},{3,2},{4,5},{5,4},{6,7},{7,6},{8,9},{9,8},{10,11... | collective-permute-start | bytes 2359304 | tf_op jit(solution)/shard_map/ppermute | solution.py:49
  82.9 16.8 %collective-permute-start.21 = (bf16[96,4096]{1,0:T(8,128)(2,1)}, bf16[96,4096]{1,0:T(8,128)(2,1)}, u32[]{:S(2)}, u32[]{:S(2)}) collective-permute-start(bf16[96,4096]{1,0:T(8,128)(2,1)} %collective-permute-done.16.refs_2_), channel_id=1, source_target_pairs={{0,1},{1,0},{2,3},{3,2},{4,5},{5,4},{6,7},{7,6},{8,9},{9,8},{10,11... | collective-permute-start | bytes 2359304 | tf_op jit(solution)/shard_map/ppermute | solution.py:49
  83.4 14.0 %collective-permute-start.17 = (bf16[48,4096]{1,0:T(8,128)(2,1)S(1)}, bf16[48,4096]{1,0:T(8,128)(2,1)S(1)}, u32[]{:S(2)}, u32[]{:S(2)}) collective-permute-start(bf16[48,4096]{1,0:T(8,128)(2,1)S(1)} %slice.120), channel_id=1, source_target_pairs={{0,2},{1,3},{2,0},{3,1},{4,6},{5,7},{6,4},{7,5},{8,10},{9,11},{10,... | collective-permute-start | bytes 1179656 | tf_op jit(solution)/shard_map/ppermute | solution.py:49
  84.6 12.8 %collective-permute-start.18 = (bf16[48,4096]{1,0:T(8,128)(2,1)S(1)}, bf16[48,4096]{1,0:T(8,128)(2,1)S(1)}, u32[]{:S(2)}, u32[]{:S(2)}) collective-permute-start(bf16[48,4096]{1,0:T(8,128)(2,1)S(1)} %slice.121), channel_id=1, source_target_pairs={{0,4},{1,5},{2,6},{3,7},{4,0},{5,1},{6,2},{7,3},{8,12},{9,13},{10,... | collective-permute-start | bytes 1179656 | tf_op jit(solution)/shard_map/ppermute | solution.py:49
  132.2 12.0 %collective-permute-start.24 = (bf16[384,2048]{1,0:T(8,128)(2,1)}, bf16[384,2048]{1,0:T(8,128)(2,1)}, u32[]{:S(2)}, u32[]{:S(2)}) collective-permute-start(bf16[384,2048]{1,0:T(8,128)(2,1)} %get-tuple-element.49), channel_id=1, source_target_pairs={{0,1},{1,0},{2,3},{3,2},{4,5},{5,4},{6,7},{7,6},{8,9},{9,8},{10,11... | collective-permute-start | bytes 4718600 | tf_op jit(solution)/shard_map/ppermute | solution.py:49
  143.7 9.6 %collective-permute-start.32 = (bf16[384,2176]{1,0:T(8,128)(2,1)}, bf16[384,2176]{1,0:T(8,128)(2,1)S(1)}, u32[]{:S(2)}, u32[]{:S(2)}) collective-permute-start(bf16[384,2176]{1,0:T(8,128)(2,1)} %get-tuple-element.50), channel_id=1, source_target_pairs={{0,1},{1,0},{2,3},{3,2},{4,5},{5,4},{6,7},{7,6},{8,9},{9,8},{10,11... | collective-permute-start | bytes 5013512 | tf_op jit(solution)/shard_map/ppermute | solution.py:49
  146.8 9.2 %collective-permute-start.27 = (bf16[48,2048]{1,0:T(8,128)(2,1)S(1)}, bf16[48,2048]{1,0:T(8,128)(2,1)S(1)}, u32[]{:S(2)}, u32[]{:S(2)}) collective-permute-start(bf16[48,2048]{1,0:T(8,128)(2,1)S(1)} %get-tuple-element.71), channel_id=1, source_target_pairs={{0,2},{1,3},{2,0},{3,1},{4,6},{5,7},{6,4},{7,5},{8,10},{9,11},{10,... | collective-permute-start | bytes 589832 | tf_op jit(solution)/shard_map/ppermute | solution.py:49
  153.7 10.8 %collective-permute-start.35 = (bf16[48,2176]{1,0:T(8,128)(2,1)S(1)}, bf16[48,2176]{1,0:T(8,128)(2,1)S(1)}, u32[]{:S(2)}, u32[]{:S(2)}) collective-permute-start(bf16[48,2176]{1,0:T(8,128)(2,1)S(1)} %get-tuple-element.65), channel_id=1, source_target_pairs={{0,2},{1,3},{2,0},{3,1},{4,6},{5,7},{6,4},{7,5},{8,10},{9,11},{10,... | collective-permute-start | bytes 626696 | tf_op jit(solution)/shard_map/ppermute | solution.py:49
  154.9 9.6 %collective-permute-start.33 = (bf16[48,2176]{1,0:T(8,128)(2,1)S(1)}, bf16[48,2176]{1,0:T(8,128)(2,1)S(1)}, u32[]{:S(2)}, u32[]{:S(2)}) collective-permute-start(bf16[48,2176]{1,0:T(8,128)(2,1)S(1)} %get-tuple-element.66), channel_id=1, source_target_pairs={{0,4},{1,5},{2,6},{3,7},{4,0},{5,1},{6,2},{7,3},{8,12},{9,13},{10,... | collective-permute-start | bytes 626696 | tf_op jit(solution)/shard_map/ppermute | solution.py:49
  156.2 15.3 %collective-permute-start.26 = (bf16[96,2048]{1,0:T(8,128)(2,1)S(1)}, bf16[96,2048]{1,0:T(8,128)(2,1)S(1)}, u32[]{:S(2)}, u32[]{:S(2)}) collective-permute-start(bf16[96,2048]{1,0:T(8,128)(2,1)S(1)} %pad_maximum_fusion.3), channel_id=1, source_target_pairs={{0,2},{1,3},{2,0},{3,1},{4,6},{5,7},{6,4},{7,5},{8,10},{9,11},{10,... | collective-permute-start | bytes 1179656 | tf_op jit(solution)/shard_map/ppermute | solution.py:49
  157.4 14.0 %collective-permute-start.28 = (bf16[96,2048]{1,0:T(8,128)(2,1)S(1)}, bf16[96,2048]{1,0:T(8,128)(2,1)S(1)}, u32[]{:S(2)}, u32[]{:S(2)}) collective-permute-start(bf16[96,2048]{1,0:T(8,128)(2,1)S(1)} %pad_maximum_fusion.4), channel_id=1, source_target_pairs={{0,4},{1,5},{2,6},{3,7},{4,0},{5,1},{6,2},{7,3},{8,12},{9,13},{10,... | collective-permute-start | bytes 1179656 | tf_op jit(solution)/shard_map/ppermute | solution.py:49
  164.7 16.3 %collective-permute-start.36 = (bf16[96,2176]{1,0:T(8,128)(2,1)S(1)}, bf16[96,2176]{1,0:T(8,128)(2,1)S(1)}, u32[]{:S(2)}, u32[]{:S(2)}) collective-permute-start(bf16[96,2176]{1,0:T(8,128)(2,1)S(1)} %pad_maximum_fusion.2), channel_id=1, source_target_pairs={{0,4},{1,5},{2,6},{3,7},{4,0},{5,1},{6,2},{7,3},{8,12},{9,13},{10,... | collective-permute-start | bytes 1253384 | tf_op jit(solution)/shard_map/ppermute | solution.py:49
  171.7 9.1 %collective-permute-start.29 = (bf16[24,2048]{1,0:T(8,128)(2,1)S(1)}, bf16[24,2048]{1,0:T(8,128)(2,1)S(1)}, u32[]{:S(2)}, u32[]{:S(2)}) collective-permute-start(bf16[24,2048]{1,0:T(8,128)(2,1)S(1)} %get-tuple-element.78), channel_id=1, source_target_pairs={{0,8},{1,9},{2,10},{3,11},{4,12},{5,13},{6,14},{7,15},{8,0},{9,1},... | collective-permute-start | bytes 294920 | tf_op jit(solution)/shard_map/ppermute | solution.py:49
  172.1 8.7 %collective-permute-start.31 = (bf16[24,2048]{1,0:T(8,128)(2,1)S(1)}, bf16[24,2048]{1,0:T(8,128)(2,1)S(1)}, u32[]{:S(2)}, u32[]{:S(2)}) collective-permute-start(bf16[24,2048]{1,0:T(8,128)(2,1)S(1)} %get-tuple-element.79), channel_id=1, source_target_pairs={{0,24},{1,25},{2,26},{3,27},{4,28},{5,29},{6,30},{7,31},{8,16},{9,... | collective-permute-start | bytes 294920 | tf_op jit(solution)/shard_map/ppermute | solution.py:49
  175.3 8.1 %collective-permute-start.34 = (bf16[96,2176]{1,0:T(8,128)(2,1)S(1)}, bf16[96,2176]{1,0:T(8,128)(2,1)S(1)}, u32[]{:S(2)}, u32[]{:S(2)}) collective-permute-start(bf16[96,2176]{1,0:T(8,128)(2,1)S(1)} %pad_maximum_fusion.1), channel_id=1, source_target_pairs={{0,2},{1,3},{2,0},{3,1},{4,6},{5,7},{6,4},{7,5},{8,10},{9,11},{10,... | collective-permute-start | bytes 1253384 | tf_op jit(solution)/shard_map/ppermute | solution.py:49
  183.5 10.0 %collective-permute-start.37 = (bf16[24,2176]{1,0:T(8,128)(2,1)S(1)}, bf16[24,2176]{1,0:T(8,128)(2,1)S(1)}, u32[]{:S(2)}, u32[]{:S(2)}) collective-permute-start(bf16[24,2176]{1,0:T(8,128)(2,1)S(1)} %get-tuple-element.75), channel_id=1, source_target_pairs={{0,8},{1,9},{2,10},{3,11},{4,12},{5,13},{6,14},{7,15},{8,0},{9,1},... | collective-permute-start | bytes 313352 | tf_op jit(solution)/shard_map/ppermute | solution.py:49
  184.9 8.6 %collective-permute-start.39 = (bf16[24,2176]{1,0:T(8,128)(2,1)S(1)}, bf16[24,2176]{1,0:T(8,128)(2,1)S(1)}, u32[]{:S(2)}, u32[]{:S(2)}) collective-permute-start(bf16[24,2176]{1,0:T(8,128)(2,1)S(1)} %get-tuple-element.76), channel_id=1, source_target_pairs={{0,24},{1,25},{2,26},{3,27},{4,28},{5,29},{6,30},{7,31},{8,16},{9,... | collective-permute-start | bytes 313352 | tf_op jit(solution)/shard_map/ppermute | solution.py:49
  (23 other events, 166.6 us)

commit v2 on v1

v2 whole, which is shorter than its diff:
```python
import functools

import jax
import jax.numpy as jnp
from jax import lax
from jax.experimental import pallas as pl
from jax.experimental.pallas import tpu as pltpu
from jax.sharding import PartitionSpec as P

LANES = 128
CHUNKS = 2
bf16, f32 = jnp.bfloat16, jnp.float32


def dot(a, b, dims):
    return lax.dot_general(a, b, ((dims[0], dims[1]), ((), ())), preferred_element_type=f32)


def add(*terms):
    total = terms[0].astype(f32)
    for term in terms[1:]:
        total = total + term.astype(f32)
    return total.astype(terms[0].dtype)


def tile(size, most):
    fits = [t for t in range(LANES, min(size, most) + 1, LANES) if size % t == 0]
    return fits[-1] if fits else size


def call(kernel, flops, moved, **kwargs):
    return pl.pallas_call(
        kernel,
        compiler_params=pltpu.CompilerParams(vmem_limit_bytes=52 * 1024 * 1024),
        cost_estimate=pl.CostEstimate(flops=flops, bytes_accessed=moved, transcendentals=0),
        **kwargs,
    )


def whole(*shape):
    return pl.BlockSpec(shape, lambda i: (0,) * len(shape))


CORE, X, Y, Z = 1, 2, 4, 8


def flip(value, mask):
    count = lax.axis_size("wide")
    return lax.ppermute(value, "wide", [(i, i ^ mask) for i in range(count)])


def after(value, *deps):
    return lax.optimization_barrier((value, *deps))[0]


def depth():
    return lax.axis_size("wide") // Z


def gather_z(shard):
    return jnp.concatenate([shard] + [flip(shard, Z * k) for k in range(1, depth())], axis=0)


def gather_sides(first):
    return flip(first, X), flip(first, Y)


def gather_far(by_x, by_y):
    half = by_x.shape[0] // 2
    return [flip(by_y[:half], X), flip(by_x[half:], Y)]


def gather_core(pieces):
    return pieces + [flip(piece, CORE) for piece in pieces]


def offsets():
    return [Z * k + m + c for c in (0, CORE) for m in (0, X, Y, X | Y) for k in range(depth())]


def quarters(mine):
    size = mine.shape[0] // 4
    return [mine[k * size : (k + 1) * size] for k in range(4)]


def scatter_far(mine):
    first, by_x, by_y, far = quarters(mine)
    half = far.shape[0] // 2
    to_y, to_x = flip(far[:half], X), flip(far[half:], Y)
    by_y = jnp.concatenate([add(by_y[:half], to_y), by_y[half:]], axis=0)
    by_x = jnp.concatenate([by_x[:half], add(by_x[half:], to_x)], axis=0)
    return first, by_x, by_y


def scatter_sides(first, by_x, by_y):
    return add(first, flip(by_x, X), flip(by_y, Y))


def scatter_z(first):
    step = first.shape[0] // depth()
    blocks = [first[k * step : (k + 1) * step] for k in range(depth())]
    return add(blocks[0], *[flip(blocks[k], Z * k) for k in range(1, depth())])


def meta_kernel(sizes, cols, *refs):
    pieces, (out_ref, sems) = refs[: len(sizes)], refs[len(sizes) :]
    starts = [sum(sizes[:k]) for k in range(len(sizes))]
    copies = [
        pltpu.make_async_copy(
            pieces[k].at[:, pl.ds(cols, LANES)], out_ref.at[pl.ds(starts[k], sizes[k]), :], sems.at[k]
        )
        for k in range(len(sizes))
    ]
    for copy in copies:
        copy.start()
    for copy in copies:
        copy.wait()


def gather_meta(pieces, cols):
    sizes = [piece.shape[0] for piece in pieces]
    return call(
        functools.partial(meta_kernel, sizes, cols),
        0,
        4 * sum(sizes) * LANES,
        grid=(1,),
        in_specs=[pl.BlockSpec(memory_space=pl.ANY)] * len(pieces),
        out_specs=whole(sum(sizes), LANES),
        out_shape=jax.ShapeDtypeStruct((sum(sizes), LANES), bf16),
        scratch_shapes=[pltpu.SemaphoreType.DMA((len(sizes),))],
    )(*pieces)


class Rows:
    def __init__(self, slot, pieces, rows, cols):
        self.slot, self.pieces, self.rows, self.cols = slot, pieces, rows, cols
        self.sizes = [piece.shape[0] for piece in pieces]
        self.total = sum(self.sizes)
        self.block = tile(cols, 512)
        self.steps = cols // self.block
        self.picked = slot is not None
        self.flops = 2 * rows * self.total * cols if self.picked else 0

    def args(self):
        return ([self.slot.reshape(1, self.total)] if self.picked else []) + list(self.pieces)

    def specs(self):
        if not self.picked:
            return [pl.BlockSpec((self.rows, self.block), lambda i: (0, i))]
        return [whole(1, self.total)] + [pl.BlockSpec(memory_space=pl.ANY)] * len(self.sizes)

    def scratch(self):
        if not self.picked:
            return []
        return [
            pltpu.VMEM((self.steps, self.total, self.block), bf16),
            pltpu.VMEM((self.rows, self.total), bf16),
            pltpu.SemaphoreType.DMA((self.steps, len(self.sizes))),
        ]

    def take(self, refs):
        args, scratch = len(self.sizes) + self.picked, len(self.scratch())
        return refs[:args], refs[args : len(refs) - scratch], refs[len(refs) - scratch :]

    def load(self, refs, scratch):
        if not self.picked:
            return refs[0][...]
        slot_ref, *pieces = refs
        held, place, sems = scratch
        step = pl.program_id(0)
        starts = [sum(self.sizes[:k]) for k in range(len(self.sizes))]

        def copy(at, k):
            return pltpu.make_async_copy(
                pieces[k].at[:, pl.ds(pl.multiple_of(at * self.block, LANES), self.block)],
                held.at[at, pl.ds(starts[k], self.sizes[k]), :],
                sems.at[at, k],
            )

        @pl.when(step == 0)
        def _():
            @pl.loop(0, self.steps)
            def _(at):
                for k in range(len(self.sizes)):
                    copy(at, k).start()

            number = lax.broadcasted_iota(jnp.int32, place.shape, 0)
            place[...] = jnp.where(number == slot_ref[...], 1.0, 0.0).astype(bf16)

        for k in range(len(self.sizes)):
            copy(step, k).wait()
        return dot(place[...], held[step], ((1,), (0,))).astype(bf16)


def pick_kernel(source, *refs):
    args, (out_ref,), scratch = source.take(refs)
    out_ref[...] = source.load(args, scratch)


def pick_rows(source):
    return call(
        functools.partial(pick_kernel, source),
        source.flops,
        2 * (source.rows + source.total) * source.cols,
        grid=(source.steps,),
        in_specs=source.specs(),
        out_specs=pl.BlockSpec((source.rows, source.block), lambda i: (0, i)),
        out_shape=jax.ShapeDtypeStruct((source.rows, source.cols), bf16),
        scratch_shapes=source.scratch(),
    )(*source.args())


def forward_kernel(source, *refs):
    args, rest, scratch = source.take(refs)
    gate_ref, up_ref, hidden_ref, active_ref, pull_ref, gate_sum, up_sum = rest
    step = pl.program_id(0)
    x = source.load(args, scratch)

    @pl.when(step == 0)
    def _():
        gate_sum[...] = dot(x, gate_ref[...], ((1,), (0,)))
        up_sum[...] = dot(x, up_ref[...], ((1,), (0,)))

    @pl.when(step > 0)
    def _():
        gate_sum[...] += dot(x, gate_ref[...], ((1,), (0,)))
        up_sum[...] += dot(x, up_ref[...], ((1,), (0,)))

    @pl.when(step == pl.num_programs(0) - 1)
    def _():
        units = gate_sum.shape[1]
        part = tile(units, 256)
        for low in range(0, units, part):
            gate_pre = gate_sum[:, low : low + part].T
            up_pre = up_sum[:, low : low + part].T
            sig = jax.nn.sigmoid(gate_pre)
            active = gate_pre * sig
            hidden_ref[low : low + part, :] = (active * up_pre).astype(bf16)
            active_ref[low : low + part, :] = active.astype(bf16)
            pull_ref[low : low + part, :] = (up_pre * (sig * (1.0 + gate_pre * (1.0 - sig)))).astype(bf16)


def forward(source, w_gate, w_up):
    rows, width = source.rows, source.cols
    units = w_gate.shape[1]
    weight = pl.BlockSpec((source.block, units), lambda i: (i, 0))
    return call(
        functools.partial(forward_kernel, source),
        4 * rows * width * units + source.flops,
        4 * width * units + 2 * source.total * width,
        grid=(source.steps,),
        in_specs=source.specs() + [weight, weight],
        out_specs=[whole(units, rows)] * 3,
        out_shape=[jax.ShapeDtypeStruct((units, rows), bf16)] * 3,
        scratch_shapes=[pltpu.VMEM((rows, units), f32)] * 2 + source.scratch(),
    )(*source.args(), w_gate, w_up)


def back_kernel(source, *refs):
    args, rest, scratch = source.take(refs)
    (gain_col, gain_row, down_ref, hidden_ref, active_ref, pull_ref) = rest[:6]
    (scaled_ref, d_gate_ref, d_up_ref, route_ref, back_sum) = rest[6:]
    step = pl.program_id(0)
    g = source.load(args, scratch)
    scaled_ref[...] = (gain_col[...] * g.astype(f32)).astype(bf16)
    g = g.T

    @pl.when(step == 0)
    def _():
        back_sum[...] = dot(down_ref[...], g, ((1,), (0,)))

    @pl.when(step > 0)
    def _():
        back_sum[...] += dot(down_ref[...], g, ((1,), (0,)))

    @pl.when(step == pl.num_programs(0) - 1)
    def _():
        units = back_sum.shape[0]
        part = tile(units, 256)
        route = jnp.zeros(route_ref.shape, f32)
        for low in range(0, units, part):
            at = slice(low, low + part)
            back = back_sum[at, :]
            d_hidden = gain_row[...] * back
            d_gate_ref[at, :] = (d_hidden * pull_ref[at, :].astype(f32)).astype(bf16)
            d_up_ref[at, :] = (d_hidden * active_ref[at, :].astype(f32)).astype(bf16)
            route = route + jnp.sum(hidden_ref[at, :].astype(f32) * back, axis=0, keepdims=True)
        route_ref[...] = route


def back_project(source, gain, w_down, hidden, active, pull):
    rows, width = source.rows, source.cols
    units = w_down.shape[0]
    unit = whole(units, rows)
    shape = jax.ShapeDtypeStruct((units, rows), bf16)
    return call(
        functools.partial(back_kernel, source),
        2 * rows * width * units + source.flops,
        2 * width * units + 2 * source.total * width,
        grid=(source.steps,),
        in_specs=source.specs()
        + [whole(rows, 1), whole(1, rows), pl.BlockSpec((units, source.block), lambda i: (0, i))]
        + [unit] * 3,
        out_specs=[pl.BlockSpec((rows, source.block), lambda i: (0, i)), unit, unit, whole(1, rows)],
        out_shape=[jax.ShapeDtypeStruct((rows, width), bf16), shape, shape, jax.ShapeDtypeStruct((1, rows), f32)],
        scratch_shapes=[pltpu.VMEM((units, rows), f32)] + source.scratch(),
    )(*source.args(), gain.reshape(rows, 1), gain.reshape(1, rows), w_down, hidden, active, pull)


def token_kernel(steps, spread, d_gate_ref, d_up_ref, slot_ref, route_ref, gate_ref, up_ref, *outs):
    step = pl.program_id(0)

    def store(part):
        half = slot_ref.shape[0] // 2
        width, rows = part.shape
        for k in range(2):
            slot = slot_ref[k * half : (k + 1) * half, :]
            lanes = lax.broadcasted_iota(jnp.int32, (half, rows), 1)
            place = jnp.where(lanes == slot, 1.0, 0.0).astype(bf16)
            outs[k][:, :width] = dot(place, part, ((1,), (1,))).astype(bf16)

    @pl.when(step < steps)
    def _():
        part = dot(gate_ref[...], d_gate_ref[...], ((1,), (0,)))
        part = (part + dot(up_ref[...], d_up_ref[...], ((1,), (0,)))).astype(bf16)
        if spread:
            store(part)
        else:
            outs[0][...] = part.T

    if spread:

        @pl.when(step >= steps)
        def _():
            store(route_ref[...])


def token_grad(d_gate, d_up, slot, route, w_gate, w_up, chunk, chunks, spread):
    units, rows = d_gate.shape
    width = w_gate.shape[0] // chunks
    total = slot.shape[0]
    block = tile(width, 512)
    steps = width // block
    first = chunk * steps
    extra = route.shape[0] if spread and chunk == chunks - 1 else 0
    weight = pl.BlockSpec((block, units), lambda i: (first + jnp.minimum(i, steps - 1), 0))
    out_rows = [total // 2] * 2 if spread else [rows]
    return call(
        functools.partial(token_kernel, steps, spread),
        4 * rows * width * units + 2 * rows * width * total * spread,
        4 * width * units + 2 * total * width,
        grid=(steps + (extra > 0),),
        in_specs=[whole(units, rows), whole(units, rows), whole(total, 1), whole(*route.shape), weight, weight],
        out_specs=[pl.BlockSpec((n, block), lambda i: (0, i)) for n in out_rows],
        out_shape=[jax.ShapeDtypeStruct((n, width + extra), bf16) for n in out_rows],
    )(d_gate, d_up, slot.reshape(total, 1), route, w_gate, w_up)


def down_kernel(hidden_ref, scaled_ref, *refs):
    refs[-1][...] = dot(hidden_ref[...], scaled_ref[...], ((1,), (0,))).astype(bf16)


def down_grad(hidden, scaled, chunk, chunks, into):
    units, rows = hidden.shape
    width = scaled.shape[1]
    block = tile(width // chunks, 512)
    steps = width // chunks // block
    first = chunk * steps
    kept = [] if into is None else [into]
    return call(
        down_kernel,
        2 * rows * width * units // chunks,
        2 * width * units // chunks,
        grid=(steps,),
        in_specs=[whole(units, rows), pl.BlockSpec((rows, block), lambda i: (0, first + i))]
        + [pl.BlockSpec(memory_space=pl.ANY)] * len(kept),
        out_specs=pl.BlockSpec((units, block), lambda i: (0, first + i)),
        out_shape=jax.ShapeDtypeStruct((units, width), bf16),
        input_output_aliases={2: 0} if kept else {},
    )(hidden, scaled, *kept)


def body(tokens, grad_out, expert_ids, route_weights, w_gate, w_up, w_down):
    wide_count = lax.axis_size("wide")
    narrow_count = lax.axis_size("narrow")
    local_experts = w_gate.shape[0]
    experts_all = local_experts * wide_count
    tok_count, top_count = expert_ids.shape
    capacity = min(tok_count, 2 * tok_count * top_count // experts_all)
    rows = wide_count * capacity
    total = wide_count * tok_count
    cols = tokens.shape[1]
    me = lax.axis_index("wide")
    pad = -2 * top_count % LANES
    meta = jnp.concatenate(
        [expert_ids.astype(bf16), route_weights, jnp.zeros((tok_count, pad), bf16)], axis=1
    )
    first_t = gather_z(jnp.concatenate([tokens, meta], axis=1))
    x_t, y_t = gather_sides(first_t)
    first_g = gather_z(after(grad_out, first_t))
    far_t = gather_far(x_t, y_t)
    x_g, y_g = gather_sides(after(first_g, *far_t))
    pieces_t = gather_core([first_t, x_t, y_t] + far_t)
    all_meta = gather_meta(pieces_t, cols)
    all_ids = all_meta[:, :top_count].astype(jnp.int32)
    all_weights = all_meta[:, top_count : 2 * top_count].astype(f32)
    first = me * local_experts
    fused = narrow_count == 1 and local_experts == 1
    chunks = CHUNKS if fused else 1
    picked = []
    for j in range(local_experts):
        match = all_ids == first + j
        chosen = jnp.any(match, axis=1)
        gain = jnp.sum(jnp.where(match, all_weights, 0.0), axis=1)
        rank = jnp.cumsum(chosen.astype(jnp.int32)) - 1
        slot = jnp.where(chosen, rank, -1)
        place = slot[None, :] == jnp.arange(rows, dtype=jnp.int32)[:, None]
        row_gain = jnp.sum(jnp.where(place, gain[None, :], 0.0), axis=1)
        source = Rows(slot, pieces_t, rows, cols)
        if narrow_count > 1:
            x = lax.all_gather(pick_rows(source), "narrow", axis=1, tiled=True)
            source = Rows(None, [x], rows, x.shape[1])
        picked.append((slot, place, row_gain, forward(source, w_gate[j], w_up[j])))
    x_g, y_g, *_ = lax.optimization_barrier((x_g, y_g, *[ahead[0] for *_, ahead in picked]))
    pieces_g = gather_core([first_g, x_g, y_g] + gather_far(x_g, y_g))
    expert_cols = experts_all + -experts_all % LANES
    dense = [0, 0]
    ends = []
    for j in range(local_experts):
        slot, place, row_gain, (hidden, active, pull) = picked[j]
        source = Rows(slot, pieces_g, rows, cols)
        if narrow_count > 1:
            g = lax.all_gather(pick_rows(source), "narrow", axis=1, tiled=True)
            source = Rows(None, [g], rows, g.shape[1])
        scaled, d_gate, d_up, route = back_project(source, row_gain, w_down[j], hidden, active, pull)
        route = lax.psum(route.astype(bf16).astype(f32), "narrow")
        at = jnp.arange(expert_cols, dtype=jnp.int32) == first + j
        route = jnp.where(at[:, None], route, 0.0).astype(bf16)
        ends.append((hidden, scaled))
        if fused:
            own, other = token_grad(d_gate, d_up, slot, route, w_gate[j], w_up[j], 0, chunks, True)
            dense = [own, other]
            continue
        (part,) = token_grad(d_gate, d_up, slot, route, w_gate[j], w_up[j], 0, 1, False)
        part = lax.psum_scatter(part, "narrow", scatter_dimension=1, tiled=True)
        part = jnp.concatenate([part, route.T], axis=1)
        part = dot(place.astype(bf16), part, ((0,), (0,)))
        dense = [dense[0] + part[: total // 2], dense[1] + part[total // 2 :]]
    mine = [add(dense[0].astype(bf16), flip(dense[1].astype(bf16), CORE))]
    if fused and chunks == 2:
        own, other = token_grad(after(d_gate, dense[0]), d_up, slot, route, w_gate[0], w_up[0], 1, chunks, True)
        mine[0] = add(after(dense[0], own), flip(dense[1], CORE))
        mine.append(add(own, flip(other, CORE)))
    sides = [scatter_far(rows_) for rows_ in mine]
    firsts = [scatter_sides(*side) for side in sides]
    shares = [scatter_z(first_) for first_ in firsts]
    grad_downs = []
    for hidden, scaled in ends:
        out = down_grad(after(hidden, mine[0]), scaled, 0, 2, None)
        grad_downs.append(down_grad(after(hidden, *sides[0]), scaled, 1, 2, out))
    joined = jnp.concatenate(shares, axis=1)
    width = tokens.shape[1]
    by_expert = joined[:, width : width + experts_all].astype(f32)
    pick = expert_ids[:, :, None] == jnp.arange(experts_all, dtype=jnp.int32)[None, None, :]
    grad_route = jnp.sum(jnp.where(pick, by_expert[:, None, :], 0.0), axis=2)
    return (joined[:, :width], grad_route.astype(bf16), jnp.stack(grad_downs))


def solution(mesh):
    in_specs = (
        P("wide", "narrow"),
        P("wide", "narrow"),
        P("wide", None),
        P("wide", None),
        P("wide", None, "narrow"),
        P("wide", None, "narrow"),
        P("wide", "narrow", None),
    )
    out_specs = (P("wide", "narrow"), P("wide", None), P("wide", "narrow", None))
    return jax.shard_map(body, mesh=mesh, in_specs=in_specs, out_specs=out_specs, check_vma=False)
```

time: 196 us -> 199 us (1.015)
  waiting for transfers between devices: 46.2 us -> 62.1 us
  Pallas kernels: 91 us -> 80.9 us
    ppermute x40, waiting for transfers between devices: 46.2 us -> 62.1 us  [flip(): return lax.ppermute(value, 'wide', [(i, i ^ mask) for i in range(count)])]
    pallas_call x9 -> x4, Pallas kernels: 67.6 us -> 54.5 us  [the longest x1 22.3 us: forward(): call(functools.partial(forward_kernel, source), 4 * rows * width * units...]
    pallas_call x2, Pallas kernels: 22.6 us -> 25.6 us  [token_grad(): call(functools.partial(token_kernel, steps, spread), 4 * rows * width * u...]
    unnamed x37 -> x31, local copies, waits for them, and re-layouts: 7.85 us -> 6.96 us
  transfers between devices with their start and end apart: 40 -> 40, of which waited for: 14 -> 15; matrix products, arithmetic and copies ran while one was open for 5% -> 5% of each run, Pallas kernels for 31% -> 25%
where the time goes in v2:
time: 199 us
  Pallas kernels  80.9 us (41%)
  waiting for transfers between devices  62.1 us (31%)
  starting transfers between devices  37 us (19%)
  local copies, waits for them, and re-layouts  11.3 us (6%)
  other arithmetic  6.16 us (3%)
    ppermute x40, waiting for transfers between devices, flip(): return lax.ppermute(value, 'wide', [(i, i ^ mask) for i in range(count)])  62.1 us
    ppermute x40, starting transfers between devices, flip(): return lax.ppermute(value, 'wide', [(i, i ^ mask) for i in range(count)])  37 us
    pallas_call x2, Pallas kernels, token_grad(): call(functools.partial(token_kernel, steps, spread), 4 * rows * width * u...  25.6 us
    pallas_call x1, Pallas kernels, forward(): call(functools.partial(forward_kernel, source), 4 * rows * width * units...  22.3 us
    pallas_call x1, Pallas kernels, back_project(): call(functools.partial(back_kernel, source), 2 * rows * width * units + s...  18.9 us
    pallas_call x2, Pallas kernels, down_grad(): call(down_kernel, 2 * rows * width * units // chunks, 2 * width * units /...  13.2 us
    unnamed x31, local copies, waits for them, and re-layouts  6.96 us
  transfers between devices with their start and end apart: 40, of which 15 were waited for; matrix products, arithmetic and copies ran while one was open for 5% of the time, Pallas kernels for 25%

profile of v2, /device:TPU:0, one launch (start us, length us, event | category | flops | bytes accessed | tf_op | source)
XLA Modules:
  0.0 198.5 jit_solution(4423980786000805818)
XLA Ops:
  3.2 5.1 %collective-permute-start.2 = (bf16[24,4224]{1,0:T(8,128)(2,1)S(1)}, bf16[24,4224]{1,0:T(8,128)(2,1)S(1)}, u32[]{:S(2)}, u32[]{:S(2)}) collective-permute-start(bf16[24,4224]{1,0:T(8,128)(2,1)S(1)} %concatenate.24), channel_id=1, source_target_pairs={{0,24},{1,25},{2,26},{3,27},{4,28},{5,29},{6,30},{7,31},{8,16},{9,... | collective-permute-start | bytes 608264 | tf_op jit(solution)/shard_map/ppermute | solution.py:49
  8.9 5.4 %collective-permute-done.2 = bf16[24,4224]{1,0:T(8,128)(2,1)S(1)} collective-permute-done((bf16[24,4224]{1,0:T(8,128)(2,1)S(1)}, bf16[24,4224]{1,0:T(8,128)(2,1)S(1)}, u32[]{:S(2)}, u32[]{:S(2)}) %collective-permute-start.2) | collective-permute-done | bytes 202784 | tf_op jit(solution)/shard_map/ppermute | solution.py:49
  14.3 11.2 %collective-permute-done.1 = bf16[24,4224]{1,0:T(8,128)(2,1)S(1)} collective-permute-done((bf16[24,4224]{1,0:T(8,128)(2,1)S(1)}, bf16[24,4224]{1,0:T(8,128)(2,1)S(1)}, u32[]{:S(2)}, u32[]{:S(2)}) %collective-permute-start.1) | collective-permute-done | bytes 202784 | tf_op jit(solution)/shard_map/ppermute | solution.py:49
  25.6 2.5 %collective-permute-start.14 = (bf16[24,4096]{1,0:T(8,128)(2,1)}, bf16[24,4096]{1,0:T(8,128)(2,1)S(1)}, u32[]{:S(2)}, u32[]{:S(2)}) collective-permute-start(bf16[24,4096]{1,0:T(8,128)(2,1)} %param.8), channel_id=1, source_target_pairs={{0,24},{1,25},{2,26},{3,27},{4,28},{5,29},{6,30},{7,31},{8,16},{9,... | collective-permute-start | bytes 589832 | tf_op jit(solution)/shard_map/ppermute | solution.py:49
  28.1 1.9 collective-permute-start.12
  30.0 1.5 collective-permute-start.4
  31.6 1.5 collective-permute-start.3
  33.1 1.6 constant_dynamic-update-slice_fusion.3
  34.7 5.6 %collective-permute-done.12 = bf16[24,4096]{1,0:T(8,128)(2,1)S(1)} collective-permute-done((bf16[24,4096]{1,0:T(8,128)(2,1)}, bf16[24,4096]{1,0:T(8,128)(2,1)S(1)}, u32[]{:S(2)}, u32[]{:S(2)}) %collective-permute-start.12) | collective-permute-done | bytes 196640 | tf_op jit(solution)/shard_map/ppermute | solution.py:49
  40.9 7.4 %collective-permute-done.4.refs_2_.refs_3_ = bf16[96,4224]{1,0:T(8,128)(2,1)S(1)} collective-permute-done((bf16[96,4224]{1,0:T(8,128)(2,1)S(1)}, bf16[96,4224]{1,0:T(8,128)(2,1)S(1)}, u32[]{:S(2)}, u32[]{:S(2)}) %collective-permute-start.4) | collective-permute-done | bytes 811040 | tf_op jit(solution)/shard_map/ppermute | solution.py:49
  48.4 1.6 collective-permute-start.5
  52.7 5.5 %collective-permute-done.5.refs_3_.refs_4_ = bf16[48,4224]{1,0:T(8,128)(2,1)S(1)} collective-permute-done((bf16[48,4224]{1,0:T(8,128)(2,1)S(1)}, bf16[48,4224]{1,0:T(8,128)(2,1)S(1)}, u32[]{:S(2)}, u32[]{:S(2)}) %collective-permute-start.5) | collective-permute-done | bytes 405536 | tf_op jit(solution)/shard_map/ppermute | solution.py:49
  64.1 22.3 %shard_map.95 = (bf16[1536,384]{1,0:T(8,128)(2,1)}, bf16[1536,384]{1,0:T(8,128)(2,1)}, bf16[1536,384]{1,0:T(8,128)(2,1)}) custom-call(s32[1,768]{1,0:T(1,128)S(1)} %get-tuple-element.47.refs_0_, bf16[96,4224]{1,0:T(8,128)(2,1)} %copy-done.2, bf16[96,4224]{1,0:T(8,128)(2,1)} %copy-done.4, bf16[96,4224]{1,0:T(8,128)(2,1)} %copy-done.3, ...), custom_call_target="tpu_custom_call" | custom-call | flops 12079595520 | bytes 31457280 | tf_op jit(solution)/shard_map/pallas_call | solution.py:247
  91.2 7.0 %collective-permute-done.17.refs_4_ = bf16[48,4096]{1,0:T(8,128)(2,1)S(1)} collective-permute-done((bf16[48,4096]{1,0:T(8,128)(2,1)S(1)}, bf16[48,4096]{1,0:T(8,128)(2,1)S(1)}, u32[]{:S(2)}, u32[]{:S(2)}) %collective-permute-start.17) | collective-permute-done | bytes 393248 | tf_op jit(solution)/shard_map/ppermute | solution.py:49
  98.2 2.2 %collective-permute-done.18.refs_5_ = bf16[48,4096]{1,0:T(8,128)(2,1)S(1)} collective-permute-done((bf16[48,4096]{1,0:T(8,128)(2,1)S(1)}, bf16[48,4096]{1,0:T(8,128)(2,1)S(1)}, u32[]{:S(2)}, u32[]{:S(2)}) %collective-permute-start.18) | collective-permute-done | bytes 393248 | tf_op jit(solution)/shard_map/ppermute | solution.py:49
  102.3 18.9 %shard_map.96 = (bf16[384,4096]{1,0:T(8,128)(2,1)}, bf16[1536,384]{1,0:T(8,128)(2,1)}, bf16[1536,384]{1,0:T(8,128)(2,1)}, f32[1,384]{1,0:T(1,128)S(1)}) custom-call(s32[1,768]{1,0:T(1,128)S(1)} %get-tuple-element.47.refs_0_, bf16[96,4096]{1,0:T(8,128)(2,1)} %constant_dynamic-update-slice_fusion.refs_1_, bf16[96,4096]{1,0:T(8,128)(2,1)} %collective-permute-done.15.refs_2_, ...), custom_call_target="tpu_custom_call" | custom-call | flops 7247757312 | bytes 18874368 | tf_op jit(solution)/shard_map/pallas_call | solution.py:296
  121.4 1.3 copy-done.1
  122.7 12.6 %shard_map.97 = (bf16[384,2048]{1,0:T(8,128)(2,1)}, bf16[384,2048]{1,0:T(8,128)(2,1)}) custom-call(bf16[1536,384]{1,0:T(8,128)(2,1)S(1)} %copy-done.1, bf16[1536,384]{1,0:T(8,128)(2,1)} %get-tuple-element.30.d_up_ref, s32[768,1]{1,0:T(8,128)S(1)} %bitcast_select_fusion.slot_ref, bf16[128,384]{1,0:T(8,128)(2,1)S(1)} %select_convert_fusion.route_ref, ...), custom_call_target="tpu_custom_call" | custom-call | flops 6039797760 | bytes 15728640 | tf_op jit(solution)/shard_map/pallas_call | solution.py:348
  135.7 13.0 %shard_map.98 = (bf16[384,2176]{1,0:T(8,128)(2,1)}, bf16[384,2176]{1,0:T(8,128)(2,1)}) custom-call(bf16[1536,384]{1,0:T(8,128)(2,1)S(1)} %copy-done.1, bf16[1536,384]{1,0:T(8,128)(2,1)} %get-tuple-element.30.d_up_ref, s32[768,1]{1,0:T(8,128)S(1)} %bitcast_select_fusion.slot_ref, bf16[128,384]{1,0:T(8,128)(2,1)S(1)} %select_convert_fusion.route_ref, ...), custom_call_target="tpu_custom_call" | custom-call | flops 6039797760 | bytes 15728640 | tf_op jit(solution)/shard_map/pallas_call | solution.py:348
  148.8 2.0 %add_convert_fusion.1 = bf16[384,2048]{1,0:T(8,128)(2,1)S(1)} fusion(bf16[384,2048]{1,0:T(8,128)(2,1)} %collective-permute-done.24, bf16[384,2048]{1,0:T(8,128)(2,1)S(1)} %copy-done.6), kind=kLoop, calls=%fused_computation.1 | loop fusion | flops 3145728 | bytes 4718592 | tf_op jit(solution)/shard_map/convert_element_type | solution.py:23
  151.5 1.7 collective-permute-start.25
  153.2 6.7 %shard_map.99.refs_0_ = bf16[1536,4096]{1,0:T(8,128)(2,1)} custom-call(bf16[1536,384]{1,0:T(8,128)(2,1)S(1)} %copy-done, bf16[384,4096]{1,0:T(8,128)(2,1)} %get-tuple-element.39.scaled_ref), custom_call_target="tpu_custom_call" | custom-call | flops 2415919104 | bytes 6291456 | tf_op jit(solution)/shard_map/pallas_call | solution.py:370
  163.3 1.5 collective-permute-start.26
  164.8 6.6 %shard_map.100 = bf16[1536,4096]{1,0:T(8,128)(2,1)} custom-call(bf16[1536,384]{1,0:T(8,128)(2,1)S(1)} %copy-done, bf16[384,4096]{1,0:T(8,128)(2,1)} %get-tuple-element.39.scaled_ref, bf16[1536,4096]{1,0:T(8,128)(2,1)} %shard_map.99.refs_0_), custom_call_target="tpu_custom_call", output_to_operand_aliasing={{}: (2, {})} | custom-call | flops 2415919104 | bytes 6291456 | tf_op jit(solution)/shard_map/pallas_call | solution.py:370
  172.0 1.5 collective-permute-start.34
  173.5 4.0 %collective-permute-done.28 = bf16[96,2048]{1,0:T(8,128)(2,1)S(1)} collective-permute-done((bf16[96,2048]{1,0:T(8,128)(2,1)S(1)}, bf16[96,2048]{1,0:T(8,128)(2,1)S(1)}, u32[]{:S(2)}, u32[]{:S(2)}) %collective-permute-start.28) | collective-permute-done | bytes 393248 | tf_op jit(solution)/shard_map/ppermute | solution.py:49
  177.9 2.4 %collective-permute-start.31 = (bf16[24,2048]{1,0:T(8,128)(2,1)S(1)}, bf16[24,2048]{1,0:T(8,128)(2,1)S(1)}, u32[]{:S(2)}, u32[]{:S(2)}) collective-permute-start(bf16[24,2048]{1,0:T(8,128)(2,1)S(1)} %get-tuple-element.65), channel_id=1, source_target_pairs={{0,24},{1,25},{2,26},{3,27},{4,28},{5,29},{6,30},{7,31},{8,16},{9,... | collective-permute-start | bytes 294920 | tf_op jit(solution)/shard_map/ppermute | solution.py:49
  181.3 3.8 %collective-permute-done.36 = bf16[96,2176]{1,0:T(8,128)(2,1)S(1)} collective-permute-done((bf16[96,2176]{1,0:T(8,128)(2,1)S(1)}, bf16[96,2176]{1,0:T(8,128)(2,1)S(1)}, u32[]{:S(2)}, u32[]{:S(2)}) %collective-permute-start.36) | collective-permute-done | bytes 417824 | tf_op jit(solution)/shard_map/ppermute | solution.py:49
  185.6 2.4 %collective-permute-start.39 = (bf16[24,2176]{1,0:T(8,128)(2,1)S(1)}, bf16[24,2176]{1,0:T(8,128)(2,1)S(1)}, u32[]{:S(2)}, u32[]{:S(2)}) collective-permute-start(bf16[24,2176]{1,0:T(8,128)(2,1)S(1)} %get-tuple-element.62), channel_id=1, source_target_pairs={{0,24},{1,25},{2,26},{3,27},{4,28},{5,29},{6,30},{7,31},{8,16},{9,... | collective-permute-start | bytes 313352 | tf_op jit(solution)/shard_map/ppermute | solution.py:49
  188.9 2.4 %collective-permute-done.37 = bf16[24,2176]{1,0:T(8,128)(2,1)S(1)} collective-permute-done((bf16[24,2176]{1,0:T(8,128)(2,1)S(1)}, bf16[24,2176]{1,0:T(8,128)(2,1)S(1)}, u32[]{:S(2)}, u32[]{:S(2)}) %collective-permute-start.37) | collective-permute-done | bytes 104480 | tf_op jit(solution)/shard_map/ppermute | solution.py:49
  191.4 1.8 collective-permute-done.39
  193.1 3.8 %collective-permute-done.38 = bf16[24,2176]{1,0:T(8,128)(2,1)S(1)} collective-permute-done((bf16[24,2176]{1,0:T(8,128)(2,1)S(1)}, bf16[24,2176]{1,0:T(8,128)(2,1)S(1)}, u32[]{:S(2)}, u32[]{:S(2)}) %collective-permute-start.38) | collective-permute-done | bytes 104480 | tf_op jit(solution)/shard_map/ppermute | solution.py:49
  (132 shorter events, 29.0 us)
Async XLA Ops:
  3.2 11.1 %collective-permute-start.2 = (bf16[24,4224]{1,0:T(8,128)(2,1)S(1)}, bf16[24,4224]{1,0:T(8,128)(2,1)S(1)}, u32[]{:S(2)}, u32[]{:S(2)}) collective-permute-start(bf16[24,4224]{1,0:T(8,128)(2,1)S(1)} %concatenate.24), channel_id=1, source_target_pairs={{0,24},{1,25},{2,26},{3,27},{4,28},{5,29},{6,30},{7,31},{8,16},{9,... | collective-permute-start | bytes 608264 | tf_op jit(solution)/shard_map/ppermute | solution.py:49
  8.3 17.2 %collective-permute-start.1 = (bf16[24,4224]{1,0:T(8,128)(2,1)S(1)}, bf16[24,4224]{1,0:T(8,128)(2,1)S(1)}, u32[]{:S(2)}, u32[]{:S(2)}) collective-permute-start(bf16[24,4224]{1,0:T(8,128)(2,1)S(1)} %concatenate.24), channel_id=1, source_target_pairs={{0,16},{1,17},{2,18},{3,19},{4,20},{5,21},{6,22},{7,23},{8,24},{9,... | collective-permute-start | bytes 608264 | tf_op jit(solution)/shard_map/ppermute | solution.py:49
  8.3 17.2 %collective-permute-start = (bf16[24,4224]{1,0:T(8,128)(2,1)S(1)}, bf16[24,4224]{1,0:T(8,128)(2,1)S(1)}, u32[]{:S(2)}, u32[]{:S(2)}) collective-permute-start(bf16[24,4224]{1,0:T(8,128)(2,1)S(1)} %concatenate.24), channel_id=1, source_target_pairs={{0,8},{1,9},{2,10},{3,11},{4,12},{5,13},{6,14},{7,15},{8,0},{9,1},... | collective-permute-start | bytes 608264 | tf_op jit(solution)/shard_map/ppermute | solution.py:49
  25.6 26.0 %collective-permute-start.14 = (bf16[24,4096]{1,0:T(8,128)(2,1)}, bf16[24,4096]{1,0:T(8,128)(2,1)S(1)}, u32[]{:S(2)}, u32[]{:S(2)}) collective-permute-start(bf16[24,4096]{1,0:T(8,128)(2,1)} %param.8), channel_id=1, source_target_pairs={{0,24},{1,25},{2,26},{3,27},{4,28},{5,29},{6,30},{7,31},{8,16},{9,... | collective-permute-start | bytes 589832 | tf_op jit(solution)/shard_map/ppermute | solution.py:49
  28.1 23.4 %collective-permute-start.13 = (bf16[24,4096]{1,0:T(8,128)(2,1)}, bf16[24,4096]{1,0:T(8,128)(2,1)S(1)}, u32[]{:S(2)}, u32[]{:S(2)}) collective-permute-start(bf16[24,4096]{1,0:T(8,128)(2,1)} %param.8), channel_id=1, source_target_pairs={{0,16},{1,17},{2,18},{3,19},{4,20},{5,21},{6,22},{7,23},{8,24},{9,... | collective-permute-start | bytes 589832 | tf_op jit(solution)/shard_map/ppermute | solution.py:49
  28.1 12.1 %collective-permute-start.12 = (bf16[24,4096]{1,0:T(8,128)(2,1)}, bf16[24,4096]{1,0:T(8,128)(2,1)S(1)}, u32[]{:S(2)}, u32[]{:S(2)}) collective-permute-start(bf16[24,4096]{1,0:T(8,128)(2,1)} %param.8), channel_id=1, source_target_pairs={{0,8},{1,9},{2,10},{3,11},{4,12},{5,13},{6,14},{7,15},{8,0},{9,1},... | collective-permute-start | bytes 589832 | tf_op jit(solution)/shard_map/ppermute | solution.py:49
  30.0 18.3 %collective-permute-start.4 = (bf16[96,4224]{1,0:T(8,128)(2,1)S(1)}, bf16[96,4224]{1,0:T(8,128)(2,1)S(1)}, u32[]{:S(2)}, u32[]{:S(2)}) collective-permute-start(bf16[96,4224]{1,0:T(8,128)(2,1)S(1)} %pad_maximum_fusion.refs_0_.refs_1_), channel_id=1, source_target_pairs={{0,4},{1,5},{2,6},{3,7},{4,0},{5,1},{6,2},{7,3},{8,12},{9,13},{10,... | collective-permute-start | bytes 2433032 | tf_op jit(solution)/shard_map/ppermute | solution.py:49
  31.6 19.1 %collective-permute-start.3 = (bf16[96,4224]{1,0:T(8,128)(2,1)S(1)}, bf16[96,4224]{1,0:T(8,128)(2,1)S(1)}, u32[]{:S(2)}, u32[]{:S(2)}) collective-permute-start(bf16[96,4224]{1,0:T(8,128)(2,1)S(1)} %pad_maximum_fusion.refs_0_.refs_1_), channel_id=1, source_target_pairs={{0,2},{1,3},{2,0},{3,1},{4,6},{5,7},{6,4},{7,5},{8,10},{9,11},{10,... | collective-permute-start | bytes 2433032 | tf_op jit(solution)/shard_map/ppermute | solution.py:49
  40.2 19.2 %collective-permute-start.7 = (bf16[96,4224]{1,0:T(8,128)(2,1)S(1)}, bf16[96,4224]{1,0:T(8,128)(2,1)S(1)}, u32[]{:S(2)}, u32[]{:S(2)}) collective-permute-start(bf16[96,4224]{1,0:T(8,128)(2,1)S(1)} %pad_maximum_fusion.refs_0_.refs_1_), channel_id=1, source_target_pairs={{0,1},{1,0},{2,3},{3,2},{4,5},{5,4},{6,7},{7,6},{8,9},{9,8},{10,11... | collective-permute-start | bytes 2433032 | tf_op jit(solution)/shard_map/ppermute | solution.py:49
  48.4 9.9 %collective-permute-start.5 = (bf16[48,4224]{1,0:T(8,128)(2,1)S(1)}, bf16[48,4224]{1,0:T(8,128)(2,1)S(1)}, u32[]{:S(2)}, u32[]{:S(2)}) collective-permute-start(bf16[48,4224]{1,0:T(8,128)(2,1)S(1)} %slice.147), channel_id=1, source_target_pairs={{0,2},{1,3},{2,0},{3,1},{4,6},{5,7},{6,4},{7,5},{8,10},{9,11},{10,... | collective-permute-start | bytes 1216520 | tf_op jit(solution)/shard_map/ppermute | solution.py:49
  51.5 9.1 %collective-permute-start.9 = (bf16[96,4224]{1,0:T(8,128)(2,1)S(1)}, bf16[96,4224]{1,0:T(8,128)(2,1)S(1)}, u32[]{:S(2)}, u32[]{:S(2)}) collective-permute-start(bf16[96,4224]{1,0:T(8,128)(2,1)S(1)} %collective-permute-done.4.refs_2_.refs_3_), channel_id=1, source_target_pairs={{0,1},{1,0},{2,3},{3,2},{4,5},{5,4},{6,7},{7,6},{8,9},{9,8},{10,11... | collective-permute-start | bytes 2433032 | tf_op jit(solution)/shard_map/ppermute | solution.py:49
  51.5 9.9 %collective-permute-start.8 = (bf16[96,4224]{1,0:T(8,128)(2,1)S(1)}, bf16[96,4224]{1,0:T(8,128)(2,1)S(1)}, u32[]{:S(2)}, u32[]{:S(2)}) collective-permute-start(bf16[96,4224]{1,0:T(8,128)(2,1)S(1)} %collective-permute-done.3.refs_1_.refs_2_), channel_id=1, source_target_pairs={{0,1},{1,0},{2,3},{3,2},{4,5},{5,4},{6,7},{7,6},{8,9},{9,8},{10,11... | collective-permute-start | bytes 2433032 | tf_op jit(solution)/shard_map/ppermute | solution.py:49
  59.5 26.9 %collective-permute-start.16 = (bf16[96,4096]{1,0:T(8,128)(2,1)}, bf16[96,4096]{1,0:T(8,128)(2,1)}, u32[]{:S(2)}, u32[]{:S(2)}) collective-permute-start(bf16[96,4096]{1,0:T(8,128)(2,1)} %constant_dynamic-update-slice_fusion.refs_1_), channel_id=1, source_target_pairs={{0,4},{1,5},{2,6},{3,7},{4,0},{5,1},{6,2},{7,3},{8,12},{9,13},{10,... | collective-permute-start | bytes 2359304 | tf_op jit(solution)/shard_map/ppermute | solution.py:49
  60.6 25.8 %collective-permute-start.15 = (bf16[96,4096]{1,0:T(8,128)(2,1)}, bf16[96,4096]{1,0:T(8,128)(2,1)}, u32[]{:S(2)}, u32[]{:S(2)}) collective-permute-start(bf16[96,4096]{1,0:T(8,128)(2,1)} %constant_dynamic-update-slice_fusion.refs_1_), channel_id=1, source_target_pairs={{0,2},{1,3},{2,0},{3,1},{4,6},{5,7},{6,4},{7,5},{8,10},{9,11},{10,... | collective-permute-start | bytes 2359304 | tf_op jit(solution)/shard_map/ppermute | solution.py:49
  87.4 10.8 %collective-permute-start.17 = (bf16[48,4096]{1,0:T(8,128)(2,1)S(1)}, bf16[48,4096]{1,0:T(8,128)(2,1)S(1)}, u32[]{:S(2)}, u32[]{:S(2)}) collective-permute-start(bf16[48,4096]{1,0:T(8,128)(2,1)S(1)} %slice.120), channel_id=1, source_target_pairs={{0,2},{1,3},{2,0},{3,1},{4,6},{5,7},{6,4},{7,5},{8,10},{9,11},{10,... | collective-permute-start | bytes 1179656 | tf_op jit(solution)/shard_map/ppermute | solution.py:49
  89.7 10.8 %collective-permute-start.18 = (bf16[48,4096]{1,0:T(8,128)(2,1)S(1)}, bf16[48,4096]{1,0:T(8,128)(2,1)S(1)}, u32[]{:S(2)}, u32[]{:S(2)}) collective-permute-start(bf16[48,4096]{1,0:T(8,128)(2,1)S(1)} %slice.121), channel_id=1, source_target_pairs={{0,4},{1,5},{2,6},{3,7},{4,0},{5,1},{6,2},{7,3},{8,12},{9,13},{10,... | collective-permute-start | bytes 1179656 | tf_op jit(solution)/shard_map/ppermute | solution.py:49
  90.6 10.8 %collective-permute-start.19 = (bf16[96,4096]{1,0:T(8,128)(2,1)}, bf16[96,4096]{1,0:T(8,128)(2,1)S(1)}, u32[]{:S(2)}, u32[]{:S(2)}) collective-permute-start(bf16[96,4096]{1,0:T(8,128)(2,1)} %constant_dynamic-update-slice_fusion.refs_1_), channel_id=1, source_target_pairs={{0,1},{1,0},{2,3},{3,2},{4,5},{5,4},{6,7},{7,6},{8,9},{9,8},{10,11... | collective-permute-start | bytes 2359304 | tf_op jit(solution)/shard_map/ppermute | solution.py:49
  90.7 11.6 %collective-permute-start.20 = (bf16[96,4096]{1,0:T(8,128)(2,1)}, bf16[96,4096]{1,0:T(8,128)(2,1)}, u32[]{:S(2)}, u32[]{:S(2)}) collective-permute-start(bf16[96,4096]{1,0:T(8,128)(2,1)} %collective-permute-done.15.refs_2_), channel_id=1, source_target_pairs={{0,1},{1,0},{2,3},{3,2},{4,5},{5,4},{6,7},{7,6},{8,9},{9,8},{10,11... | collective-permute-start | bytes 2359304 | tf_op jit(solution)/shard_map/ppermute | solution.py:49
  91.2 11.0 %collective-permute-start.21 = (bf16[96,4096]{1,0:T(8,128)(2,1)}, bf16[96,4096]{1,0:T(8,128)(2,1)}, u32[]{:S(2)}, u32[]{:S(2)}) collective-permute-start(bf16[96,4096]{1,0:T(8,128)(2,1)} %collective-permute-done.16.refs_3_), channel_id=1, source_target_pairs={{0,1},{1,0},{2,3},{3,2},{4,5},{5,4},{6,7},{7,6},{8,9},{9,8},{10,11... | collective-permute-start | bytes 2359304 | tf_op jit(solution)/shard_map/ppermute | solution.py:49
  135.2 13.6 %collective-permute-start.24 = (bf16[384,2048]{1,0:T(8,128)(2,1)}, bf16[384,2048]{1,0:T(8,128)(2,1)}, u32[]{:S(2)}, u32[]{:S(2)}) collective-permute-start(bf16[384,2048]{1,0:T(8,128)(2,1)} %get-tuple-element.36), channel_id=1, source_target_pairs={{0,1},{1,0},{2,3},{3,2},{4,5},{5,4},{6,7},{7,6},{8,9},{9,8},{10,11... | collective-permute-start | bytes 4718600 | tf_op jit(solution)/shard_map/ppermute | solution.py:49
  148.7 11.2 %collective-permute-start.32 = (bf16[384,2176]{1,0:T(8,128)(2,1)}, bf16[384,2176]{1,0:T(8,128)(2,1)S(1)}, u32[]{:S(2)}, u32[]{:S(2)}) collective-permute-start(bf16[384,2176]{1,0:T(8,128)(2,1)} %get-tuple-element.37), channel_id=1, source_target_pairs={{0,1},{1,0},{2,3},{3,2},{4,5},{5,4},{6,7},{7,6},{8,9},{9,8},{10,11... | collective-permute-start | bytes 5013512 | tf_op jit(solution)/shard_map/ppermute | solution.py:49
  150.9 11.4 %collective-permute-start.27 = (bf16[48,2048]{1,0:T(8,128)(2,1)S(1)}, bf16[48,2048]{1,0:T(8,128)(2,1)S(1)}, u32[]{:S(2)}, u32[]{:S(2)}) collective-permute-start(bf16[48,2048]{1,0:T(8,128)(2,1)S(1)} %get-tuple-element.57), channel_id=1, source_target_pairs={{0,2},{1,3},{2,0},{3,1},{4,6},{5,7},{6,4},{7,5},{8,10},{9,11},{10,... | collective-permute-start | bytes 589832 | tf_op jit(solution)/shard_map/ppermute | solution.py:49
  151.5 10.7 %collective-permute-start.25 = (bf16[48,2048]{1,0:T(8,128)(2,1)S(1)}, bf16[48,2048]{1,0:T(8,128)(2,1)S(1)}, u32[]{:S(2)}, u32[]{:S(2)}) collective-permute-start(bf16[48,2048]{1,0:T(8,128)(2,1)S(1)} %get-tuple-element.58), channel_id=1, source_target_pairs={{0,4},{1,5},{2,6},{3,7},{4,0},{5,1},{6,2},{7,3},{8,12},{9,13},{10,... | collective-permute-start | bytes 589832 | tf_op jit(solution)/shard_map/ppermute | solution.py:49
  160.4 11.0 %collective-permute-start.35 = (bf16[48,2176]{1,0:T(8,128)(2,1)S(1)}, bf16[48,2176]{1,0:T(8,128)(2,1)S(1)}, u32[]{:S(2)}, u32[]{:S(2)}) collective-permute-start(bf16[48,2176]{1,0:T(8,128)(2,1)S(1)} %get-tuple-element.51), channel_id=1, source_target_pairs={{0,2},{1,3},{2,0},{3,1},{4,6},{5,7},{6,4},{7,5},{8,10},{9,11},{10,... | collective-permute-start | bytes 626696 | tf_op jit(solution)/shard_map/ppermute | solution.py:49
  161.0 10.3 %collective-permute-start.33 = (bf16[48,2176]{1,0:T(8,128)(2,1)S(1)}, bf16[48,2176]{1,0:T(8,128)(2,1)S(1)}, u32[]{:S(2)}, u32[]{:S(2)}) collective-permute-start(bf16[48,2176]{1,0:T(8,128)(2,1)S(1)} %get-tuple-element.52), channel_id=1, source_target_pairs={{0,4},{1,5},{2,6},{3,7},{4,0},{5,1},{6,2},{7,3},{8,12},{9,13},{10,... | collective-permute-start | bytes 626696 | tf_op jit(solution)/shard_map/ppermute | solution.py:49
  162.4 15.1 %collective-permute-start.28 = (bf16[96,2048]{1,0:T(8,128)(2,1)S(1)}, bf16[96,2048]{1,0:T(8,128)(2,1)S(1)}, u32[]{:S(2)}, u32[]{:S(2)}) collective-permute-start(bf16[96,2048]{1,0:T(8,128)(2,1)S(1)} %pad_maximum_fusion.4), channel_id=1, source_target_pairs={{0,4},{1,5},{2,6},{3,7},{4,0},{5,1},{6,2},{7,3},{8,12},{9,13},{10,... | collective-permute-start | bytes 1179656 | tf_op jit(solution)/shard_map/ppermute | solution.py:49
  163.3 14.2 %collective-permute-start.26 = (bf16[96,2048]{1,0:T(8,128)(2,1)S(1)}, bf16[96,2048]{1,0:T(8,128)(2,1)S(1)}, u32[]{:S(2)}, u32[]{:S(2)}) collective-permute-start(bf16[96,2048]{1,0:T(8,128)(2,1)S(1)} %pad_maximum_fusion.3), channel_id=1, source_target_pairs={{0,2},{1,3},{2,0},{3,1},{4,6},{5,7},{6,4},{7,5},{8,10},{9,11},{10,... | collective-permute-start | bytes 1179656 | tf_op jit(solution)/shard_map/ppermute | solution.py:49
  171.5 13.6 %collective-permute-start.36 = (bf16[96,2176]{1,0:T(8,128)(2,1)S(1)}, bf16[96,2176]{1,0:T(8,128)(2,1)S(1)}, u32[]{:S(2)}, u32[]{:S(2)}) collective-permute-start(bf16[96,2176]{1,0:T(8,128)(2,1)S(1)} %pad_maximum_fusion.2), channel_id=1, source_target_pairs={{0,4},{1,5},{2,6},{3,7},{4,0},{5,1},{6,2},{7,3},{8,12},{9,13},{10,... | collective-permute-start | bytes 1253384 | tf_op jit(solution)/shard_map/ppermute | solution.py:49
  172.0 13.1 %collective-permute-start.34 = (bf16[96,2176]{1,0:T(8,128)(2,1)S(1)}, bf16[96,2176]{1,0:T(8,128)(2,1)S(1)}, u32[]{:S(2)}, u32[]{:S(2)}) collective-permute-start(bf16[96,2176]{1,0:T(8,128)(2,1)S(1)} %pad_maximum_fusion.1), channel_id=1, source_target_pairs={{0,2},{1,3},{2,0},{3,1},{4,6},{5,7},{6,4},{7,5},{8,10},{9,11},{10,... | collective-permute-start | bytes 1253384 | tf_op jit(solution)/shard_map/ppermute | solution.py:49
  177.7 10.2 %collective-permute-start.29 = (bf16[24,2048]{1,0:T(8,128)(2,1)S(1)}, bf16[24,2048]{1,0:T(8,128)(2,1)S(1)}, u32[]{:S(2)}, u32[]{:S(2)}) collective-permute-start(bf16[24,2048]{1,0:T(8,128)(2,1)S(1)} %get-tuple-element.64), channel_id=1, source_target_pairs={{0,8},{1,9},{2,10},{3,11},{4,12},{5,13},{6,14},{7,15},{8,0},{9,1},... | collective-permute-start | bytes 294920 | tf_op jit(solution)/shard_map/ppermute | solution.py:49
  177.9 10.9 %collective-permute-start.31 = (bf16[24,2048]{1,0:T(8,128)(2,1)S(1)}, bf16[24,2048]{1,0:T(8,128)(2,1)S(1)}, u32[]{:S(2)}, u32[]{:S(2)}) collective-permute-start(bf16[24,2048]{1,0:T(8,128)(2,1)S(1)} %get-tuple-element.65), channel_id=1, source_target_pairs={{0,24},{1,25},{2,26},{3,27},{4,28},{5,29},{6,30},{7,31},{8,16},{9,... | collective-permute-start | bytes 294920 | tf_op jit(solution)/shard_map/ppermute | solution.py:49
  187.9 9.0 %collective-permute-start.38 = (bf16[24,2176]{1,0:T(8,128)(2,1)S(1)}, bf16[24,2176]{1,0:T(8,128)(2,1)S(1)}, u32[]{:S(2)}, u32[]{:S(2)}) collective-permute-start(bf16[24,2176]{1,0:T(8,128)(2,1)S(1)} %get-tuple-element.63), channel_id=1, source_target_pairs={{0,16},{1,17},{2,18},{3,19},{4,20},{5,21},{6,22},{7,23},{8,24},{9,... | collective-permute-start | bytes 313352 | tf_op jit(solution)/shard_map/ppermute | solution.py:49
  (20 other events, 142.3 us)

commit v3 on v1

--- a/solution.py
+++ b/solution.py
@@ -58,16 +58,13 @@
 
 
 def gather_z(shard):
-    return jnp.concatenate([shard] + [flip(shard, Z * k) for k in range(1, depth())], axis=0)
-
-
-def gather_sides(first):
-    return flip(first, X), flip(first, Y)
-
-
-def gather_far(by_x, by_y):
-    half = by_x.shape[0] // 2
-    return [flip(by_y[:half], X), flip(by_x[half:], Y)]
+    blocks = [shard] + [flip(shard, Z * k) for k in range(1, depth())]
+    half = depth() // 2
+    return jnp.concatenate(blocks[:half], axis=0), blocks[half:]
+
+
+def join(blocks, *deps):
+    return jnp.concatenate(lax.optimization_barrier((*blocks, *deps))[: len(blocks)], axis=0)
 
 
 def gather_core(pieces):
@@ -81,19 +78,6 @@
 def quarters(mine):
     size = mine.shape[0] // 4
     return [mine[k * size : (k + 1) * size] for k in range(4)]
-
-
-def scatter_far(mine):
-    first, by_x, by_y, far = quarters(mine)
-    half = far.shape[0] // 2
-    to_y, to_x = flip(far[:half], X), flip(far[half:], Y)
-    by_y = jnp.concatenate([add(by_y[:half], to_y), by_y[half:]], axis=0)
-    by_x = jnp.concatenate([by_x[:half], add(by_x[half:], to_x)], axis=0)
-    return first, by_x, by_y
-
-
-def scatter_sides(first, by_x, by_y):
-    return add(first, flip(by_x, X), flip(by_y, Y))
 
 
 def scatter_z(first):
@@ -179,12 +163,14 @@
     )(slot.reshape(1, total), *pieces)
 
 
-def forward_kernel(x_ref, gate_ref, up_ref, hidden_ref, active_ref, pull_ref):
+def forward_kernel(x_ref, gate_ref, up_ref, hidden_ref, turned_ref, active_ref, pull_ref):
     gate_pre = dot(x_ref[...], gate_ref[...], ((1,), (0,)))
     up_pre = dot(x_ref[...], up_ref[...], ((1,), (0,)))
     sig = jax.nn.sigmoid(gate_pre)
     active = gate_pre * sig
-    hidden_ref[...] = (active * up_pre).astype(bf16)
+    hidden = active * up_pre
+    hidden_ref[...] = hidden.astype(bf16)
+    turned_ref[...] = hidden.T.astype(bf16)
     active_ref[...] = active.astype(bf16)
     pull_ref[...] = (up_pre * (sig * (1.0 + gate_pre * (1.0 - sig)))).astype(bf16)
 
@@ -196,6 +182,7 @@
     first = part * (units // block)
     weight = pl.BlockSpec((width, block), lambda i: (0, first + i))
     unit = pl.BlockSpec((rows, block), lambda i: (0, i))
+    turned = pl.BlockSpec((block, rows), lambda i: (i, 0))
     shape = jax.ShapeDtypeStruct((rows, units), bf16)
     return call(
         forward_kernel,
@@ -203,8 +190,8 @@
         4 * width * units,
         grid=(units // block,),
         in_specs=[whole(rows, width), weight, weight],
-        out_specs=[unit] * 3,
-        out_shape=[shape] * 3,
+        out_specs=[unit, turned, unit, unit],
+        out_shape=[shape, jax.ShapeDtypeStruct((units, rows), bf16), shape, shape],
     )(x, w_gate, w_up)
 
 
@@ -231,7 +218,7 @@
 def back_project(g, gain, w_down, parts):
     rows, width = g.shape
     units = w_down.shape[0]
-    block = tile(parts[0][0].shape[1], 256)
+    block = tile(parts[0][0].shape[1], 768)
     steps = units // block // len(parts)
     unit = pl.BlockSpec((rows, block), lambda i: (0, i))
 
@@ -263,10 +250,10 @@
             outs[0][...] = part
             return
         half = slot_ref.shape[0] // 2
-        width = part.shape[1]
+        rows, width = part.shape
         for k in range(2):
             slot = slot_ref[k * half : (k + 1) * half, :]
-            lanes = lax.broadcasted_iota(jnp.int32, (half, part.shape[0]), 1)
+            lanes = lax.broadcasted_iota(jnp.int32, (half, rows), 1)
             place = jnp.where(lanes == slot, 1.0, 0.0).astype(bf16)
             outs[k][:, :width] = dot(place, part, ((1,), (0,))).astype(bf16)
 
@@ -303,33 +290,34 @@
     )(d_gate, d_up, slot.reshape(total, 1), route, w_gate, w_up)
 
 
-def down_kernel(g_ref, gain_ref, hidden_ref, *refs):
-    out_ref, scaled = refs[-2:]
-
-    @pl.when(pl.program_id(0) == 0)
-    def _():
-        scaled[...] = (gain_ref[...] * g_ref[...].astype(f32)).astype(bf16)
-
-    out_ref[...] = dot(hidden_ref[...], scaled[...], ((0,), (0,))).astype(bf16)
-
-
-def down_grad(g, gain, hidden, low, mine, first, units, into):
+def down_kernel(count, g_ref, gain_ref, *refs):
+    turned, out_ref = refs[:count], refs[-1]
+    scaled = (gain_ref[...] * g_ref[...].astype(f32)).astype(bf16)
+    at = 0
+    for ref in turned:
+        out_ref[at : at + ref.shape[0], :] = dot(ref[...], scaled, ((1,), (0,))).astype(bf16)
+        at += ref.shape[0]
+
+
+def down_grad(turned, g, gain, chunk, chunks, into):
     rows, width = g.shape
-    block = tile(mine, 256)
-    start, source = first // block, low // block
+    units = sum(part.shape[0] for part in turned)
+    block = tile(width // chunks, 512)
+    steps = width // chunks // block
+    first = chunk * steps
     kept = [] if into is None else [into]
     return call(
-        down_kernel,
-        2 * rows * width * mine,
-        2 * width * mine,
-        grid=(mine // block,),
-        in_specs=[whole(rows, width), whole(rows, 1), pl.BlockSpec((rows, block), lambda i: (0, source + i))]
+        functools.partial(down_kernel, len(turned)),
+        2 * rows * width * units // chunks,
+        2 * width * units // chunks,
+        grid=(steps,),
+        in_specs=[pl.BlockSpec((rows, block), lambda i: (0, first + i)), whole(rows, 1)]
+        + [whole(*part.shape) for part in turned]
         + [pl.BlockSpec(memory_space=pl.ANY)] * len(kept),
-        out_specs=pl.BlockSpec((block, width), lambda i: (start + i, 0)),
+        out_specs=pl.BlockSpec((units, block), lambda i: (0, first + i)),
         out_shape=jax.ShapeDtypeStruct((units, width), bf16),
-        scratch_shapes=[pltpu.VMEM((rows, width), bf16)],
-        input_output_aliases={3: 0} if kept else {},
-    )(g, gain, hidden, *kept)
+        input_output_aliases={2 + len(turned): 0} if kept else {},
+    )(g, gain, *turned, *kept)
 
 
 def body(tokens, grad_out, expert_ids, route_weights, w_gate, w_up, w_down):
@@ -347,20 +335,24 @@
     meta = jnp.concatenate(
         [expert_ids.astype(bf16), route_weights, jnp.zeros((tok_count, pad), bf16)], axis=1
     )
-    first_t = gather_z(jnp.concatenate([tokens, meta], axis=1))
-    x_t, y_t = gather_sides(first_t)
-    first_g = gather_z(after(grad_out, first_t))
-    far_t = gather_far(x_t, y_t)
-    x_g, y_g = gather_sides(after(first_g, *far_t))
-    pieces_t = gather_core([first_t, x_t, y_t] + far_t)
+    t_a, t_b = gather_z(jnp.concatenate([tokens, meta], axis=1))
+    t_xa, t_ya = flip(t_a, X), flip(t_a, Y)
+    t_b = join(t_b, t_xa, t_ya)
+    g_a, g_b = gather_z(after(grad_out, t_b))
+    t_xb, t_yb = flip(t_b, X), flip(t_b, Y)
+    t_da, t_db = flip(t_ya, X), flip(t_xb, Y)
+    pieces_t = gather_core([t_a, t_b, t_xa, t_xb, t_ya, t_yb, t_da, t_db])
+    g_a = after(g_a, t_xb, t_yb)
+    g_xa, g_ya = flip(g_a, X), flip(g_a, Y)
+    g_b = join(g_b, t_da, t_db)
+    g_xb, g_yb = flip(g_b, X), flip(g_b, Y)
     all_meta = gather_meta(pieces_t, cols)
     all_ids = all_meta[:, :top_count].astype(jnp.int32)
     all_weights = all_meta[:, top_count : 2 * top_count].astype(f32)
     first = me * local_experts
     fused = narrow_count == 1 and local_experts == 1
     chunks = CHUNKS if fused else 1
-    units = w_gate.shape[2]
-    parts = 2 if units % (2 * LANES) == 0 else 1
+    parts = 2 if w_gate.shape[2] % (2 * LANES) == 0 else 1
     picked = []
     for j in range(local_experts):
         match = all_ids == first + j
@@ -372,59 +364,79 @@
         row_gain = jnp.sum(jnp.where(place, gain[None, :], 0.0), axis=1, keepdims=True)
         x = pick_rows(slot, pieces_t, rows, cols)
         x = lax.all_gather(x, "narrow", axis=1, tiled=True)
-        ahead = [forward(x, w_gate[j], w_up[j], 0, parts)]
-        picked.append((slot, place, row_gain, x, ahead))
-    x_g, y_g, *_ = lax.optimization_barrier((x_g, y_g, *[ahead[0][0] for *_, ahead in picked]))
-    far_g = gather_far(x_g, y_g)
+        picked.append([slot, place, row_gain, x])
+    g_xa, g_ya, *_ = lax.optimization_barrier((g_xa, g_ya, *[entry[3] for entry in picked]))
+    g_da = flip(g_ya, X)
     for j in range(local_experts):
-        slot, place, row_gain, x, ahead = picked[j]
+        x = after(picked[j][3], g_xa, g_ya)
+        picked[j] += [x, [forward(x, w_gate[j], w_up[j], 0, parts)]]
+    g_xb, g_yb, *_ = lax.optimization_barrier((g_xb, g_yb, *[entry[5][0][0] for entry in picked]))
+    g_db = flip(g_xb, Y)
+    for j in range(local_experts):
         if parts == 2:
-            ahead.append(forward(after(x, x_g, y_g), w_gate[j], w_up[j], 1, parts))
-    far_g = lax.optimization_barrier((*far_g, *[ahead[-1][0] for *_, ahead in picked]))[: len(far_g)]
-    pieces_g = gather_core([first_g, x_g, y_g, *far_g])
+            x = after(picked[j][4], g_xb, g_yb)
+            picked[j][5].append(forward(x, w_gate[j], w_up[j], 1, parts))
+    g_da, g_db, *_ = lax.optimization_barrier((g_da, g_db, *[entry[5][-1][0] for entry in picked]))
+    pieces_g = gather_core([g_a, g_b, g_xa, g_xb, g_ya, g_yb, g_da, g_db])
     expert_cols = experts_all + -experts_all % LANES
     dense = [0, 0]
-    route_all = 0
     ends = []
     for j in range(local_experts):
-        slot, place, row_gain, x, ahead = picked[j]
+        slot, place, row_gain, _, _, ahead = picked[j]
         g = pick_rows(slot, pieces_g, rows, cols)
         g = lax.all_gather(g, "narrow", axis=1, tiled=True)
-        d_gate, d_up, route = back_project(g, row_gain, w_down[j], ahead)
+        straight = [(hidden, active, pull) for hidden, _, active, pull in ahead]
+        d_gate, d_up, route = back_project(g, row_gain, w_down[j], straight)
         route = lax.psum(route.astype(bf16).astype(f32), "narrow")
         at = jnp.arange(expert_cols, dtype=jnp.int32) == first + j
         route = jnp.where(at[None, :], route, 0.0).astype(bf16)
-        ends.append((g, row_gain, [part[0] for part in ahead]))
+        ends.append(([part[1] for part in ahead], g, row_gain))
         if fused:
-            own, other = token_grad(d_gate, d_up, slot, route, w_gate[j], w_up[j], 0, chunks, True)
-            dense = [own, other]
+            dense = token_grad(d_gate, d_up, slot, route, w_gate[j], w_up[j], 0, chunks, True)
             continue
         (part,) = token_grad(d_gate, d_up, slot, route, w_gate[j], w_up[j], 0, 1, False)
         part = lax.psum_scatter(part, "narrow", scatter_dimension=1, tiled=True)
         part = jnp.concatenate([part, route], axis=1)
         part = dot(place.astype(bf16), part, ((0,), (0,)))
         dense = [dense[0] + part[: total // 2], dense[1] + part[total // 2 :]]
-    mine = [add(dense[0].astype(bf16), flip(dense[1].astype(bf16), CORE))]
+
+    def send_far(mine):
+        near, by_x, by_y, far = quarters(mine)
+        half = far.shape[0] // 2
+        return [near, by_x, by_y, flip(far[:half], X), flip(far[half:], Y)]
+
+    def add_far(near, by_x, by_y, to_y, to_x):
+        half = to_y.shape[0]
+        by_y = jnp.concatenate([add(by_y[:half], to_y), by_y[half:]], axis=0)
+        by_x = jnp.concatenate([by_x[:half], add(by_x[half:], to_x)], axis=0)
+        return near, by_x, by_y
+
+    def send_sides(near, by_x, by_y):
+        return near, flip(by_x, X), flip(by_y, Y)
+
+    mine = add(dense[0].astype(bf16), flip(dense[1].astype(bf16), CORE))
+    sent = send_far(mine)
     if fused and chunks == 2:
-        own, other = token_grad(after(d_gate, dense[0]), d_up, slot, route, w_gate[0], w_up[0], 1, chunks, True)
-        mine[0] = add(after(dense[0], own), flip(dense[1], CORE))
-        mine.append(add(own, flip(other, CORE)))
-    sides = [scatter_far(rows_) for rows_ in mine]
-    firsts = [scatter_sides(*side) for side in sides]
-    shares = [scatter_z(first_) for first_ in firsts]
-    gates = iter([mine[0], sides[0][1], firsts[0], firsts[-1]])
-    grad_downs = []
-    for g, row_gain, hidden in ends:
-        out, first_unit = None, 0
-        for piece in hidden:
-            count = piece.shape[1]
-            cut = 2 * LANES * (count // (4 * LANES)) if len(hidden) > 1 and count % (2 * LANES) == 0 else 0
-            for low, high in ((0, cut), (cut, count)):
-                if high > low:
-                    ready = after(piece, next(gates)) if local_experts == 1 else piece
-                    out = down_grad(g, row_gain, ready, low, high - low, first_unit + low, units, out)
-            first_unit += count
-        grad_downs.append(out)
+        (turned, g, row_gain), = ends
+        own, other = token_grad(after(d_gate, mine), d_up, slot, route, w_gate[0], w_up[0], 1, chunks, True)
+        *_, to_y, to_x = sent
+        to_y, to_x, own, other = lax.optimization_barrier((to_y, to_x, own, other))
+        near, by_x, by_y = send_sides(*add_far(*sent[:3], to_y, to_x))
+        mine = add(own, flip(other, CORE))
+        sent = send_far(mine)
+        out = down_grad(turned, after(g, mine), row_gain, 0, 2, None)
+        *_, to_y, to_x = sent
+        by_x, by_y, to_y, to_x, out = lax.optimization_barrier((by_x, by_y, to_y, to_x, out))
+        first_near = add(near, by_x, by_y)
+        sides = add_far(*sent[:3], to_y, to_x)
+        near, by_x, by_y = send_sides(*sides)
+        out = down_grad(turned, after(g, *sides, first_near), row_gain, 1, 2, out)
+        by_x, by_y, out = lax.optimization_barrier((by_x, by_y, out))
+        shares = [scatter_z(first_near), scatter_z(add(near, by_x, by_y))]
+        grad_downs = [out]
+    else:
+        shares = [scatter_z(add(*send_sides(*add_far(*sent))))]
+        grad_downs = [down_grad(*end, 0, 1, None) for end in ends]
     joined = jnp.concatenate(shares, axis=1)
     width = tokens.shape[1]
     by_expert = joined[:, width : width + experts_all].astype(f32)

time: 196 us -> 199 us (1.015)
  starting transfers between devices: 37.9 us -> 50.2 us
  Pallas kernels: 91 us -> 84.8 us
  local copies, waits for them, and re-layouts: 12.2 us -> 9.03 us
    ppermute x40 -> x50, starting transfers between devices: 37.9 us -> 50.2 us  [flip(): return lax.ppermute(value, 'wide', [(i, i ^ mask) for i in range(count)])]
    pallas_call x4 -> x2, Pallas kernels: 21.9 us -> 13.5 us  [down_grad(): call(functools.partial(down_kernel, len(turned)), 2 * rows * width * unit...]
    slice x7 -> x3, local copies, waits for them, and re-layouts: 2.31 us -> 0.2 us  [the longest x2 0.12 us: add_far(): by_y = jnp.concatenate([add(by_y[:half], to_y), by_y[half:]], axis=0)]
    ppermute x40 -> x50, waiting for transfers between devices: 46.2 us -> 44.4 us  [flip(): return lax.ppermute(value, 'wide', [(i, i ^ mask) for i in range(count)])]
    unnamed x37 -> x56, local copies, waits for them, and re-layouts: 7.85 us -> 7.41 us
  transfers between devices with their start and end apart: 40 -> 50, of which waited for: 14 -> 14; matrix products, arithmetic and copies ran while one was open for 5% -> 3% of each run, Pallas kernels for 31% -> 27%
where the time goes in v3:
time: 199 us; the launch traced here: 198 us
  Pallas kernels  84.8 us (43%)
  starting transfers between devices  50.2 us (25%)
  waiting for transfers between devices  44.4 us (22%)
  local copies, waits for them, and re-layouts  9.03 us (5%)
  other arithmetic  8.82 us (4%)
    ppermute x50, starting transfers between devices, flip(): return lax.ppermute(value, 'wide', [(i, i ^ mask) for i in range(count)])  50.2 us
    ppermute x50, waiting for transfers between devices, flip(): return lax.ppermute(value, 'wide', [(i, i ^ mask) for i in range(count)])  44.4 us
    pallas_call x2, Pallas kernels, token_grad(): call(functools.partial(token_kernel, steps, spread), 4 * rows * width * u...  22.6 us
    pallas_call x2, Pallas kernels, forward(): call(forward_kernel, 4 * rows * width * units, 4 * width * units, grid=(u...  20.2 us
    pallas_call x2, Pallas kernels, pick_rows(): call(functools.partial(pick_kernel, sizes, block), 2 * rows * total * col...  15.6 us
    pallas_call x2, Pallas kernels, down_grad(): call(functools.partial(down_kernel, len(turned)), 2 * rows * width * unit...  13.5 us
    pallas_call x1, Pallas kernels, back_project(): call(functools.partial(back_kernel, steps), 2 * rows * width * units, 2 *...  11.9 us
    unnamed x56, local copies, waits for them, and re-layouts  7.41 us
  transfers between devices with their start and end apart: 50, of which 14 were waited for; matrix products, arithmetic and copies ran while one was open for 3% of the time, Pallas kernels for 27%

profile of v3, /device:TPU:0, one launch (start us, length us, event | category | flops | bytes accessed | tf_op | source)
XLA Modules:
  0.0 198.3 jit_solution(6563757451287523482)
XLA Ops:
  3.2 3.1 %collective-permute-start = (bf16[24,4224]{1,0:T(8,128)(2,1)S(1)}, bf16[24,4224]{1,0:T(8,128)(2,1)S(1)}, u32[]{:S(2)}, u32[]{:S(2)}) collective-permute-start(bf16[24,4224]{1,0:T(8,128)(2,1)S(1)} %concatenate.30), channel_id=1, source_target_pairs={{0,8},{1,9},{2,10},{3,11},{4,12},{5,13},{6,14},{7,15},{8,0},{9,1},... | collective-permute-start | bytes 608264 | tf_op jit(solution)/shard_map/ppermute | solution.py:49
  6.3 5.0 %collective-permute-done = bf16[24,4224]{1,0:T(8,128)(2,1)S(1)} collective-permute-done((bf16[24,4224]{1,0:T(8,128)(2,1)S(1)}, bf16[24,4224]{1,0:T(8,128)(2,1)S(1)}, u32[]{:S(2)}, u32[]{:S(2)}) %collective-permute-start) | collective-permute-done | bytes 202784 | tf_op jit(solution)/shard_map/ppermute | solution.py:49
  11.4 1.7 collective-permute-start.4
  13.1 1.5 collective-permute-start.3
  14.6 2.6 %collective-permute-start.1 = (bf16[24,4224]{1,0:T(8,128)(2,1)S(1)}, bf16[24,4224]{1,0:T(8,128)(2,1)S(1)}, u32[]{:S(2)}, u32[]{:S(2)}) collective-permute-start(bf16[24,4224]{1,0:T(8,128)(2,1)S(1)} %concatenate.30), channel_id=1, source_target_pairs={{0,16},{1,17},{2,18},{3,19},{4,20},{5,21},{6,22},{7,23},{8,24},{9,... | collective-permute-start | bytes 608264 | tf_op jit(solution)/shard_map/ppermute | solution.py:49
  18.6 12.2 %collective-permute-done.1 = bf16[24,4224]{1,0:T(8,128)(2,1)S(1)} collective-permute-done((bf16[24,4224]{1,0:T(8,128)(2,1)S(1)}, bf16[24,4224]{1,0:T(8,128)(2,1)S(1)}, u32[]{:S(2)}, u32[]{:S(2)}) %collective-permute-start.1) | collective-permute-done | bytes 202784 | tf_op jit(solution)/shard_map/ppermute | solution.py:49
  31.4 3.8 %collective-permute-start.17 = (bf16[24,4096]{1,0:T(8,128)(2,1)S(1)}, bf16[24,4096]{1,0:T(8,128)(2,1)S(1)}, u32[]{:S(2)}, u32[]{:S(2)}) collective-permute-start(bf16[24,4096]{1,0:T(8,128)(2,1)S(1)} %copy-done.23), channel_id=1, source_target_pairs={{0,8},{1,9},{2,10},{3,11},{4,12},{5,13},{6,14},{7,15},{8,0},{9,1},... | collective-permute-start | bytes 589832 | tf_op jit(solution)/shard_map/ppermute | solution.py:49
  35.8 1.9 collective-permute-start.18
  37.7 1.4 collective-permute-start.19
  39.1 4.1 %collective-permute-done.17 = bf16[24,4096]{1,0:T(8,128)(2,1)S(1)} collective-permute-done((bf16[24,4096]{1,0:T(8,128)(2,1)S(1)}, bf16[24,4096]{1,0:T(8,128)(2,1)S(1)}, u32[]{:S(2)}, u32[]{:S(2)}) %collective-permute-start.17) | collective-permute-done | bytes 196640 | tf_op jit(solution)/shard_map/ppermute | solution.py:49
  43.3 1.5 collective-permute-start.7
  46.0 7.0 %collective-permute-done.18 = bf16[24,4096]{1,0:T(8,128)(2,1)S(1)} collective-permute-done((bf16[24,4096]{1,0:T(8,128)(2,1)S(1)}, bf16[24,4096]{1,0:T(8,128)(2,1)S(1)}, u32[]{:S(2)}, u32[]{:S(2)}) %collective-permute-start.18) | collective-permute-done | bytes 196640 | tf_op jit(solution)/shard_map/ppermute | solution.py:49
  55.9 1.5 collective-permute-start.20
  57.4 1.4 collective-permute-start.21
  63.5 7.7 %shard_map.95.x_ref = bf16[384,4096]{1,0:T(8,128)(2,1)} custom-call(s32[1,768]{1,0:T(1,128)S(1)} %get-tuple-element.97.slot_ref, bf16[48,4224]{1,0:T(8,128)(2,1)S(1)} %pad_maximum_fusion.2.refs_0_, bf16[48,4224]{1,0:T(8,128)(2,1)S(1)} %constant_dynamic-update-slice_fusion.refs_1_, bf16[48,4224]{1,0:T(8,128)(2,1)S(1)} %collective-permute-done.3.refs_2_, ...), custom_call_target="tpu_custom_call" | custom-call | flops 2415919104 | bytes 9437184 | tf_op jit(solution)/shard_map/pallas_call | solution.py:150
  72.5 10.1 %shard_map.96 = (bf16[384,768]{1,0:T(8,128)(2,1)S(1)}, bf16[768,384]{1,0:T(8,128)(2,1)S(1)}, bf16[384,768]{1,0:T(8,128)(2,1)S(1)}, bf16[384,768]{1,0:T(8,128)(2,1)}) custom-call(bf16[384,4096]{1,0:T(8,128)(2,1)} %shard_map.95.x_ref, bf16[4096,1536]{1,0:T(8,128)(2,1)} %bitcast.19, bf16[4096,1536]{1,0:T(8,128)(2,1)} %bitcast.23), custom_call_target="tpu_custom_call" | custom-call | flops 4831838208 | bytes 12582912 | tf_op jit(solution)/shard_map/pallas_call | solution.py:187
  85.7 10.1 %shard_map.97 = (bf16[384,768]{1,0:T(8,128)(2,1)S(1)}, bf16[768,384]{1,0:T(8,128)(2,1)S(1)}, bf16[384,768]{1,0:T(8,128)(2,1)S(1)}, bf16[384,768]{1,0:T(8,128)(2,1)}) custom-call(bf16[384,4096]{1,0:T(8,128)(2,1)} %shard_map.95.x_ref, bf16[4096,1536]{1,0:T(8,128)(2,1)} %bitcast.20, bf16[4096,1536]{1,0:T(8,128)(2,1)} %bitcast.24), custom_call_target="tpu_custom_call" | custom-call | flops 4831838208 | bytes 12582912 | tf_op jit(solution)/shard_map/pallas_call | solution.py:187
  101.8 7.9 %shard_map.98.g_ref = bf16[384,4096]{1,0:T(8,128)(2,1)} custom-call(s32[1,768]{1,0:T(1,128)S(1)} %get-tuple-element.97.slot_ref, bf16[48,4096]{1,0:T(8,128)(2,1)S(1)} %pad_maximum_fusion.3.refs_0_, bf16[48,4096]{1,0:T(8,128)(2,1)S(1)} %constant_dynamic-update-slice_fusion.2.refs_1_, bf16[48,4096]{1,0:T(8,128)(2,1)S(1)} %collective-permute-done.20.refs_2_, ...), custom_call_target="tpu_custom_call" | custom-call | flops 2415919104 | bytes 9437184 | tf_op jit(solution)/shard_map/pallas_call | solution.py:150
  109.8 11.9 %shard_map.99 = (bf16[384,1536]{1,0:T(8,128)(2,1)}, bf16[384,1536]{1,0:T(8,128)(2,1)}, f32[384,1]{1,0:T(8,128)S(1)}) custom-call(bf16[384,4096]{1,0:T(8,128)(2,1)} %shard_map.98.g_ref, f32[384,1]{1,0:T(8,128)S(1)} %broadcast_in_dim.81.gain_ref, bf16[1536,4096]{1,0:T(8,128)(2,1)} %bitcast.28, bf16[384,768]{1,0:T(8,128)(2,1)S(1)} %copy-done.4, ...), custom_call_target="tpu_custom_call" | custom-call | flops 4831838208 | bytes 12582912 | tf_op jit(solution)/shard_map/pallas_call | solution.py:229
  123.2 11.2 %shard_map.100 = (bf16[384,2048]{1,0:T(8,128)(2,1)}, bf16[384,2048]{1,0:T(8,128)(2,1)}) custom-call(bf16[384,1536]{1,0:T(8,128)(2,1)S(1)} %copy-done, bf16[384,1536]{1,0:T(8,128)(2,1)} %get-tuple-element.68.d_up_ref, s32[768,1]{1,0:T(8,128)S(1)} %bitcast_select_fusion.slot_ref, bf16[384,128]{1,0:T(8,128)(2,1)S(1)} %select_convert_fusion.route_ref, ...), custom_call_target="tpu_custom_call" | custom-call | flops 6039797760 | bytes 15728640 | tf_op jit(solution)/shard_map/pallas_call | solution.py:282
  134.8 3.2 %collective-permute-done.34 = bf16[384,2048]{1,0:T(8,128)(2,1)S(1)} collective-permute-done((bf16[384,2048]{1,0:T(8,128)(2,1)}, bf16[384,2048]{1,0:T(8,128)(2,1)S(1)}, u32[]{:S(2)}, u32[]{:S(2)}) %collective-permute-start.34) | collective-permute-done | bytes 1572896 | tf_op jit(solution)/shard_map/ppermute | solution.py:49
  138.0 2.0 %add_convert_fusion.1 = bf16[384,2048]{1,0:T(8,128)(2,1)S(1)} fusion(bf16[384,2048]{1,0:T(8,128)(2,1)S(1)} %collective-permute-done.34, bf16[384,2048]{1,0:T(8,128)(2,1)} %get-tuple-element.70), kind=kLoop, calls=%fused_computation.1 | loop fusion | flops 3145728 | bytes 4718592 | tf_op jit(solution)/shard_map/convert_element_type | solution.py:23
  141.8 11.4 %shard_map.101 = (bf16[384,2176]{1,0:T(8,128)(2,1)}, bf16[384,2176]{1,0:T(8,128)(2,1)}) custom-call(bf16[384,1536]{1,0:T(8,128)(2,1)S(1)} %copy-done, bf16[384,1536]{1,0:T(8,128)(2,1)} %get-tuple-element.68.d_up_ref, s32[768,1]{1,0:T(8,128)S(1)} %bitcast_select_fusion.slot_ref, bf16[384,128]{1,0:T(8,128)(2,1)S(1)} %select_convert_fusion.route_ref, ...), custom_call_target="tpu_custom_call" | custom-call | flops 6039797760 | bytes 15728640 | tf_op jit(solution)/shard_map/pallas_call | solution.py:282
  155.7 1.5 collective-permute-start.37
  157.2 1.8 add_convert_fusion
  161.6 6.7 %shard_map.102.refs_2_ = bf16[1536,4096]{1,0:T(8,128)(2,1)} custom-call(bf16[384,4096]{1,0:T(8,128)(2,1)} %shard_map.98.g_ref, f32[384,1]{1,0:T(8,128)S(1)} %broadcast_in_dim.81.gain_ref, bf16[768,384]{1,0:T(8,128)(2,1)S(1)} %get-tuple-element.80.refs_0_, bf16[768,384]{1,0:T(8,128)(2,1)S(1)} %get-tuple-element.81.refs_1_), custom_call_target="tpu_custom_call" | custom-call | flops 2415919104 | bytes 6291456 | tf_op jit(solution)/shard_map/pallas_call | solution.py:309
  168.3 3.1 %collective-permute-done.40 = bf16[48,2176]{1,0:T(8,128)(2,1)S(1)} collective-permute-done((bf16[48,2176]{1,0:T(8,128)(2,1)S(1)}, bf16[48,2176]{1,0:T(8,128)(2,1)S(1)}, u32[]{:S(2)}, u32[]{:S(2)}) %collective-permute-start.40) | collective-permute-done | bytes 208928 | tf_op jit(solution)/shard_map/ppermute | solution.py:49
  174.2 2.5 %collective-permute-start.42 = (bf16[24,2048]{1,0:T(8,128)(2,1)S(1)}, bf16[24,2048]{1,0:T(8,128)(2,1)S(1)}, u32[]{:S(2)}, u32[]{:S(2)}) collective-permute-start(bf16[24,2048]{1,0:T(8,128)(2,1)S(1)} %get-tuple-element.114), channel_id=1, source_target_pairs={{0,8},{1,9},{2,10},{3,11},{4,12},{5,13},{6,14},{7,15},{8,0},{9,1},... | collective-permute-start | bytes 294920 | tf_op jit(solution)/shard_map/ppermute | solution.py:49
  176.6 1.9 collective-permute-start.43
  179.9 6.7 %shard_map.103 = bf16[1536,4096]{1,0:T(8,128)(2,1)} custom-call(bf16[384,4096]{1,0:T(8,128)(2,1)} %shard_map.98.g_ref, f32[384,1]{1,0:T(8,128)S(1)} %broadcast_in_dim.81.gain_ref, bf16[768,384]{1,0:T(8,128)(2,1)S(1)} %get-tuple-element.80.refs_0_, bf16[768,384]{1,0:T(8,128)(2,1)S(1)} %get-tuple-element.81.refs_1_, ...), custom_call_target="tpu_custom_call", output_to_operand_aliasing={{}: (4, {})} | custom-call | flops 2415919104 | bytes 6291456 | tf_op jit(solution)/shard_map/pallas_call | solution.py:309
  187.4 2.4 %collective-permute-start.48 = (bf16[24,2176]{1,0:T(8,128)(2,1)S(1)}, bf16[24,2176]{1,0:T(8,128)(2,1)S(1)}, u32[]{:S(2)}, u32[]{:S(2)}) collective-permute-start(bf16[24,2176]{1,0:T(8,128)(2,1)S(1)} %get-tuple-element.113), channel_id=1, source_target_pairs={{0,16},{1,17},{2,18},{3,19},{4,20},{5,21},{6,22},{7,23},{8,24},{9,... | collective-permute-start | bytes 313352 | tf_op jit(solution)/shard_map/ppermute | solution.py:49
  191.6 5.2 %collective-permute-done.48 = bf16[24,2176]{1,0:T(8,128)(2,1)S(1)} collective-permute-done((bf16[24,2176]{1,0:T(8,128)(2,1)S(1)}, bf16[24,2176]{1,0:T(8,128)(2,1)S(1)}, u32[]{:S(2)}, u32[]{:S(2)}) %collective-permute-start.48) | collective-permute-done | bytes 104480 | tf_op jit(solution)/shard_map/ppermute | solution.py:49
  (177 shorter events, 41.0 us)
Async XLA Ops:
  11.4 19.4 %collective-permute-start.4 = (bf16[48,4224]{1,0:T(8,128)(2,1)S(1)}, bf16[48,4224]{1,0:T(8,128)(2,1)S(1)}, u32[]{:S(2)}, u32[]{:S(2)}) collective-permute-start(bf16[48,4224]{1,0:T(8,128)(2,1)S(1)} %pad_maximum_fusion.2.refs_0_), channel_id=1, source_target_pairs={{0,4},{1,5},{2,6},{3,7},{4,0},{5,1},{6,2},{7,3},{8,12},{9,13},{10,... | collective-permute-start | bytes 1216520 | tf_op jit(solution)/shard_map/ppermute | solution.py:49
  13.1 17.6 %collective-permute-start.3 = (bf16[48,4224]{1,0:T(8,128)(2,1)S(1)}, bf16[48,4224]{1,0:T(8,128)(2,1)S(1)}, u32[]{:S(2)}, u32[]{:S(2)}) collective-permute-start(bf16[48,4224]{1,0:T(8,128)(2,1)S(1)} %pad_maximum_fusion.2.refs_0_), channel_id=1, source_target_pairs={{0,2},{1,3},{2,0},{3,1},{4,6},{5,7},{6,4},{7,5},{8,10},{9,11},{10,... | collective-permute-start | bytes 1216520 | tf_op jit(solution)/shard_map/ppermute | solution.py:49
  14.6 16.1 %collective-permute-start.1 = (bf16[24,4224]{1,0:T(8,128)(2,1)S(1)}, bf16[24,4224]{1,0:T(8,128)(2,1)S(1)}, u32[]{:S(2)}, u32[]{:S(2)}) collective-permute-start(bf16[24,4224]{1,0:T(8,128)(2,1)S(1)} %concatenate.30), channel_id=1, source_target_pairs={{0,16},{1,17},{2,18},{3,19},{4,20},{5,21},{6,22},{7,23},{8,24},{9,... | collective-permute-start | bytes 608264 | tf_op jit(solution)/shard_map/ppermute | solution.py:49
  17.2 13.5 %collective-permute-start.2 = (bf16[24,4224]{1,0:T(8,128)(2,1)S(1)}, bf16[24,4224]{1,0:T(8,128)(2,1)S(1)}, u32[]{:S(2)}, u32[]{:S(2)}) collective-permute-start(bf16[24,4224]{1,0:T(8,128)(2,1)S(1)} %concatenate.30), channel_id=1, source_target_pairs={{0,24},{1,25},{2,26},{3,27},{4,28},{5,29},{6,30},{7,31},{8,16},{9,... | collective-permute-start | bytes 608264 | tf_op jit(solution)/shard_map/ppermute | solution.py:49
  30.8 14.0 %collective-permute-start.5 = (bf16[48,4224]{1,0:T(8,128)(2,1)S(1)}, bf16[48,4224]{1,0:T(8,128)(2,1)S(1)}, u32[]{:S(2)}, u32[]{:S(2)}) collective-permute-start(bf16[48,4224]{1,0:T(8,128)(2,1)S(1)} %constant_dynamic-update-slice_fusion.refs_1_), channel_id=1, source_target_pairs={{0,2},{1,3},{2,0},{3,1},{4,6},{5,7},{6,4},{7,5},{8,10},{9,11},{10,... | collective-permute-start | bytes 1216520 | tf_op jit(solution)/shard_map/ppermute | solution.py:49
  31.4 11.9 %collective-permute-start.17 = (bf16[24,4096]{1,0:T(8,128)(2,1)S(1)}, bf16[24,4096]{1,0:T(8,128)(2,1)S(1)}, u32[]{:S(2)}, u32[]{:S(2)}) collective-permute-start(bf16[24,4096]{1,0:T(8,128)(2,1)S(1)} %copy-done.23), channel_id=1, source_target_pairs={{0,8},{1,9},{2,10},{3,11},{4,12},{5,13},{6,14},{7,15},{8,0},{9,1},... | collective-permute-start | bytes 589832 | tf_op jit(solution)/shard_map/ppermute | solution.py:49
  35.2 10.7 %collective-permute-start.6 = (bf16[48,4224]{1,0:T(8,128)(2,1)S(1)}, bf16[48,4224]{1,0:T(8,128)(2,1)S(1)}, u32[]{:S(2)}, u32[]{:S(2)}) collective-permute-start(bf16[48,4224]{1,0:T(8,128)(2,1)S(1)} %constant_dynamic-update-slice_fusion.refs_1_), channel_id=1, source_target_pairs={{0,4},{1,5},{2,6},{3,7},{4,0},{5,1},{6,2},{7,3},{8,12},{9,13},{10,... | collective-permute-start | bytes 1216520 | tf_op jit(solution)/shard_map/ppermute | solution.py:49
  35.8 17.2 %collective-permute-start.18 = (bf16[24,4096]{1,0:T(8,128)(2,1)S(1)}, bf16[24,4096]{1,0:T(8,128)(2,1)S(1)}, u32[]{:S(2)}, u32[]{:S(2)}) collective-permute-start(bf16[24,4096]{1,0:T(8,128)(2,1)S(1)} %copy-done.23), channel_id=1, source_target_pairs={{0,16},{1,17},{2,18},{3,19},{4,20},{5,21},{6,22},{7,23},{8,24},{9,... | collective-permute-start | bytes 589832 | tf_op jit(solution)/shard_map/ppermute | solution.py:49
  37.7 15.2 %collective-permute-start.19 = (bf16[24,4096]{1,0:T(8,128)(2,1)S(1)}, bf16[24,4096]{1,0:T(8,128)(2,1)S(1)}, u32[]{:S(2)}, u32[]{:S(2)}) collective-permute-start(bf16[24,4096]{1,0:T(8,128)(2,1)S(1)} %copy-done.23), channel_id=1, source_target_pairs={{0,24},{1,25},{2,26},{3,27},{4,28},{5,29},{6,30},{7,31},{8,16},{9,... | collective-permute-start | bytes 589832 | tf_op jit(solution)/shard_map/ppermute | solution.py:49
  43.3 10.2 %collective-permute-start.7 = (bf16[48,4224]{1,0:T(8,128)(2,1)S(1)}, bf16[48,4224]{1,0:T(8,128)(2,1)S(1)}, u32[]{:S(2)}, u32[]{:S(2)}) collective-permute-start(bf16[48,4224]{1,0:T(8,128)(2,1)S(1)} %collective-permute-done.4.refs_4_), channel_id=1, source_target_pairs={{0,2},{1,3},{2,0},{3,1},{4,6},{5,7},{6,4},{7,5},{8,10},{9,11},{10,... | collective-permute-start | bytes 1216520 | tf_op jit(solution)/shard_map/ppermute | solution.py:49
  44.8 9.9 %collective-permute-start.8 = (bf16[48,4224]{1,0:T(8,128)(2,1)S(1)}, bf16[48,4224]{1,0:T(8,128)(2,1)S(1)}, u32[]{:S(2)}, u32[]{:S(2)}) collective-permute-start(bf16[48,4224]{1,0:T(8,128)(2,1)S(1)} %collective-permute-done.5.refs_3_), channel_id=1, source_target_pairs={{0,4},{1,5},{2,6},{3,7},{4,0},{5,1},{6,2},{7,3},{8,12},{9,13},{10,... | collective-permute-start | bytes 1216520 | tf_op jit(solution)/shard_map/ppermute | solution.py:49
  55.9 15.4 %collective-permute-start.20 = (bf16[48,4096]{1,0:T(8,128)(2,1)S(1)}, bf16[48,4096]{1,0:T(8,128)(2,1)S(1)}, u32[]{:S(2)}, u32[]{:S(2)}) collective-permute-start(bf16[48,4096]{1,0:T(8,128)(2,1)S(1)} %pad_maximum_fusion.3.refs_0_), channel_id=1, source_target_pairs={{0,2},{1,3},{2,0},{3,1},{4,6},{5,7},{6,4},{7,5},{8,10},{9,11},{10,... | collective-permute-start | bytes 1179656 | tf_op jit(solution)/shard_map/ppermute | solution.py:49
  57.4 13.9 %collective-permute-start.21 = (bf16[48,4096]{1,0:T(8,128)(2,1)S(1)}, bf16[48,4096]{1,0:T(8,128)(2,1)}, u32[]{:S(2)}, u32[]{:S(2)}) collective-permute-start(bf16[48,4096]{1,0:T(8,128)(2,1)S(1)} %pad_maximum_fusion.3.refs_0_), channel_id=1, source_target_pairs={{0,4},{1,5},{2,6},{3,7},{4,0},{5,1},{6,2},{7,3},{8,12},{9,13},{10,... | collective-permute-start | bytes 1179656 | tf_op jit(solution)/shard_map/ppermute | solution.py:49
  58.8 39.1 %collective-permute-start.26 = (bf16[48,4096]{1,0:T(8,128)(2,1)S(1)}, bf16[48,4096]{1,0:T(8,128)(2,1)}, u32[]{:S(2)}, u32[]{:S(2)}) collective-permute-start(bf16[48,4096]{1,0:T(8,128)(2,1)S(1)} %pad_maximum_fusion.3.refs_0_), channel_id=1, source_target_pairs={{0,1},{1,0},{2,3},{3,2},{4,5},{5,4},{6,7},{7,6},{8,9},{9,8},{10,11... | collective-permute-start | bytes 1179656 | tf_op jit(solution)/shard_map/ppermute | solution.py:49
  58.9 25.5 %collective-permute-start.22 = (bf16[48,4096]{1,0:T(8,128)(2,1)S(1)}, bf16[48,4096]{1,0:T(8,128)(2,1)}, u32[]{:S(2)}, u32[]{:S(2)}) collective-permute-start(bf16[48,4096]{1,0:T(8,128)(2,1)S(1)} %constant_dynamic-update-slice_fusion.2.refs_1_), channel_id=1, source_target_pairs={{0,2},{1,3},{2,0},{3,1},{4,6},{5,7},{6,4},{7,5},{8,10},{9,11},{10,... | collective-permute-start | bytes 1179656 | tf_op jit(solution)/shard_map/ppermute | solution.py:49
  59.5 24.9 %collective-permute-start.23 = (bf16[48,4096]{1,0:T(8,128)(2,1)S(1)}, bf16[48,4096]{1,0:T(8,128)(2,1)}, u32[]{:S(2)}, u32[]{:S(2)}) collective-permute-start(bf16[48,4096]{1,0:T(8,128)(2,1)S(1)} %constant_dynamic-update-slice_fusion.2.refs_1_), channel_id=1, source_target_pairs={{0,4},{1,5},{2,6},{3,7},{4,0},{5,1},{6,2},{7,3},{8,12},{9,13},{10,... | collective-permute-start | bytes 1179656 | tf_op jit(solution)/shard_map/ppermute | solution.py:49
  71.3 27.2 %collective-permute-start.27 = (bf16[48,4096]{1,0:T(8,128)(2,1)S(1)}, bf16[48,4096]{1,0:T(8,128)(2,1)S(1)}, u32[]{:S(2)}, u32[]{:S(2)}) collective-permute-start(bf16[48,4096]{1,0:T(8,128)(2,1)S(1)} %constant_dynamic-update-slice_fusion.2.refs_1_), channel_id=1, source_target_pairs={{0,1},{1,0},{2,3},{3,2},{4,5},{5,4},{6,7},{7,6},{8,9},{9,8},{10,11... | collective-permute-start | bytes 1179656 | tf_op jit(solution)/shard_map/ppermute | solution.py:49
  71.3 26.6 %collective-permute-start.24 = (bf16[48,4096]{1,0:T(8,128)(2,1)}, bf16[48,4096]{1,0:T(8,128)(2,1)}, u32[]{:S(2)}, u32[]{:S(2)}) collective-permute-start(bf16[48,4096]{1,0:T(8,128)(2,1)} %collective-permute-done.21.refs_4_), channel_id=1, source_target_pairs={{0,2},{1,3},{2,0},{3,1},{4,6},{5,7},{6,4},{7,5},{8,10},{9,11},{10,... | collective-permute-start | bytes 1179656 | tf_op jit(solution)/shard_map/ppermute | solution.py:49
  84.4 13.0 %collective-permute-start.25 = (bf16[48,4096]{1,0:T(8,128)(2,1)}, bf16[48,4096]{1,0:T(8,128)(2,1)}, u32[]{:S(2)}, u32[]{:S(2)}) collective-permute-start(bf16[48,4096]{1,0:T(8,128)(2,1)} %collective-permute-done.22.refs_3_), channel_id=1, source_target_pairs={{0,4},{1,5},{2,6},{3,7},{4,0},{5,1},{6,2},{7,3},{8,12},{9,13},{10,... | collective-permute-start | bytes 1179656 | tf_op jit(solution)/shard_map/ppermute | solution.py:49
  85.6 12.9 %collective-permute-start.29 = (bf16[48,4096]{1,0:T(8,128)(2,1)}, bf16[48,4096]{1,0:T(8,128)(2,1)S(1)}, u32[]{:S(2)}, u32[]{:S(2)}) collective-permute-start(bf16[48,4096]{1,0:T(8,128)(2,1)} %collective-permute-done.22.refs_3_), channel_id=1, source_target_pairs={{0,1},{1,0},{2,3},{3,2},{4,5},{5,4},{6,7},{7,6},{8,9},{9,8},{10,11... | collective-permute-start | bytes 1179656 | tf_op jit(solution)/shard_map/ppermute | solution.py:49
  140.1 13.1 %collective-permute-start.35 = (bf16[48,2048]{1,0:T(8,128)(2,1)S(1)}, bf16[48,2048]{1,0:T(8,128)(2,1)S(1)}, u32[]{:S(2)}, u32[]{:S(2)}) collective-permute-start(bf16[48,2048]{1,0:T(8,128)(2,1)S(1)} %get-tuple-element.109), channel_id=1, source_target_pairs={{0,2},{1,3},{2,0},{3,1},{4,6},{5,7},{6,4},{7,5},{8,10},{9,11},{10,... | collective-permute-start | bytes 589832 | tf_op jit(solution)/shard_map/ppermute | solution.py:49
  140.8 12.5 %collective-permute-start.36 = (bf16[48,2048]{1,0:T(8,128)(2,1)S(1)}, bf16[48,2048]{1,0:T(8,128)(2,1)}, u32[]{:S(2)}, u32[]{:S(2)}) collective-permute-start(bf16[48,2048]{1,0:T(8,128)(2,1)S(1)} %get-tuple-element.108), channel_id=1, source_target_pairs={{0,4},{1,5},{2,6},{3,7},{4,0},{5,1},{6,2},{7,3},{8,12},{9,13},{10,... | collective-permute-start | bytes 589832 | tf_op jit(solution)/shard_map/ppermute | solution.py:49
  154.6 13.7 %collective-permute-start.38 = (bf16[96,2048]{1,0:T(8,128)(2,1)S(1)}, bf16[96,2048]{1,0:T(8,128)(2,1)S(1)}, u32[]{:S(2)}, u32[]{:S(2)}) collective-permute-start(bf16[96,2048]{1,0:T(8,128)(2,1)S(1)} %pad_maximum_fusion.5), channel_id=1, source_target_pairs={{0,4},{1,5},{2,6},{3,7},{4,0},{5,1},{6,2},{7,3},{8,12},{9,13},{10,... | collective-permute-start | bytes 1179656 | tf_op jit(solution)/shard_map/ppermute | solution.py:49
  155.7 12.7 %collective-permute-start.37 = (bf16[96,2048]{1,0:T(8,128)(2,1)S(1)}, bf16[96,2048]{1,0:T(8,128)(2,1)S(1)}, u32[]{:S(2)}, u32[]{:S(2)}) collective-permute-start(bf16[96,2048]{1,0:T(8,128)(2,1)S(1)} %pad_maximum_fusion.4), channel_id=1, source_target_pairs={{0,2},{1,3},{2,0},{3,1},{4,6},{5,7},{6,4},{7,5},{8,10},{9,11},{10,... | collective-permute-start | bytes 1179656 | tf_op jit(solution)/shard_map/ppermute | solution.py:49
  159.1 12.3 %collective-permute-start.40 = (bf16[48,2176]{1,0:T(8,128)(2,1)S(1)}, bf16[48,2176]{1,0:T(8,128)(2,1)S(1)}, u32[]{:S(2)}, u32[]{:S(2)}) collective-permute-start(bf16[48,2176]{1,0:T(8,128)(2,1)S(1)} %get-tuple-element.104), channel_id=1, source_target_pairs={{0,2},{1,3},{2,0},{3,1},{4,6},{5,7},{6,4},{7,5},{8,10},{9,11},{10,... | collective-permute-start | bytes 626696 | tf_op jit(solution)/shard_map/ppermute | solution.py:49
  160.3 11.1 %collective-permute-start.41 = (bf16[48,2176]{1,0:T(8,128)(2,1)S(1)}, bf16[48,2176]{1,0:T(8,128)(2,1)S(1)}, u32[]{:S(2)}, u32[]{:S(2)}) collective-permute-start(bf16[48,2176]{1,0:T(8,128)(2,1)S(1)} %get-tuple-element.103), channel_id=1, source_target_pairs={{0,4},{1,5},{2,6},{3,7},{4,0},{5,1},{6,2},{7,3},{8,12},{9,13},{10,... | collective-permute-start | bytes 626696 | tf_op jit(solution)/shard_map/ppermute | solution.py:49
  171.6 15.0 %collective-permute-start.46 = (bf16[96,2176]{1,0:T(8,128)(2,1)S(1)}, bf16[96,2176]{1,0:T(8,128)(2,1)S(1)}, u32[]{:S(2)}, u32[]{:S(2)}) collective-permute-start(bf16[96,2176]{1,0:T(8,128)(2,1)S(1)} %pad_maximum_fusion.1), channel_id=1, source_target_pairs={{0,4},{1,5},{2,6},{3,7},{4,0},{5,1},{6,2},{7,3},{8,12},{9,13},{10,... | collective-permute-start | bytes 1253384 | tf_op jit(solution)/shard_map/ppermute | solution.py:49
  172.8 13.8 %collective-permute-start.45 = (bf16[96,2176]{1,0:T(8,128)(2,1)S(1)}, bf16[96,2176]{1,0:T(8,128)(2,1)S(1)}, u32[]{:S(2)}, u32[]{:S(2)}) collective-permute-start(bf16[96,2176]{1,0:T(8,128)(2,1)S(1)} %pad_maximum_fusion), channel_id=1, source_target_pairs={{0,2},{1,3},{2,0},{3,1},{4,6},{5,7},{6,4},{7,5},{8,10},{9,11},{10,... | collective-permute-start | bytes 1253384 | tf_op jit(solution)/shard_map/ppermute | solution.py:49
  174.2 15.7 %collective-permute-start.42 = (bf16[24,2048]{1,0:T(8,128)(2,1)S(1)}, bf16[24,2048]{1,0:T(8,128)(2,1)S(1)}, u32[]{:S(2)}, u32[]{:S(2)}) collective-permute-start(bf16[24,2048]{1,0:T(8,128)(2,1)S(1)} %get-tuple-element.114), channel_id=1, source_target_pairs={{0,8},{1,9},{2,10},{3,11},{4,12},{5,13},{6,14},{7,15},{8,0},{9,1},... | collective-permute-start | bytes 294920 | tf_op jit(solution)/shard_map/ppermute | solution.py:49
  176.6 14.7 %collective-permute-start.43 = (bf16[24,2048]{1,0:T(8,128)(2,1)S(1)}, bf16[24,2048]{1,0:T(8,128)(2,1)S(1)}, u32[]{:S(2)}, u32[]{:S(2)}) collective-permute-start(bf16[24,2048]{1,0:T(8,128)(2,1)S(1)} %get-tuple-element.116), channel_id=1, source_target_pairs={{0,16},{1,17},{2,18},{3,19},{4,20},{5,21},{6,22},{7,23},{8,24},{9,... | collective-permute-start | bytes 294920 | tf_op jit(solution)/shard_map/ppermute | solution.py:49
  178.5 12.8 %collective-permute-start.44 = (bf16[24,2048]{1,0:T(8,128)(2,1)S(1)}, bf16[24,2048]{1,0:T(8,128)(2,1)S(1)}, u32[]{:S(2)}, u32[]{:S(2)}) collective-permute-start(bf16[24,2048]{1,0:T(8,128)(2,1)S(1)} %get-tuple-element.115), channel_id=1, source_target_pairs={{0,24},{1,25},{2,26},{3,27},{4,28},{5,29},{6,30},{7,31},{8,16},{9,... | collective-permute-start | bytes 294920 | tf_op jit(solution)/shard_map/ppermute | solution.py:49
  187.4 9.3 %collective-permute-start.48 = (bf16[24,2176]{1,0:T(8,128)(2,1)S(1)}, bf16[24,2176]{1,0:T(8,128)(2,1)S(1)}, u32[]{:S(2)}, u32[]{:S(2)}) collective-permute-start(bf16[24,2176]{1,0:T(8,128)(2,1)S(1)} %get-tuple-element.113), channel_id=1, source_target_pairs={{0,16},{1,17},{2,18},{3,19},{4,20},{5,21},{6,22},{7,23},{8,24},{9,... | collective-permute-start | bytes 313352 | tf_op jit(solution)/shard_map/ppermute | solution.py:49
  (43 other events, 235.2 us)

commit v4 on v3

--- a/solution.py
+++ b/solution.py
@@ -44,6 +44,11 @@
 CORE, X, Y, Z = 1, 2, 4, 8
 
 
+def silu_parts(gate_pre):
+    sigmoid_val = jax.nn.sigmoid(gate_pre)
+    return (gate_pre * sigmoid_val, sigmoid_val * (1.0 + gate_pre * (1.0 - sigmoid_val)))
+
+
 def flip(value, mask):
     count = lax.axis_size("wide")
     return lax.ppermute(value, "wide", [(i, i ^ mask) for i in range(count)])
@@ -57,14 +62,17 @@
     return lax.axis_size("wide") // Z
 
 
-def gather_z(shard):
-    blocks = [shard] + [flip(shard, Z * k) for k in range(1, depth())]
-    half = depth() // 2
-    return jnp.concatenate(blocks[:half], axis=0), blocks[half:]
-
-
-def join(blocks, *deps):
-    return jnp.concatenate(lax.optimization_barrier((*blocks, *deps))[: len(blocks)], axis=0)
+def along_z(shard):
+    return [flip(shard, Z * k) for k in range(1, depth())]
+
+
+def far_corner(by_x, by_y):
+    cut = (by_x.shape[0] // 16 + 1) * 8
+    return [flip(by_y[:cut], X), flip(by_x[cut:], Y)]
+
+
+def join(*blocks):
+    return jnp.concatenate(blocks, axis=0)
 
 
 def gather_core(pieces):
@@ -163,85 +171,6 @@
     )(slot.reshape(1, total), *pieces)
 
 
-def forward_kernel(x_ref, gate_ref, up_ref, hidden_ref, turned_ref, active_ref, pull_ref):
-    gate_pre = dot(x_ref[...], gate_ref[...], ((1,), (0,)))
-    up_pre = dot(x_ref[...], up_ref[...], ((1,), (0,)))
-    sig = jax.nn.sigmoid(gate_pre)
-    active = gate_pre * sig
-    hidden = active * up_pre
-    hidden_ref[...] = hidden.astype(bf16)
-    turned_ref[...] = hidden.T.astype(bf16)
-    active_ref[...] = active.astype(bf16)
-    pull_ref[...] = (up_pre * (sig * (1.0 + gate_pre * (1.0 - sig)))).astype(bf16)
-
-
-def forward(x, w_gate, w_up, part, parts):
-    rows, width = x.shape
-    units = w_gate.shape[1] // parts
-    block = tile(units, 256)
-    first = part * (units // block)
-    weight = pl.BlockSpec((width, block), lambda i: (0, first + i))
-    unit = pl.BlockSpec((rows, block), lambda i: (0, i))
-    turned = pl.BlockSpec((block, rows), lambda i: (i, 0))
-    shape = jax.ShapeDtypeStruct((rows, units), bf16)
-    return call(
-        forward_kernel,
-        4 * rows * width * units,
-        4 * width * units,
-        grid=(units // block,),
-        in_specs=[whole(rows, width), weight, weight],
-        out_specs=[unit, turned, unit, unit],
-        out_shape=[shape, jax.ShapeDtypeStruct((units, rows), bf16), shape, shape],
-    )(x, w_gate, w_up)
-
-
-def back_kernel(steps, g_ref, gain_ref, down_ref, *refs):
-    parts, (d_gate_ref, d_up_ref, route_ref) = refs[:-3], refs[-3:]
-    step = pl.program_id(0)
-    back = dot(g_ref[...], down_ref[...], ((1,), (1,)))
-    d_hidden = gain_ref[...] * back
-
-    @pl.when(step == 0)
-    def _():
-        route_ref[...] = jnp.zeros_like(route_ref)
-
-    for k in range(len(parts) // 3):
-        hidden_ref, active_ref, pull_ref = parts[3 * k : 3 * k + 3]
-
-        @pl.when((step >= k * steps) & (step < (k + 1) * steps))
-        def _(hidden_ref=hidden_ref, active_ref=active_ref, pull_ref=pull_ref):
-            d_gate_ref[...] = (d_hidden * pull_ref[...].astype(f32)).astype(bf16)
-            d_up_ref[...] = (d_hidden * active_ref[...].astype(f32)).astype(bf16)
-            route_ref[...] += jnp.sum(hidden_ref[...].astype(f32) * back, axis=1, keepdims=True)
-
-
-def back_project(g, gain, w_down, parts):
-    rows, width = g.shape
-    units = w_down.shape[0]
-    block = tile(parts[0][0].shape[1], 768)
-    steps = units // block // len(parts)
-    unit = pl.BlockSpec((rows, block), lambda i: (0, i))
-
-    def unit_of(part):
-        return pl.BlockSpec((rows, block), lambda i: (0, jnp.clip(i - part * steps, 0, steps - 1)))
-
-    shape = jax.ShapeDtypeStruct((rows, units), bf16)
-    return call(
-        functools.partial(back_kernel, steps),
-        2 * rows * width * units,
-        2 * width * units,
-        grid=(units // block,),
-        in_specs=[
-            whole(rows, width),
-            whole(rows, 1),
-            pl.BlockSpec((block, width), lambda i: (i, 0)),
-        ]
-        + [unit_of(k) for k in range(len(parts)) for _ in range(3)],
-        out_specs=[unit, unit, whole(rows, 1)],
-        out_shape=[shape, shape, jax.ShapeDtypeStruct((rows, 1), f32)],
-    )(g, gain, w_down, *[array for part in parts for array in part])
-
-
 def token_kernel(steps, spread, d_gate_ref, d_up_ref, slot_ref, route_ref, gate_ref, up_ref, *outs):
     step = pl.program_id(0)
 
@@ -335,24 +264,30 @@
     meta = jnp.concatenate(
         [expert_ids.astype(bf16), route_weights, jnp.zeros((tok_count, pad), bf16)], axis=1
     )
-    t_a, t_b = gather_z(jnp.concatenate([tokens, meta], axis=1))
-    t_xa, t_ya = flip(t_a, X), flip(t_a, Y)
-    t_b = join(t_b, t_xa, t_ya)
-    g_a, g_b = gather_z(after(grad_out, t_b))
-    t_xb, t_yb = flip(t_b, X), flip(t_b, Y)
-    t_da, t_db = flip(t_ya, X), flip(t_xb, Y)
-    pieces_t = gather_core([t_a, t_b, t_xa, t_xb, t_ya, t_yb, t_da, t_db])
-    g_a = after(g_a, t_xb, t_yb)
-    g_xa, g_ya = flip(g_a, X), flip(g_a, Y)
-    g_b = join(g_b, t_da, t_db)
-    g_xb, g_yb = flip(g_b, X), flip(g_b, Y)
-    all_meta = gather_meta(pieces_t, cols)
+    tokens = jnp.concatenate([tokens, meta], axis=1)
+    t_z = along_z(tokens)
+    t_x, t_y = flip(tokens, X), flip(tokens, Y)
+    g_x, g_y = flip(grad_out, X), flip(grad_out, Y)
+    t_far, g_far = flip(t_y, X), flip(g_x, Y)
+    t_rest = join(*t_z)
+    g_z = along_z(after(grad_out, t_rest))
+    t_xs, t_ys = flip(t_rest, X), flip(t_rest, Y)
+    t_fars = far_corner(t_xs, t_ys)
+    pieces = gather_core(
+        [join(tokens, *t_z), join(t_x, t_xs), join(t_y, t_ys), join(t_far, *t_fars)]
+    )
+    g_z = lax.optimization_barrier((*g_z, *t_fars))[: len(g_z)]
+    g_rest = join(*g_z)
+    g_xs, g_ys = flip(g_rest, X), flip(g_rest, Y)
+    all_meta = gather_meta(pieces, cols)
     all_ids = all_meta[:, :top_count].astype(jnp.int32)
     all_weights = all_meta[:, top_count : 2 * top_count].astype(f32)
     first = me * local_experts
     fused = narrow_count == 1 and local_experts == 1
     chunks = CHUNKS if fused else 1
-    parts = 2 if w_gate.shape[2] % (2 * LANES) == 0 else 1
+    expert_cols = experts_all + -experts_all % LANES
+    dense = [0, 0]
+    ends = []
     picked = []
     for j in range(local_experts):
         match = all_ids == first + j
@@ -360,37 +295,39 @@
         gain = jnp.sum(jnp.where(match, all_weights, 0.0), axis=1)
         rank = jnp.cumsum(chosen.astype(jnp.int32)) - 1
         slot = jnp.where(chosen, rank, -1)
-        place = slot[None, :] == jnp.arange(rows, dtype=jnp.int32)[:, None]
+        numbers = jnp.arange(rows, dtype=jnp.int32)[:, None]
+        place = slot[None, :] == numbers
         row_gain = jnp.sum(jnp.where(place, gain[None, :], 0.0), axis=1, keepdims=True)
-        x = pick_rows(slot, pieces_t, rows, cols)
+        x = pick_rows(slot, pieces, rows, cols)
         x = lax.all_gather(x, "narrow", axis=1, tiled=True)
-        picked.append([slot, place, row_gain, x])
-    g_xa, g_ya, *_ = lax.optimization_barrier((g_xa, g_ya, *[entry[3] for entry in picked]))
-    g_da = flip(g_ya, X)
+        gate_pre = dot(x, w_gate[j], ((1,), (0,)))
+        picked.append((slot, place, row_gain, x, gate_pre))
+    g_xs, g_ys, *_ = lax.optimization_barrier((g_xs, g_ys, *[entry[4] for entry in picked]))
+    g_fars = far_corner(g_xs, g_ys)
+    ups = [
+        dot(after(entry[3], g_xs, g_ys), w_up[j], ((1,), (0,))) for j, entry in enumerate(picked)
+    ]
+    *g_fars, _ = lax.optimization_barrier((*g_fars, ups[-1]))
+    pieces_g = gather_core(
+        [join(grad_out, *g_z), join(g_x, g_xs), join(g_y, g_ys), join(g_far, *g_fars)]
+    )
     for j in range(local_experts):
-        x = after(picked[j][3], g_xa, g_ya)
-        picked[j] += [x, [forward(x, w_gate[j], w_up[j], 0, parts)]]
-    g_xb, g_yb, *_ = lax.optimization_barrier((g_xb, g_yb, *[entry[5][0][0] for entry in picked]))
-    g_db = flip(g_xb, Y)
-    for j in range(local_experts):
-        if parts == 2:
-            x = after(picked[j][4], g_xb, g_yb)
-            picked[j][5].append(forward(x, w_gate[j], w_up[j], 1, parts))
-    g_da, g_db, *_ = lax.optimization_barrier((g_da, g_db, *[entry[5][-1][0] for entry in picked]))
-    pieces_g = gather_core([g_a, g_b, g_xa, g_xb, g_ya, g_yb, g_da, g_db])
-    expert_cols = experts_all + -experts_all % LANES
-    dense = [0, 0]
-    ends = []
-    for j in range(local_experts):
-        slot, place, row_gain, _, _, ahead = picked[j]
+        slot, place, row_gain, _, gate_pre = picked[j]
+        up_pre = ups[j]
+        active, slope = silu_parts(gate_pre)
+        hidden = (active * up_pre).astype(bf16)
+        turned = hidden.T
         g = pick_rows(slot, pieces_g, rows, cols)
         g = lax.all_gather(g, "narrow", axis=1, tiled=True)
-        straight = [(hidden, active, pull) for hidden, _, active, pull in ahead]
-        d_gate, d_up, route = back_project(g, row_gain, w_down[j], straight)
+        back = dot(g, w_down[j], ((1,), (1,)))
+        d_hidden = row_gain * back
+        d_gate = (d_hidden * up_pre * slope).astype(bf16)
+        d_up = (d_hidden * active).astype(bf16)
+        route = jnp.sum(hidden.astype(f32) * back, axis=1, keepdims=True)
         route = lax.psum(route.astype(bf16).astype(f32), "narrow")
         at = jnp.arange(expert_cols, dtype=jnp.int32) == first + j
         route = jnp.where(at[None, :], route, 0.0).astype(bf16)
-        ends.append(([part[1] for part in ahead], g, row_gain))
+        ends.append(([turned], g, row_gain))
         if fused:
             dense = token_grad(d_gate, d_up, slot, route, w_gate[j], w_up[j], 0, chunks, True)
             continue
@@ -438,7 +375,7 @@
         shares = [scatter_z(add(*send_sides(*add_far(*sent))))]
         grad_downs = [down_grad(*end, 0, 1, None) for end in ends]
     joined = jnp.concatenate(shares, axis=1)
-    width = tokens.shape[1]
+    width = cols
     by_expert = joined[:, width : width + experts_all].astype(f32)
     pick = expert_ids[:, :, None] == jnp.arange(experts_all, dtype=jnp.int32)[None, None, :]
     grad_route = jnp.sum(jnp.where(pick, by_expert[:, None, :], 0.0), axis=2)

time: 199 us -> 200 us (level)
  Pallas kernels: 84.8 us -> 51.8 us
  matrix products: 0 us -> 28.8 us
  local copies, waits for them, and re-layouts: 9.03 us -> 22.1 us
  starting transfers between devices: 50.2 us -> 45.2 us
  waiting for transfers between devices: 44.4 us -> 39.9 us
    pallas_call x3 -> x0, Pallas kernels: 32.1 us -> none  [the longest x2 20.2 us: forward(): call(forward_kernel, 4 * rows * width * units, 4 * width * units, grid=(u...]
    dot_general x0 -> x3, matrix products: none -> 28.8 us  [dot(): lax.dot_general(a, b, ((dims[0], dims[1]), ((), ())), preferred_element_t...]
    dot_general x0 -> x2, local copies, waits for them, and re-layouts: none -> 5.08 us  [dot(): lax.dot_general(a, b, ((dims[0], dims[1]), ((), ())), preferred_element_t...]
    ppermute x50 -> x44, starting transfers between devices: 50.2 us -> 45.2 us  [flip(): return lax.ppermute(value, 'wide', [(i, i ^ mask) for i in range(count)])]
    ppermute x50 -> x44, waiting for transfers between devices: 44.4 us -> 39.9 us  [flip(): return lax.ppermute(value, 'wide', [(i, i ^ mask) for i in range(count)])]
    concatenate x3 -> x9, local copies, waits for them, and re-layouts: 1.06 us -> 4.83 us  [the longest x8 3.81 us: join(): return jnp.concatenate(blocks, axis=0)]
    convert_element_type x0 -> x1, other arithmetic: none -> 2.43 us  [body(): hidden = (active * up_pre).astype(bf16)]
    slice x1 -> x5, local copies, waits for them, and re-layouts: 0.07 us -> 2.23 us  [the longest x4 2.16 us: far_corner(): return [flip(by_y[:cut], X), flip(by_x[cut:], Y)]]
  transfers between devices with their start and end apart: 50 -> 44, of which waited for: 14 -> 13; matrix products, arithmetic and copies ran while one was open for 3% -> 21% of each run, Pallas kernels for 27% -> 17%
where the time goes in v4:
time: 200 us; the launch traced here: 199 us
  Pallas kernels  51.8 us (26%)
  starting transfers between devices  45.2 us (23%)
  waiting for transfers between devices  39.9 us (20%)
  matrix products  28.8 us (14%)
  local copies, waits for them, and re-layouts  22.1 us (11%)
  other arithmetic  10.1 us (5%)
    ppermute x44, starting transfers between devices, flip(): return lax.ppermute(value, 'wide', [(i, i ^ mask) for i in range(count)])  45.2 us
    ppermute x44, waiting for transfers between devices, flip(): return lax.ppermute(value, 'wide', [(i, i ^ mask) for i in range(count)])  39.9 us
    dot_general x3, matrix products, dot(): lax.dot_general(a, b, ((dims[0], dims[1]), ((), ())), preferred_element_t...  28.8 us
    pallas_call x2, Pallas kernels, token_grad(): call(functools.partial(token_kernel, steps, spread), 4 * rows * width * u...  22.6 us
    pallas_call x2, Pallas kernels, pick_rows(): call(functools.partial(pick_kernel, sizes, block), 2 * rows * total * col...  14.8 us
    pallas_call x2, Pallas kernels, down_grad(): call(functools.partial(down_kernel, len(turned)), 2 * rows * width * unit...  13.5 us
    unnamed x55, local copies, waits for them, and re-layouts  9.5 us
    dot_general x2, local copies, waits for them, and re-layouts, dot(): lax.dot_general(a, b, ((dims[0], dims[1]), ((), ())), preferred_element_t...  5.08 us
  transfers between devices with their start and end apart: 44, of which 13 were waited for; matrix products, arithmetic and copies ran while one was open for 21% of the time, Pallas kernels for 17%

profile of v4, /device:TPU:0, one launch (start us, length us, event | category | flops | bytes accessed | tf_op | source)
XLA Modules:
  0.0 199.1 jit_solution(17934592085614427129)
XLA Ops:
  3.2 3.1 %collective-permute-start = (bf16[24,4224]{1,0:T(8,128)(2,1)S(1)}, bf16[24,4224]{1,0:T(8,128)(2,1)S(1)}, u32[]{:S(2)}, u32[]{:S(2)}) collective-permute-start(bf16[24,4224]{1,0:T(8,128)(2,1)S(1)} %concatenate.48), channel_id=1, source_target_pairs={{0,8},{1,9},{2,10},{3,11},{4,12},{5,13},{6,14},{7,15},{8,0},{9,1},... | collective-permute-start | bytes 608264 | tf_op jit(solution)/shard_map/ppermute | solution.py:54
  6.3 2.6 %collective-permute-start.1 = (bf16[24,4224]{1,0:T(8,128)(2,1)S(1)}, bf16[24,4224]{1,0:T(8,128)(2,1)S(1)}, u32[]{:S(2)}, u32[]{:S(2)}) collective-permute-start(bf16[24,4224]{1,0:T(8,128)(2,1)S(1)} %concatenate.48), channel_id=1, source_target_pairs={{0,16},{1,17},{2,18},{3,19},{4,20},{5,21},{6,22},{7,23},{8,24},{9,... | collective-permute-start | bytes 608264 | tf_op jit(solution)/shard_map/ppermute | solution.py:54
  8.9 1.7 collective-permute-start.5
  13.1 3.5 %collective-permute-done.17 = bf16[24,4096]{1,0:T(8,128)(2,1)} collective-permute-done((bf16[24,4096]{1,0:T(8,128)(2,1)}, bf16[24,4096]{1,0:T(8,128)(2,1)}, u32[]{:S(2)}, u32[]{:S(2)}) %collective-permute-start.17) | collective-permute-done | bytes 196640 | tf_op jit(solution)/shard_map/ppermute | solution.py:54
  17.9 4.5 %collective-permute-done.20 = bf16[24,4096]{1,0:T(8,128)(2,1)S(1)} collective-permute-done((bf16[24,4096]{1,0:T(8,128)(2,1)}, bf16[24,4096]{1,0:T(8,128)(2,1)S(1)}, u32[]{:S(2)}, u32[]{:S(2)}) %collective-permute-start.20) | collective-permute-done | bytes 196640 | tf_op jit(solution)/shard_map/ppermute | solution.py:54
  25.3 1.6 collective-permute-start.6
  27.5 3.1 %collective-permute-start.14 = (bf16[24,4096]{1,0:T(8,128)(2,1)S(1)}, bf16[24,4096]{1,0:T(8,128)(2,1)S(1)}, u32[]{:S(2)}, u32[]{:S(2)}) collective-permute-start(bf16[24,4096]{1,0:T(8,128)(2,1)S(1)} %copy-done.14), channel_id=1, source_target_pairs={{0,8},{1,9},{2,10},{3,11},{4,12},{5,13},{6,14},{7,15},{8,0},{9,1},... | collective-permute-start | bytes 589832 | tf_op jit(solution)/shard_map/ppermute | solution.py:54
  34.1 11.1 %collective-permute-done.7 = bf16[24,4224]{1,0:T(8,128)(2,1)S(1)} collective-permute-done((bf16[24,4224]{1,0:T(8,128)(2,1)S(1)}, bf16[24,4224]{1,0:T(8,128)(2,1)S(1)}, u32[]{:S(2)}, u32[]{:S(2)}) %collective-permute-start.7) | collective-permute-done | bytes 202784 | tf_op jit(solution)/shard_map/ppermute | solution.py:54
  45.1 3.5 %collective-permute-start.16 = (bf16[24,4096]{1,0:T(8,128)(2,1)S(1)}, bf16[24,4096]{1,0:T(8,128)(2,1)S(1)}, u32[]{:S(2)}, u32[]{:S(2)}) collective-permute-start(bf16[24,4096]{1,0:T(8,128)(2,1)S(1)} %copy-done.14), channel_id=1, source_target_pairs={{0,24},{1,25},{2,26},{3,27},{4,28},{5,29},{6,30},{7,31},{8,16},{9,... | collective-permute-start | bytes 589832 | tf_op jit(solution)/shard_map/ppermute | solution.py:54
  50.6 2.0 %collective-permute-done.16 = bf16[24,4096]{1,0:T(8,128)(2,1)S(1)} collective-permute-done((bf16[24,4096]{1,0:T(8,128)(2,1)S(1)}, bf16[24,4096]{1,0:T(8,128)(2,1)S(1)}, u32[]{:S(2)}, u32[]{:S(2)}) %collective-permute-start.16) | collective-permute-done | bytes 196640 | tf_op jit(solution)/shard_map/ppermute | solution.py:54
  52.7 3.2 %collective-permute-done.9 = bf16[32,4224]{1,0:T(8,128)(2,1)S(1)} collective-permute-done((bf16[32,4224]{1,0:T(8,128)(2,1)S(1)}, bf16[32,4224]{1,0:T(8,128)(2,1)S(1)}, u32[]{:S(2)}, u32[]{:S(2)}) %collective-permute-start.9) | collective-permute-done | bytes 270368 | tf_op jit(solution)/shard_map/ppermute | solution.py:54
  64.1 7.5 %shard_map.95 = bf16[384,4096]{1,0:T(8,128)(2,1)} custom-call(s32[1,768]{1,0:T(1,128)S(1)} %get-tuple-element.65.slot_ref, bf16[96,4224]{1,0:T(8,128)(2,1)S(1)} %pad_maximum_fusion.refs_0_, bf16[96,4224]{1,0:T(8,128)(2,1)S(1)} %constant_dynamic-update-slice_fusion.3.refs_1_, bf16[96,4224]{1,0:T(8,128)(2,1)} %copy-done.3, bf16[96,4224]{1,0:T(8,128)(2,1)} %copy-done.2, ...), custom_call_target="tpu_custom_call" | custom-call | flops 2415919104 | bytes 9437184 | tf_op jit(solution)/shard_map/pallas_call | solution.py:158
  71.6 11.5 %fusion.11 = f32[384,1536]{1,0:T(8,128)} fusion(bf16[384,4096]{1,0:T(8,128)(2,1)} %shard_map.95, bf16[1,4096,1536]{2,1,0:T(8,128)(2,1)} %param.11), kind=kOutput, calls=%fused_computation.76 | convolution fusion | flops 4831838208 | bytes 18087936 | tf_op jit(solution)/shard_map/dot_general | solution.py:16
  90.4 6.4 %fusion.9 = f32[384,1536]{1,0:T(8,128)} fusion(bf16[384,4096]{1,0:T(8,128)(2,1)S(1)} %copy-done.8, bf16[1,4096,1536]{2,1,0:T(8,128)(2,1)S(1)} %bitcast.50), kind=kOutput, calls=%fused_computation.74 | convolution fusion | flops 4831838208 | bytes 18087936 | tf_op jit(solution)/shard_map/dot_general | solution.py:16
  99.3 1.6 collective-permute-done.27.refs_7_
  100.9 7.3 %shard_map.96.g_ref = bf16[384,4096]{1,0:T(8,128)(2,1)} custom-call(s32[1,768]{1,0:T(1,128)S(1)} %get-tuple-element.65.slot_ref, bf16[96,4096]{1,0:T(8,128)(2,1)S(1)} %get-tuple-element.88.refs_0_, bf16[96,4096]{1,0:T(8,128)(2,1)S(1)} %constant_dynamic-update-slice_fusion.17.refs_1_, bf16[96,4096]{1,0:T(8,128)(2,1)} %copy-done.13, ...), custom_call_target="tpu_custom_call" | custom-call | flops 2415919104 | bytes 9437184 | tf_op jit(solution)/shard_map/pallas_call | solution.py:158
  108.2 10.9 %multiply_reduce_fusion = (bf16[384]{0:T(512)(128)(2,1)S(1)}, bf16[384,1536]{1,0:T(8,128)(2,1)S(1)}, bf16[384,1536]{1,0:T(8,128)(2,1)}) fusion(f32[384,1536]{1,0:T(8,128)S(1)} %copy-done.10, f32[384,1536]{1,0:T(8,128)S(1)} %copy-done.9, f32[384]{0:T(512)S(1)} %select_reduce_fusion, bf16[384,4096]{1,0:T(8,128)(2,1)} %shard_map.96.g_ref, ...), kind=kOutput, calls=%fused_computation.11 | convolution fusion | flops 4843044352 | bytes 22808832 | tf_op jit(solution)/shard_map/dot_general | solution.py:16
  119.3 11.2 %shard_map.97 = (bf16[384,2048]{1,0:T(8,128)(2,1)}, bf16[384,2048]{1,0:T(8,128)(2,1)}) custom-call(bf16[384,1536]{1,0:T(8,128)(2,1)S(1)} %get-tuple-element.42.d_gate_ref, bf16[384,1536]{1,0:T(8,128)(2,1)} %get-tuple-element.69.d_up_ref, s32[768,1]{1,0:T(8,128)S(1)} %bitcast_select_fusion.slot_ref, bf16[384,128]{1,0:T(8,128)(2,1)S(1)} %select_convert_fusion.route_ref, ...), custom_call_target="tpu_custom_call" | custom-call | flops 6039797760 | bytes 15728640 | tf_op jit(solution)/shard_map/pallas_call | solution.py:211
  130.7 3.4 %collective-permute-done.28 = bf16[384,2048]{1,0:T(8,128)(2,1)S(1)} collective-permute-done((bf16[384,2048]{1,0:T(8,128)(2,1)}, bf16[384,2048]{1,0:T(8,128)(2,1)S(1)}, u32[]{:S(2)}, u32[]{:S(2)}) %collective-permute-start.28) | collective-permute-done | bytes 1572896 | tf_op jit(solution)/shard_map/ppermute | solution.py:54
  134.1 2.1 %add_convert_fusion.1 = bf16[384,2048]{1,0:T(8,128)(2,1)S(1)} fusion(bf16[384,2048]{1,0:T(8,128)(2,1)S(1)} %collective-permute-done.28, bf16[384,2048]{1,0:T(8,128)(2,1)} %get-tuple-element.40), kind=kLoop, calls=%fused_computation.3 | loop fusion | flops 3145728 | bytes 4718592 | tf_op jit(solution)/shard_map/convert_element_type | solution.py:23
  138.3 11.4 %shard_map.98 = (bf16[384,2176]{1,0:T(8,128)(2,1)}, bf16[384,2176]{1,0:T(8,128)(2,1)}) custom-call(bf16[384,1536]{1,0:T(8,128)(2,1)S(1)} %get-tuple-element.42.d_gate_ref, bf16[384,1536]{1,0:T(8,128)(2,1)} %get-tuple-element.69.d_up_ref, s32[768,1]{1,0:T(8,128)S(1)} %bitcast_select_fusion.slot_ref, bf16[384,128]{1,0:T(8,128)(2,1)S(1)} %select_convert_fusion.route_ref, ...), custom_call_target="tpu_custom_call" | custom-call | flops 6039797760 | bytes 15728640 | tf_op jit(solution)/shard_map/pallas_call | solution.py:211
  149.8 2.0 %copy.40 = f32[384,1536]{0,1:T(8,128)S(1)} copy(f32[384,1536]{1,0:T(8,128)} %fusion.9) | data formatting | bytes 4718592 | tf_op jit(solution)/shard_map/dot_general | solution.py:16
  151.9 3.0 %copy.39 = f32[384,1536]{0,1:T(8,128)} copy(f32[384,1536]{1,0:T(8,128)} %fusion.11) | data formatting | bytes 4718592 | tf_op jit(solution)/shard_map/dot_general | solution.py:16
  155.0 2.4 %fusion.2.refs_0_ = bf16[1536,384]{1,0:T(8,128)(2,1)S(1)} fusion(f32[384,1536]{0,1:T(8,128)S(1)} %copy.40, f32[384,1536]{0,1:T(8,128)} %copy.39), kind=kLoop, calls=%fused_computation.5 | loop fusion | flops 3538944 | bytes 5898240 | tf_op jit(solution)/shard_map/convert_element_type | solution.py:318
  157.6 1.6 collective-permute-start.32
  159.9 1.8 add_convert_fusion
  163.8 6.7 %shard_map.99.refs_1_ = bf16[1536,4096]{1,0:T(8,128)(2,1)} custom-call(bf16[384,4096]{1,0:T(8,128)(2,1)} %shard_map.96.g_ref, f32[384,1]{1,0:T(8,128)S(1)} %broadcast_in_dim.74.gain_ref, bf16[1536,384]{1,0:T(8,128)(2,1)S(1)} %fusion.2.refs_0_), custom_call_target="tpu_custom_call" | custom-call | flops 2415919104 | bytes 6291456 | tf_op jit(solution)/shard_map/pallas_call | solution.py:238
  171.2 3.7 %collective-permute-done.34 = bf16[48,2176]{1,0:T(8,128)(2,1)S(1)} collective-permute-done((bf16[48,2176]{1,0:T(8,128)(2,1)S(1)}, bf16[48,2176]{1,0:T(8,128)(2,1)S(1)}, u32[]{:S(2)}, u32[]{:S(2)}) %collective-permute-start.34) | collective-permute-done | bytes 208928 | tf_op jit(solution)/shard_map/ppermute | solution.py:54
  178.0 3.1 %collective-permute-start.38 = (bf16[24,2048]{1,0:T(8,128)(2,1)S(1)}, bf16[24,2048]{1,0:T(8,128)(2,1)S(1)}, u32[]{:S(2)}, u32[]{:S(2)}) collective-permute-start(bf16[24,2048]{1,0:T(8,128)(2,1)S(1)} %get-tuple-element.86), channel_id=1, source_target_pairs={{0,24},{1,25},{2,26},{3,27},{4,28},{5,29},{6,30},{7,31},{8,16},{9,... | collective-permute-start | bytes 294920 | tf_op jit(solution)/shard_map/ppermute | solution.py:54
  181.1 6.7 %shard_map.100 = bf16[1536,4096]{1,0:T(8,128)(2,1)} custom-call(bf16[384,4096]{1,0:T(8,128)(2,1)} %shard_map.96.g_ref, f32[384,1]{1,0:T(8,128)S(1)} %broadcast_in_dim.74.gain_ref, bf16[1536,384]{1,0:T(8,128)(2,1)S(1)} %fusion.2.refs_0_, bf16[1536,4096]{1,0:T(8,128)(2,1)} %shard_map.99.refs_1_), custom_call_target="tpu_custom_call", output_to_operand_aliasing={{}: (3, {})} | custom-call | flops 2415919104 | bytes 6291456 | tf_op jit(solution)/shard_map/pallas_call | solution.py:238
  189.4 3.1 %collective-permute-start.43 = (bf16[24,2176]{1,0:T(8,128)(2,1)S(1)}, bf16[24,2176]{1,0:T(8,128)(2,1)S(1)}, u32[]{:S(2)}, u32[]{:S(2)}) collective-permute-start(bf16[24,2176]{1,0:T(8,128)(2,1)S(1)} %get-tuple-element.83), channel_id=1, source_target_pairs={{0,24},{1,25},{2,26},{3,27},{4,28},{5,29},{6,30},{7,31},{8,16},{9,... | collective-permute-start | bytes 313352 | tf_op jit(solution)/shard_map/ppermute | solution.py:54
  193.4 4.1 %collective-permute-done.42 = bf16[24,2176]{1,0:T(8,128)(2,1)S(1)} collective-permute-done((bf16[24,2176]{1,0:T(8,128)(2,1)S(1)}, bf16[24,2176]{1,0:T(8,128)(2,1)S(1)}, u32[]{:S(2)}, u32[]{:S(2)}) %collective-permute-start.42) | collective-permute-done | bytes 104480 | tf_op jit(solution)/shard_map/ppermute | solution.py:54
  (176 shorter events, 46.3 us)
Async XLA Ops:
  3.2 21.5 %collective-permute-start = (bf16[24,4224]{1,0:T(8,128)(2,1)S(1)}, bf16[24,4224]{1,0:T(8,128)(2,1)S(1)}, u32[]{:S(2)}, u32[]{:S(2)}) collective-permute-start(bf16[24,4224]{1,0:T(8,128)(2,1)S(1)} %concatenate.48), channel_id=1, source_target_pairs={{0,8},{1,9},{2,10},{3,11},{4,12},{5,13},{6,14},{7,15},{8,0},{9,1},... | collective-permute-start | bytes 608264 | tf_op jit(solution)/shard_map/ppermute | solution.py:54
  6.3 18.9 %collective-permute-start.1 = (bf16[24,4224]{1,0:T(8,128)(2,1)S(1)}, bf16[24,4224]{1,0:T(8,128)(2,1)S(1)}, u32[]{:S(2)}, u32[]{:S(2)}) collective-permute-start(bf16[24,4224]{1,0:T(8,128)(2,1)S(1)} %concatenate.48), channel_id=1, source_target_pairs={{0,16},{1,17},{2,18},{3,19},{4,20},{5,21},{6,22},{7,23},{8,24},{9,... | collective-permute-start | bytes 608264 | tf_op jit(solution)/shard_map/ppermute | solution.py:54
  8.9 16.4 %collective-permute-start.2 = (bf16[24,4224]{1,0:T(8,128)(2,1)S(1)}, bf16[24,4224]{1,0:T(8,128)(2,1)S(1)}, u32[]{:S(2)}, u32[]{:S(2)}) collective-permute-start(bf16[24,4224]{1,0:T(8,128)(2,1)S(1)} %concatenate.48), channel_id=1, source_target_pairs={{0,24},{1,25},{2,26},{3,27},{4,28},{5,29},{6,30},{7,31},{8,16},{9,... | collective-permute-start | bytes 608264 | tf_op jit(solution)/shard_map/ppermute | solution.py:54
  8.9 18.6 %collective-permute-start.5 = (bf16[24,4224]{1,0:T(8,128)(2,1)S(1)}, bf16[24,4224]{1,0:T(8,128)(2,1)S(1)}, u32[]{:S(2)}, u32[]{:S(2)}) collective-permute-start(bf16[24,4224]{1,0:T(8,128)(2,1)S(1)} %concatenate.48), channel_id=1, source_target_pairs={{0,4},{1,5},{2,6},{3,7},{4,0},{5,1},{6,2},{7,3},{8,12},{9,13},{10,... | collective-permute-start | bytes 608264 | tf_op jit(solution)/shard_map/ppermute | solution.py:54
  25.3 23.4 %collective-permute-start.6 = (bf16[72,4224]{1,0:T(8,128)(2,1)S(1)}, bf16[72,4224]{1,0:T(8,128)(2,1)S(1)}, u32[]{:S(2)}, u32[]{:S(2)}) collective-permute-start(bf16[72,4224]{1,0:T(8,128)(2,1)S(1)} %constant_dynamic-update-slice_fusion), channel_id=1, source_target_pairs={{0,4},{1,5},{2,6},{3,7},{4,0},{5,1},{6,2},{7,3},{8,12},{9,13},{10,... | collective-permute-start | bytes 1824776 | tf_op jit(solution)/shard_map/ppermute | solution.py:54
  26.8 22.5 %collective-permute-start.4 = (bf16[72,4224]{1,0:T(8,128)(2,1)S(1)}, bf16[72,4224]{1,0:T(8,128)(2,1)S(1)}, u32[]{:S(2)}, u32[]{:S(2)}) collective-permute-start(bf16[72,4224]{1,0:T(8,128)(2,1)S(1)} %constant_dynamic-update-slice_fusion), channel_id=1, source_target_pairs={{0,2},{1,3},{2,0},{3,1},{4,6},{5,7},{6,4},{7,5},{8,10},{9,11},{10,... | collective-permute-start | bytes 1824776 | tf_op jit(solution)/shard_map/ppermute | solution.py:54
  27.5 22.6 %collective-permute-start.14 = (bf16[24,4096]{1,0:T(8,128)(2,1)S(1)}, bf16[24,4096]{1,0:T(8,128)(2,1)S(1)}, u32[]{:S(2)}, u32[]{:S(2)}) collective-permute-start(bf16[24,4096]{1,0:T(8,128)(2,1)S(1)} %copy-done.14), channel_id=1, source_target_pairs={{0,8},{1,9},{2,10},{3,11},{4,12},{5,13},{6,14},{7,15},{8,0},{9,1},... | collective-permute-start | bytes 589832 | tf_op jit(solution)/shard_map/ppermute | solution.py:54
  30.6 19.6 %collective-permute-start.15 = (bf16[24,4096]{1,0:T(8,128)(2,1)S(1)}, bf16[24,4096]{1,0:T(8,128)(2,1)S(1)}, u32[]{:S(2)}, u32[]{:S(2)}) collective-permute-start(bf16[24,4096]{1,0:T(8,128)(2,1)S(1)} %copy-done.14), channel_id=1, source_target_pairs={{0,16},{1,17},{2,18},{3,19},{4,20},{5,21},{6,22},{7,23},{8,24},{9,... | collective-permute-start | bytes 589832 | tf_op jit(solution)/shard_map/ppermute | solution.py:54
  32.7 12.4 %collective-permute-start.7 = (bf16[24,4224]{1,0:T(8,128)(2,1)S(1)}, bf16[24,4224]{1,0:T(8,128)(2,1)S(1)}, u32[]{:S(2)}, u32[]{:S(2)}) collective-permute-start(bf16[24,4224]{1,0:T(8,128)(2,1)S(1)} %collective-permute-done.5), channel_id=1, source_target_pairs={{0,2},{1,3},{2,0},{3,1},{4,6},{5,7},{6,4},{7,5},{8,10},{9,11},{10,... | collective-permute-start | bytes 608264 | tf_op jit(solution)/shard_map/ppermute | solution.py:54
  50.1 9.7 %collective-permute-start.10 = (bf16[96,4224]{1,0:T(8,128)(2,1)S(1)}, bf16[96,4224]{1,0:T(8,128)(2,1)S(1)}, u32[]{:S(2)}, u32[]{:S(2)}) collective-permute-start(bf16[96,4224]{1,0:T(8,128)(2,1)S(1)} %pad_maximum_fusion.refs_0_), channel_id=1, source_target_pairs={{0,1},{1,0},{2,3},{3,2},{4,5},{5,4},{6,7},{7,6},{8,9},{9,8},{10,11... | collective-permute-start | bytes 2433032 | tf_op jit(solution)/shard_map/ppermute | solution.py:54
  50.2 10.1 %collective-permute-start.12 = (bf16[96,4224]{1,0:T(8,128)(2,1)S(1)}, bf16[96,4224]{1,0:T(8,128)(2,1)S(1)}, u32[]{:S(2)}, u32[]{:S(2)}) collective-permute-start(bf16[96,4224]{1,0:T(8,128)(2,1)S(1)} %constant_dynamic-update-slice_fusion.5.refs_2_), channel_id=1, source_target_pairs={{0,1},{1,0},{2,3},{3,2},{4,5},{5,4},{6,7},{7,6},{8,9},{9,8},{10,11... | collective-permute-start | bytes 2433032 | tf_op jit(solution)/shard_map/ppermute | solution.py:54
  58.3 24.8 %collective-permute-start.18 = (bf16[72,4096]{1,0:T(8,128)(2,1)}, bf16[72,4096]{1,0:T(8,128)(2,1)}, u32[]{:S(2)}, u32[]{:S(2)}) collective-permute-start(bf16[72,4096]{1,0:T(8,128)(2,1)} %get-tuple-element.89), channel_id=1, source_target_pairs={{0,2},{1,3},{2,0},{3,1},{4,6},{5,7},{6,4},{7,5},{8,10},{9,11},{10,... | collective-permute-start | bytes 1769480 | tf_op jit(solution)/shard_map/ppermute | solution.py:54
  59.8 23.4 %collective-permute-start.19 = (bf16[72,4096]{1,0:T(8,128)(2,1)}, bf16[72,4096]{1,0:T(8,128)(2,1)}, u32[]{:S(2)}, u32[]{:S(2)}) collective-permute-start(bf16[72,4096]{1,0:T(8,128)(2,1)} %get-tuple-element.89), channel_id=1, source_target_pairs={{0,4},{1,5},{2,6},{3,7},{4,0},{5,1},{6,2},{7,3},{8,12},{9,13},{10,... | collective-permute-start | bytes 1769480 | tf_op jit(solution)/shard_map/ppermute | solution.py:54
  60.3 39.0 %collective-permute-start.24 = (bf16[96,4096]{1,0:T(8,128)(2,1)S(1)}, bf16[96,4096]{1,0:T(8,128)(2,1)}, u32[]{:S(2)}, u32[]{:S(2)}) collective-permute-start(bf16[96,4096]{1,0:T(8,128)(2,1)S(1)} %get-tuple-element.88.refs_0_), channel_id=1, source_target_pairs={{0,1},{1,0},{2,3},{3,2},{4,5},{5,4},{6,7},{7,6},{8,9},{9,8},{10,11... | collective-permute-start | bytes 2359304 | tf_op jit(solution)/shard_map/ppermute | solution.py:54
  85.3 11.5 %collective-permute-start.22 = (bf16[40,4096]{1,0:T(8,128)(2,1)S(1)}, bf16[40,4096]{1,0:T(8,128)(2,1)S(1)}, u32[]{:S(2)}, u32[]{:S(2)}) collective-permute-start(bf16[40,4096]{1,0:T(8,128)(2,1)S(1)} %slice.121), channel_id=1, source_target_pairs={{0,2},{1,3},{2,0},{3,1},{4,6},{5,7},{6,4},{7,5},{8,10},{9,11},{10,... | collective-permute-start | bytes 983048 | tf_op jit(solution)/shard_map/ppermute | solution.py:54
  85.9 10.8 %collective-permute-start.23 = (bf16[32,4096]{1,0:T(8,128)(2,1)S(1)}, bf16[32,4096]{1,0:T(8,128)(2,1)S(1)}, u32[]{:S(2)}, u32[]{:S(2)}) collective-permute-start(bf16[32,4096]{1,0:T(8,128)(2,1)S(1)} %slice.122), channel_id=1, source_target_pairs={{0,4},{1,5},{2,6},{3,7},{4,0},{5,1},{6,2},{7,3},{8,12},{9,13},{10,... | collective-permute-start | bytes 786440 | tf_op jit(solution)/shard_map/ppermute | solution.py:54
  88.6 10.7 %collective-permute-start.25 = (bf16[96,4096]{1,0:T(8,128)(2,1)S(1)}, bf16[96,4096]{1,0:T(8,128)(2,1)}, u32[]{:S(2)}, u32[]{:S(2)}) collective-permute-start(bf16[96,4096]{1,0:T(8,128)(2,1)S(1)} %constant_dynamic-update-slice_fusion.17.refs_1_), channel_id=1, source_target_pairs={{0,1},{1,0},{2,3},{3,2},{4,5},{5,4},{6,7},{7,6},{8,9},{9,8},{10,11... | collective-permute-start | bytes 2359304 | tf_op jit(solution)/shard_map/ppermute | solution.py:54
  89.8 9.5 %collective-permute-start.26 = (bf16[96,4096]{1,0:T(8,128)(2,1)S(1)}, bf16[96,4096]{1,0:T(8,128)(2,1)}, u32[]{:S(2)}, u32[]{:S(2)}) collective-permute-start(bf16[96,4096]{1,0:T(8,128)(2,1)S(1)} %constant_dynamic-update-slice_fusion.19.refs_2_), channel_id=1, source_target_pairs={{0,1},{1,0},{2,3},{3,2},{4,5},{5,4},{6,7},{7,6},{8,9},{9,8},{10,11... | collective-permute-start | bytes 2359304 | tf_op jit(solution)/shard_map/ppermute | solution.py:54
  136.3 13.4 %collective-permute-start.29 = (bf16[48,2048]{1,0:T(8,128)(2,1)S(1)}, bf16[48,2048]{1,0:T(8,128)(2,1)S(1)}, u32[]{:S(2)}, u32[]{:S(2)}) collective-permute-start(bf16[48,2048]{1,0:T(8,128)(2,1)S(1)} %get-tuple-element.80), channel_id=1, source_target_pairs={{0,2},{1,3},{2,0},{3,1},{4,6},{5,7},{6,4},{7,5},{8,10},{9,11},{10,... | collective-permute-start | bytes 589832 | tf_op jit(solution)/shard_map/ppermute | solution.py:54
  137.7 11.9 %collective-permute-start.30 = (bf16[48,2048]{1,0:T(8,128)(2,1)S(1)}, bf16[48,2048]{1,0:T(8,128)(2,1)S(1)}, u32[]{:S(2)}, u32[]{:S(2)}) collective-permute-start(bf16[48,2048]{1,0:T(8,128)(2,1)S(1)} %get-tuple-element.79), channel_id=1, source_target_pairs={{0,4},{1,5},{2,6},{3,7},{4,0},{5,1},{6,2},{7,3},{8,12},{9,13},{10,... | collective-permute-start | bytes 589832 | tf_op jit(solution)/shard_map/ppermute | solution.py:54
  149.7 10.3 %collective-permute-start.33 = (bf16[384,2176]{1,0:T(8,128)(2,1)}, bf16[384,2176]{1,0:T(8,128)(2,1)}, u32[]{:S(2)}, u32[]{:S(2)}) collective-permute-start(bf16[384,2176]{1,0:T(8,128)(2,1)} %get-tuple-element.48), channel_id=1, source_target_pairs={{0,1},{1,0},{2,3},{3,2},{4,5},{5,4},{6,7},{7,6},{8,9},{9,8},{10,11... | collective-permute-start | bytes 5013512 | tf_op jit(solution)/shard_map/ppermute | solution.py:54
  157.6 12.9 %collective-permute-start.32 = (bf16[96,2048]{1,0:T(8,128)(2,1)S(1)}, bf16[96,2048]{1,0:T(8,128)(2,1)S(1)}, u32[]{:S(2)}, u32[]{:S(2)}) collective-permute-start(bf16[96,2048]{1,0:T(8,128)(2,1)S(1)} %pad_maximum_fusion.4), channel_id=1, source_target_pairs={{0,4},{1,5},{2,6},{3,7},{4,0},{5,1},{6,2},{7,3},{8,12},{9,13},{10,... | collective-permute-start | bytes 1179656 | tf_op jit(solution)/shard_map/ppermute | solution.py:54
  159.2 12.0 %collective-permute-start.31 = (bf16[96,2048]{1,0:T(8,128)(2,1)S(1)}, bf16[96,2048]{1,0:T(8,128)(2,1)S(1)}, u32[]{:S(2)}, u32[]{:S(2)}) collective-permute-start(bf16[96,2048]{1,0:T(8,128)(2,1)S(1)} %pad_maximum_fusion.3), channel_id=1, source_target_pairs={{0,2},{1,3},{2,0},{3,1},{4,6},{5,7},{6,4},{7,5},{8,10},{9,11},{10,... | collective-permute-start | bytes 1179656 | tf_op jit(solution)/shard_map/ppermute | solution.py:54
  161.8 13.2 %collective-permute-start.34 = (bf16[48,2176]{1,0:T(8,128)(2,1)S(1)}, bf16[48,2176]{1,0:T(8,128)(2,1)S(1)}, u32[]{:S(2)}, u32[]{:S(2)}) collective-permute-start(bf16[48,2176]{1,0:T(8,128)(2,1)S(1)} %get-tuple-element.75), channel_id=1, source_target_pairs={{0,2},{1,3},{2,0},{3,1},{4,6},{5,7},{6,4},{7,5},{8,10},{9,11},{10,... | collective-permute-start | bytes 626696 | tf_op jit(solution)/shard_map/ppermute | solution.py:54
  163.3 11.7 %collective-permute-start.35 = (bf16[48,2176]{1,0:T(8,128)(2,1)S(1)}, bf16[48,2176]{1,0:T(8,128)(2,1)S(1)}, u32[]{:S(2)}, u32[]{:S(2)}) collective-permute-start(bf16[48,2176]{1,0:T(8,128)(2,1)S(1)} %get-tuple-element.74), channel_id=1, source_target_pairs={{0,4},{1,5},{2,6},{3,7},{4,0},{5,1},{6,2},{7,3},{8,12},{9,13},{10,... | collective-permute-start | bytes 626696 | tf_op jit(solution)/shard_map/ppermute | solution.py:54
  175.2 12.7 %collective-permute-start.40 = (bf16[96,2176]{1,0:T(8,128)(2,1)S(1)}, bf16[96,2176]{1,0:T(8,128)(2,1)S(1)}, u32[]{:S(2)}, u32[]{:S(2)}) collective-permute-start(bf16[96,2176]{1,0:T(8,128)(2,1)S(1)} %pad_maximum_fusion.2), channel_id=1, source_target_pairs={{0,4},{1,5},{2,6},{3,7},{4,0},{5,1},{6,2},{7,3},{8,12},{9,13},{10,... | collective-permute-start | bytes 1253384 | tf_op jit(solution)/shard_map/ppermute | solution.py:54
  175.8 12.0 %collective-permute-start.39 = (bf16[96,2176]{1,0:T(8,128)(2,1)S(1)}, bf16[96,2176]{1,0:T(8,128)(2,1)S(1)}, u32[]{:S(2)}, u32[]{:S(2)}) collective-permute-start(bf16[96,2176]{1,0:T(8,128)(2,1)S(1)} %pad_maximum_fusion.1), channel_id=1, source_target_pairs={{0,2},{1,3},{2,0},{3,1},{4,6},{5,7},{6,4},{7,5},{8,10},{9,11},{10,... | collective-permute-start | bytes 1253384 | tf_op jit(solution)/shard_map/ppermute | solution.py:54
  176.6 12.8 %collective-permute-start.36 = (bf16[24,2048]{1,0:T(8,128)(2,1)S(1)}, bf16[24,2048]{1,0:T(8,128)(2,1)S(1)}, u32[]{:S(2)}, u32[]{:S(2)}) collective-permute-start(bf16[24,2048]{1,0:T(8,128)(2,1)S(1)} %get-tuple-element.85), channel_id=1, source_target_pairs={{0,8},{1,9},{2,10},{3,11},{4,12},{5,13},{6,14},{7,15},{8,0},{9,1},... | collective-permute-start | bytes 294920 | tf_op jit(solution)/shard_map/ppermute | solution.py:54
  177.8 14.7 %collective-permute-start.37 = (bf16[24,2048]{1,0:T(8,128)(2,1)S(1)}, bf16[24,2048]{1,0:T(8,128)(2,1)S(1)}, u32[]{:S(2)}, u32[]{:S(2)}) collective-permute-start(bf16[24,2048]{1,0:T(8,128)(2,1)S(1)} %get-tuple-element.87), channel_id=1, source_target_pairs={{0,16},{1,17},{2,18},{3,19},{4,20},{5,21},{6,22},{7,23},{8,24},{9,... | collective-permute-start | bytes 294920 | tf_op jit(solution)/shard_map/ppermute | solution.py:54
  178.0 14.5 %collective-permute-start.38 = (bf16[24,2048]{1,0:T(8,128)(2,1)S(1)}, bf16[24,2048]{1,0:T(8,128)(2,1)S(1)}, u32[]{:S(2)}, u32[]{:S(2)}) collective-permute-start(bf16[24,2048]{1,0:T(8,128)(2,1)S(1)} %get-tuple-element.86), channel_id=1, source_target_pairs={{0,24},{1,25},{2,26},{3,27},{4,28},{5,29},{6,30},{7,31},{8,16},{9,... | collective-permute-start | bytes 294920 | tf_op jit(solution)/shard_map/ppermute | solution.py:54
  188.3 9.2 %collective-permute-start.42 = (bf16[24,2176]{1,0:T(8,128)(2,1)S(1)}, bf16[24,2176]{1,0:T(8,128)(2,1)S(1)}, u32[]{:S(2)}, u32[]{:S(2)}) collective-permute-start(bf16[24,2176]{1,0:T(8,128)(2,1)S(1)} %get-tuple-element.84), channel_id=1, source_target_pairs={{0,16},{1,17},{2,18},{3,19},{4,20},{5,21},{6,22},{7,23},{8,24},{9,... | collective-permute-start | bytes 313352 | tf_op jit(solution)/shard_map/ppermute | solution.py:54
  189.4 8.1 %collective-permute-start.43 = (bf16[24,2176]{1,0:T(8,128)(2,1)S(1)}, bf16[24,2176]{1,0:T(8,128)(2,1)S(1)}, u32[]{:S(2)}, u32[]{:S(2)}) collective-permute-start(bf16[24,2176]{1,0:T(8,128)(2,1)S(1)} %get-tuple-element.83), channel_id=1, source_target_pairs={{0,24},{1,25},{2,26},{3,27},{4,28},{5,29},{6,30},{7,31},{8,16},{9,... | collective-permute-start | bytes 313352 | tf_op jit(solution)/shard_map/ppermute | solution.py:54
  (31 other events, 249.1 us)
